TPU v7x, 128 devices: a whole 4x4x4 slice. The times are simulated.
128 devices in a mesh: dp: 4 (over x), ctx: 32 (over y, z, core).
Axes of the slice: x: 4, y: 4, z: 4, core: 2. Of those that a mesh axis runs over, the one named last changes fastest.
Arguments:
- queries: bfloat16 [4, 16384, 2048], P('dp', 'ctx'), may hold values from -6 to 6
- key_rows: bfloat16 [4, 16384, 2048], P('dp', 'ctx'), may hold values from -6 to 6
- value_rows: bfloat16 [4, 16384, 2048], P('dp', 'ctx'), may hold values from -140 to 140
- log_gate: float32 [4, 16384, 2048], P('dp', 'ctx'), may hold values from -1 to 0, as said below
- out_gate: bfloat16 [4, 16384, 2048], P('dp', 'ctx'), may hold values from -6 to 6
- cotangent: bfloat16 [4, 16384, 4096], P('dp', 'ctx'), may hold values from -0.0234375 to 0.0234375
Outputs:
- gated_hidden: bfloat16 [4, 16384, 2048], P('dp', 'ctx')
- weight_grad: float32 [2048, 4096], P('ctx')
Inputs may be any that keep to these rules, and one draw needn't show every extreme that they name: `log_gate`: every entry is negative.
All inputs are finite; a program needn't handle non-finite values.
Results may differ from a plain program's by a relative error of at most 0.0036.
Values sent between devices are 32-bit elements; how exact they have to be, the bound alone decides.
No kernel may reach another device: no remote copies, remote signals or barrier semaphores. Data moves between devices by JAX's collectives and lax.ppermute only.
A program may use at most 192 MiB of HBM per device.

v0:
```python
import functools

import jax
import jax.numpy as jnp
from jax import lax
from jax.experimental import pallas as pl
from jax.experimental.pallas import tpu as pltpu
from jax.sharding import Mesh, PartitionSpec as P

H = 16
DK = 128
D = 4096
BLOCK = 64
TOK = 512
BLOCKS = TOK // BLOCK
HALF = DK // 2
MSG = HALF + 8
COLS = 512
AXES = ("x", "y", "z", "c")
SIZES = (4, 4, 4, 2)
F32 = jnp.float32
BF16 = jnp.bfloat16
VMEM_LIMIT = 60 * 1024 * 1024
PIECE_LIMIT = 24 * 1024 * 1024
PRODUCT_LIMIT = 40 * 1024 * 1024
SMALL_LIMIT = 16 * 1024 * 1024

KINDS = {"y": (0, 1, 2), "z": (3, 4, 5), "x": (6, 7)}
GROUP = 2
PIECE = 4


def linear(p):
    return ((p[0] * 4 + p[1]) * 4 + p[2]) * 2 + p[3]


def places():
    return [(x, y, z, c) for x in range(4) for y in range(4) for z in range(4) for c in range(2)]


def shift_pairs(axis, by):
    at = AXES.index(axis)
    pairs = []
    for p in places():
        q = list(p)
        step = by(p[3]) if callable(by) else by
        q[at] = (q[at] + step) % SIZES[at]
        pairs.append((linear(p), linear(q)))
    return pairs


def send(array, axis, by):
    return lax.ppermute(array, AXES, shift_pairs(axis, by))


def params(limit=VMEM_LIMIT):
    return pltpu.CompilerParams(dimension_semantics=("arbitrary",), vmem_limit_bytes=limit)


def cost(flops, nbytes, transcendentals=0):
    return pl.CostEstimate(
        flops=int(flops), bytes_accessed=int(nbytes), transcendentals=int(transcendentals)
    )


def split(a):
    high = a.astype(BF16)
    return high, (a - high.astype(F32)).astype(BF16)


def dot_nt(a, b):
    return lax.dot_general(a, b, (((1,), (1,)), ((), ())), preferred_element_type=F32)


def dot_tn(a, b):
    return lax.dot_general(a, b, (((0,), (0,)), ((), ())), preferred_element_type=F32)


def dot_nt3(ah, al, b):
    n = ah.shape[0]
    high, low = split(b)
    both = dot_nt(jnp.concatenate([ah, al], axis=0), jnp.concatenate([high, low], axis=0))
    m = b.shape[0]
    return both[:n, :m] + (both[:n, m:] + both[n:, :m])


def block_cumsum(g):
    x = g.reshape(TOK // 8, 8, DK)
    row = lax.broadcasted_iota(jnp.int32, x.shape, 1)
    for shift in (1, 2, 4):
        x = x + jnp.where(row >= shift, pltpu.roll(x, shift, 1), 0.0)
    x = x.reshape(BLOCKS, BLOCK // 8, 8, DK)
    parts = []
    run = None
    for i in range(BLOCK // 8):
        part = x[:, i]
        if run is not None:
            part = part + run
        parts.append(part)
        run = part[:, 7:8, :]
    return jnp.stack(parts, axis=1).reshape(BLOCKS, BLOCK, DK), run


def state_kernel(
    where_ref, k_ref, v_ref, g_ref, cotan_ref, keep_ref, send_ref, cum_ref, wide_ref
):
    first = where_ref[3] == 0
    wide_ref[...] = cotan_ref[...].astype(F32)
    for head in range(GROUP):
        lanes = slice(head * DK, (head + 1) * DK)
        cum, end = block_cumsum(g_ref[:, lanes])
        cum_ref[:, lanes] = cum.reshape(TOK, DK)
        k = k_ref[:, lanes].astype(F32).reshape(BLOCKS, BLOCK, DK)
        kend = (k * jnp.exp(end - cum)).astype(BF16)
        decay = jnp.exp(end)
        total = end[0]
        state = None
        for j in range(BLOCKS):
            term = dot_tn(v_ref[j * BLOCK : (j + 1) * BLOCK, lanes], kend[j])
            if j:
                state = state * decay[j] + term
                total = total + end[j]
            else:
                state = term
        row = jnp.broadcast_to(jnp.exp(total), (8, DK))
        low, high = state[:HALF], state[HALF:]
        keep_ref[head, :HALF] = jnp.where(first, low, high)
        send_ref[head, :HALF] = jnp.where(first, high, low)
        keep_ref[head, HALF:] = row
        send_ref[head, HALF:] = row


def local_state(where, k, v, g, cotan):
    out = jax.ShapeDtypeStruct((H, MSG, DK), F32)
    steps = H // GROUP
    heads = pl.BlockSpec((TOK, GROUP * DK), lambda h, w: (0, h))
    wide = pl.BlockSpec((TOK, D // steps), lambda h, w: (0, h))
    return pl.pallas_call(
        state_kernel,
        grid_spec=pltpu.PrefetchScalarGridSpec(
            num_scalar_prefetch=1,
            grid=(steps,),
            in_specs=[heads] * 3 + [wide],
            out_specs=[pl.BlockSpec((GROUP, MSG, DK), lambda h, w: (h, 0, 0))] * 2
            + [heads, wide],
        ),
        out_shape=[out, out]
        + [jax.ShapeDtypeStruct((TOK, n), F32) for n in (H * DK, D)],
        compiler_params=params(),
        cost_estimate=cost(2 * TOK * DK * DK * H, 26e6, TOK * DK * H),
        name="local_state",
    )(where, k, v, g, cotan)


def core_kernel(q_ref, k_ref, v_ref, cum_ref, *rest):
    out_ref, high_ref, low_ref, token_ref = rest[-4:]
    token_ref[...] = jnp.zeros_like(token_ref)
    shape = (BLOCKS, BLOCK, DK)
    two = 2 * BLOCK
    rows = lax.broadcasted_iota(jnp.int32, (two, two), 0)
    cols = lax.broadcasted_iota(jnp.int32, (two, two), 1)
    mask = (rows >= cols) & ((rows >= BLOCK) == (cols >= BLOCK))
    for head in range(GROUP):
        lanes = slice(head * DK, (head + 1) * DK)
        cum = cum_ref[:, lanes].reshape(shape)
        end = cum[:, BLOCK - 1 : BLOCK, :]
        q = q_ref[:, lanes].astype(F32).reshape(shape)
        k = k_ref[:, lanes].astype(F32).reshape(shape)
        qdec = q * jnp.exp(cum)
        qround = qdec.astype(BF16)
        qrest = (qdec - qround.astype(F32)).astype(BF16)
        decay = jnp.exp(end)
        kfull = k * jnp.exp(-cum)
        kinc = kfull.astype(BF16)
        kend = (kfull * decay).astype(BF16)
        before = jnp.zeros((1, DK), F32)
        state = None
        for pair in range(BLOCKS // 2):
            span = slice(pair * two, (pair + 1) * two)
            qq = qround[2 * pair : 2 * pair + 2].reshape(two, DK)
            kk = kinc[2 * pair : 2 * pair + 2].reshape(two, DK)
            weights = jnp.where(mask, dot_nt(qq, kk), 0.0).astype(BF16)
            intra = jnp.dot(weights, v_ref[span, lanes], preferred_element_type=F32)
            for half in range(2):
                j = 2 * pair + half
                at = slice(j * BLOCK, (j + 1) * BLOCK)
                mine = intra[half * BLOCK : (half + 1) * BLOCK]
                if state is not None:
                    mine = mine + dot_nt3(qround[j], qrest[j], state)
                out_ref[at, lanes] = mine
                far = qdec[j] * jnp.exp(before)
                high, low = split(far)
                high_ref[at, lanes] = high
                low_ref[at, lanes] = low
                before = before + end[j]
                if j < BLOCKS - 1:
                    term = dot_tn(v_ref[at, lanes], kend[j])
                    state = term if state is None else state * decay[j] + term


def local_core(piece, q, k, v, cum, after, earlier):
    steps = PIECE // GROUP
    spec = pl.BlockSpec((TOK, GROUP * DK), lambda h: (0, h + piece * steps))
    extra = list(earlier) + [after]
    shape = (TOK, H * DK)
    return pl.pallas_call(
        core_kernel,
        grid=(steps,),
        in_specs=[spec] * 4 + [pl.BlockSpec(memory_space=pl.ANY)] * len(extra),
        out_specs=[spec] * 3 + [pl.BlockSpec((8, DK), lambda h: (0, 0))],
        out_shape=[jax.ShapeDtypeStruct(shape, t) for t in (F32, BF16, BF16)]
        + [jax.ShapeDtypeStruct((8, DK), F32)],
        input_output_aliases={4 + i: i for i in range(len(earlier))},
        compiler_params=params(PIECE_LIMIT),
        cost_estimate=cost(2 * TOK * DK * DK * PIECE * 8, 20e6, 4 * TOK * DK * PIECE),
        name="local_core",
    )(q, k, v, cum, *extra)


def chip_kernel(where_ref, keep_ref, got_ref, wide_ref, *outs):
    z, c = where_ref[2], where_ref[3]
    first = c == 0
    for d in range(4):
        base = lax.rem(z + d, 4) * 4
        a = keep_ref[pl.ds(base, 4)]
        b = got_ref[pl.ds(base, 4)]
        early = jnp.where(first, a, b)
        late = jnp.where(first, b, a)
        decay = late[:, HALF : HALF + 1, :]
        outs[d][:, :HALF] = early[:, :HALF] * decay + late[:, :HALF]
        outs[d][:, HALF:] = early[:, HALF:] * late[:, HALF:]


def row_kernel(where_ref, r0, r1, r2, r3, prefix_ref, total_ref, hold):
    z = where_ref[2]
    for d, ref in zip((0, 1, 3, 2), (r0, r1, r2, r3)):
        hold[lax.rem(z - d + 4, 4)] = ref[...]
    state = jnp.zeros((4, HALF, DK), F32)
    decay = jnp.ones((4, 8, DK), F32)
    for i in range(4):
        prefix_ref[i, :, :HALF] = state
        prefix_ref[i, :, HALF:] = decay
        item = hold[i]
        late = item[:, HALF:]
        state = state * late[:, :1, :] + item[:, :HALF]
        decay = decay * late
    total_ref[:, :HALF] = state
    total_ref[:, HALF:] = decay


def back_kernel(where_ref, prefix_ref, r0, r1, r2, r3, *rest):
    outs, hold = rest[:4], rest[4]
    y, z = where_ref[1], where_ref[2]
    for d, ref in zip((0, 1, 3, 2), (r0, r1, r2, r3)):
        hold[lax.rem(y - d + 4, 4)] = ref[...]
    state = jnp.zeros((4, HALF, DK), F32)
    for i in range(3):
        item = hold[i]
        new = state * item[:, HALF : HALF + 1, :] + item[:, :HALF]
        state = jnp.where(i < y, new, state)
    for d in range(4):
        prefix = prefix_ref[lax.rem(z + d, 4)]
        outs[d][...] = state * prefix[:, HALF : HALF + 1, :] + prefix[:, :HALF]


def core_start_kernel(where_ref, keep_ref, got_ref, r0, r1, r2, r3, mine_ref, other_ref):
    z, c = where_ref[2], where_ref[3]
    first = c == 0
    for d, ref in zip((0, 1, 3, 2), (r0, r1, r2, r3)):
        at = pl.ds(lax.rem(z - d + 4, 4) * 4, 4)
        chip = ref[...]
        early = jnp.where(first, keep_ref[at], got_ref[at])
        second = chip * early[:, HALF : HALF + 1, :] + early[:, :HALF]
        mine_ref[at] = jnp.where(first, chip, second)
        other_ref[at] = jnp.where(first, second, chip)


def small_call(kernel, where, arrays, outs, scratch=(), after=(), name=None):
    whole = [pl.BlockSpec(memory_space=pltpu.VMEM)]
    nbytes = sum(a.size * 4 for a in arrays)
    used = 1 + len(arrays)

    def body(*refs):
        kernel(*refs[:used], *refs[used + len(after) :])

    return pl.pallas_call(
        body,
        in_specs=[pl.BlockSpec(memory_space=pltpu.SMEM)]
        + whole * len(arrays)
        + [pl.BlockSpec(memory_space=pl.ANY)] * len(after),
        out_specs=whole * len(outs),
        out_shape=[jax.ShapeDtypeStruct(s, F32) for s in outs],
        scratch_shapes=[pltpu.VMEM(s, F32) for s in scratch],
        compiler_params=pltpu.CompilerParams(vmem_limit_bytes=SMALL_LIMIT),
        cost_estimate=cost(nbytes, 2 * nbytes),
        name=name,
    )(where, *arrays, *after)


def chip_total(where, keep, got, wide):
    vmem = pl.BlockSpec(memory_space=pltpu.VMEM)
    away = pl.BlockSpec(memory_space=pl.ANY)
    return pl.pallas_call(
        chip_kernel,
        in_specs=[pl.BlockSpec(memory_space=pltpu.SMEM), vmem, vmem, away],
        out_specs=[vmem] * 4 + [away],
        out_shape=[jax.ShapeDtypeStruct((4, MSG, DK), F32)] * 4
        + [jax.ShapeDtypeStruct(wide.shape, F32)],
        input_output_aliases={3: 4},
        compiler_params=pltpu.CompilerParams(vmem_limit_bytes=VMEM_LIMIT),
        cost_estimate=cost(H * MSG * DK * 4, 16 * H * MSG * DK),
        name="chip_total",
    )(where, keep, got, wide)


def attend(where, q, k, v, g, own):
    keep, away, cum, wide = local_state(where, k, v, g, own)
    got = send(away, "c", 1)
    msg = (4, MSG, DK)
    *parts, wide = chip_total(where, keep, got, wide)
    other = send(wide, "c", 1)
    arrived = around(parts, "z")
    *local, token = local_core(0, q, k, v, cum, parts[1], ())
    prefix, total = small_call(
        row_kernel, where, arrived, [(4,) + msg, msg], [(4,) + msg], [token], "row_total"
    )
    rows = around([total] * 4, "y")
    *local, token = local_core(1, q, k, v, cum, total, local)
    out = (4, HALF, DK)
    back = small_call(
        back_kernel, where, [prefix] + rows, [out] * 4, [(4,) + msg], [token], "row_start"
    )
    arrived = around(back, "z")
    *local, token = local_core(2, q, k, v, cum, back[1], local)
    mine, theirs = small_call(
        core_start_kernel,
        where,
        [keep, got] + arrived,
        [(H, HALF, DK)] * 2,
        after=[token],
        name="core_start",
    )
    *local, token = local_core(3, q, k, v, cum, theirs, local)
    return mine, send(theirs, "c", 1), local, other


def hidden_kernel(
    where_ref, out_ref, high_ref, low_ref, mine_ref, got_ref, gate_ref, hid_ref, keep_ref, send_ref
):
    first = where_ref[3] == 0
    for head in range(GROUP):
        lanes = slice(head * DK, (head + 1) * DK)
        a, b = mine_ref[head], got_ref[head]
        state = jnp.concatenate([jnp.where(first, a, b), jnp.where(first, b, a)], axis=0)
        core = out_ref[:, lanes] + dot_nt3(high_ref[:, lanes], low_ref[:, lanes], state)
        mean = jnp.mean(core * core, axis=-1, keepdims=True)
        gate = 0.5 * gate_ref[:, lanes].astype(F32)
        swish = gate + gate * jnp.tanh(gate)
        hidden = (core * lax.rsqrt(mean + 1e-05) * swish).astype(BF16)
        hid_ref[:, lanes] = hidden
        turned = hidden.astype(F32).T
        low, high = turned[:HALF], turned[HALF:]
        rows = slice(head * HALF, (head + 1) * HALF)
        keep_ref[rows, :] = jnp.where(first, low, high).astype(BF16)
        send_ref[rows, :] = jnp.where(first, high, low)


def gated(where, local, mine, got, gate):
    spec = pl.BlockSpec((TOK, GROUP * DK), lambda h, w: (0, h))
    state = pl.BlockSpec((GROUP, HALF, DK), lambda h, w: (h, 0, 0))
    turned = pl.BlockSpec((GROUP * HALF, TOK), lambda h, w: (h, 0))
    return pl.pallas_call(
        hidden_kernel,
        grid_spec=pltpu.PrefetchScalarGridSpec(
            num_scalar_prefetch=1,
            grid=(H // GROUP,),
            in_specs=[spec, spec, spec, state, state, spec],
            out_specs=[spec, turned, turned],
        ),
        out_shape=[
            jax.ShapeDtypeStruct((TOK, H * DK), BF16),
            jax.ShapeDtypeStruct((H * HALF, TOK), BF16),
            jax.ShapeDtypeStruct((H * HALF, TOK), F32),
        ],
        compiler_params=params(PIECE_LIMIT),
        cost_estimate=cost(6 * TOK * DK * DK * H, 17e6, 2 * TOK * DK * H),
        name="gated_hidden",
    )(where, *local, mine, got, gate)


CHUNK = {"x": (4, 4, 1, 16, TOK), "y": (1, 4, 4, 16, TOK), "z": (4, 1, 4, 16, TOK)}


def product_kernel(where_ref, keep_ref, got_ref, own_ref, other_ref, *refs):
    outs, left_ref, right_ref = refs[:-2], refs[-2], refs[-1]
    block = pl.program_id(0)
    core = where_ref[3]

    def chunk(ref, axis, j):
        if axis == "y":
            return ref[j]
        if axis == "z":
            return ref[:, j]
        return ref[:, :, j]

    for axis, blocks in KINDS.items():

        @pl.when(block == blocks[0])
        def _():
            me = where_ref[AXES.index(axis)]
            for t, d in enumerate((2, 1 + 2 * core, 3 - 2 * core, 0)):
                j = lax.rem(me + d, 4)
                for part, ref in enumerate((keep_ref, got_ref)):
                    both = chunk(ref, axis, j).reshape(256, TOK).astype(BF16)
                    lanes = slice(part * TOK, (part + 1) * TOK)
                    low, high = both[:128], both[128:]
                    left_ref[256 * t : 256 * t + 128, lanes] = jnp.where(core == 0, low, high)
                    left_ref[256 * t + 128 : 256 * t + 256, lanes] = jnp.where(core == 0, high, low)

    right_ref[:TOK, :] = own_ref[...]
    right_ref[TOK:, :] = other_ref[...].astype(BF16)
    total = jnp.dot(left_ref[...], right_ref[...], preferred_element_type=F32)
    opposite, after, before, mine = (total[256 * t : 256 * (t + 1)] for t in range(4))
    for n, blocks in enumerate(KINDS.values()):
        out = outs[7 * n : 7 * (n + 1)]

        @pl.when((block >= blocks[0]) & (block <= blocks[-1]))
        def _():
            out[0][...] = opposite[:128]
            out[1][...] = opposite[128:]
            out[2][...] = after[128:]
            out[3][...] = before[:128]
            out[4][...] = after[:128]
            out[5][...] = before[128:]
            out[6][...] = mine


def products(where, keep, got, own, other):
    rows = (128,) * 6 + (256,)
    out_specs, out_shape = [], []
    for blocks in KINDS.values():

        def column(i, w, low=blocks[0], high=blocks[-1]):
            return 0, jnp.clip(i, low, high) - low

        out_specs += [pl.BlockSpec((r, COLS), column) for r in rows]
        out_shape += [jax.ShapeDtypeStruct((r, COLS * len(blocks)), F32) for r in rows]
    cotan = pl.BlockSpec((TOK, COLS), lambda i, w: (0, i))
    whole = pl.BlockSpec((4, 4, 4, 16, TOK), lambda i, w: (0, 0, 0, 0, 0))
    outs = pl.pallas_call(
        product_kernel,
        grid_spec=pltpu.PrefetchScalarGridSpec(
            num_scalar_prefetch=1,
            grid=(D // COLS,),
            in_specs=[whole, whole, cotan, cotan],
            out_specs=out_specs,
            scratch_shapes=[pltpu.VMEM((1024, 2 * TOK), BF16), pltpu.VMEM((2 * TOK, COLS), BF16)],
        ),
        out_shape=out_shape,
        compiler_params=params(PRODUCT_LIMIT),
        cost_estimate=cost(4 * 1024 * TOK * D, 32e6),
        name="products",
    )(where, keep, got, own, other)
    return {axis: outs[7 * n : 7 * (n + 1)] for n, axis in enumerate(KINDS)}


def relay_kernel(a, b, *rest):
    out, token = rest[-2:]
    out[...] = a[...] + b[...]
    token[...] = jnp.zeros_like(token)


def relay(term, arrived, after):
    rows, width = term.shape
    spec = pl.BlockSpec((rows, COLS), lambda i: (0, i))
    return pl.pallas_call(
        relay_kernel,
        grid=(width // COLS,),
        in_specs=[spec] * 2 + [pl.BlockSpec(memory_space=pl.ANY)] * len(after),
        out_specs=[spec, pl.BlockSpec((8, DK), lambda i: (0, 0))],
        out_shape=[
            jax.ShapeDtypeStruct((rows, width), F32),
            jax.ShapeDtypeStruct((8, DK), F32),
        ],
        compiler_params=params(SMALL_LIMIT),
        cost_estimate=cost(rows * width, 12 * rows * width),
        name="relay",
    )(term, arrived, *after)


def second_kernel(axis, me, where_ref, mine, a, b, c, d, *rest):
    outs, token, total = rest[:4], rest[4], rest[5]
    start = pl.multiple_of(128 * where_ref[3], 128)
    total[pl.ds(start, 128), :] = mine[:128] + (a[...] + b[...])
    total[pl.ds(128 - start, 128), :] = mine[128:] + (c[...] + d[...])
    for d in range(4):
        j = lax.rem(where_ref[me] + d, 4)
        if axis == "z":
            for y in range(4):
                row = pl.multiple_of(64 * y + 16 * j, 16)
                outs[d][16 * y : 16 * (y + 1), :] = total[pl.ds(row, 16), :]
        else:
            outs[d][...] = total[pl.ds(pl.multiple_of(64 * j, 64), 64), :]
    token[...] = jnp.zeros_like(token)


def third_kernel(me, where_ref, a, b, c, d, *rest):
    outs, token, total = rest[:4], rest[4], rest[5]
    total[...] = a[...] + (b[...] + c[...]) + d[...]
    for i in range(4):
        row = pl.multiple_of(16 * lax.rem(where_ref[me] + i, 4), 16)
        outs[i][...] = total[pl.ds(row, 16), :]
    token[...] = jnp.zeros_like(token)


def last_kernel(where_ref, *refs):
    out = refs[-1]
    col = 0
    for n in range(3):
        a, b, c, d = refs[4 * n : 4 * (n + 1)]
        width = a.shape[1]
        out[:, col : col + width] = a[...] + (b[...] + c[...]) + d[...]
        col += width


def around(pieces, axis):
    return [pieces[0]] + [send(pieces[d], axis, d) for d in (1, 3, 2)]


def assemble_kernel(where_ref, *refs):
    for ref, d in zip(refs, (0, 1, 3, 2)):
        row = pl.multiple_of(lax.rem(where_ref[0] - d + 4, 4) * 16, 16)
        refs[-1][pl.ds(row, 16), :] = ref[...]


def shards(queries, key_rows, value_rows, log_gate, out_gate, cotangent):
    place = {name: lax.axis_index(name) for name in AXES}
    where = jnp.stack([place[name] for name in AXES]).astype(jnp.int32)
    q, k, v, g = queries[0], key_rows[0], value_rows[0], log_gate[0]
    own = cotangent[0]

    mine, got, local, other = attend(where, q, k, v, g, own)
    hidden, keep, away = gated(where, local, mine, got, out_gate[0])
    theirs = send(away, "c", 1).reshape(4, 4, 4, 16, TOK)
    keep = keep.reshape(4, 4, 4, 16, TOK)

    terms = products(where, keep, theirs, own, other)
    forward = lambda c: 1 - 2 * c
    back = lambda c: 2 * c - 1
    ahead = {axis: send(terms[axis][0], axis, forward) for axis in KINDS}
    behind = {axis: send(terms[axis][1], axis, back) for axis in KINDS}
    near = {
        axis: (send(terms[axis][2], axis, forward), send(terms[axis][3], axis, back))
        for axis in KINDS
    }
    order = ("x", "y", "z")
    token = ()
    low, high = {}, {}
    for axis in order:
        term, *token = relay(terms[axis][4], ahead[axis], token)
        low[axis] = send(term, axis, forward)
    for axis in order:
        term, *token = relay(terms[axis][5], behind[axis], token)
        high[axis] = send(term, axis, back)
    held, rounds = {}, {}
    for axis in KINDS:
        held[axis] = terms[axis][6], near[axis][1], low[axis], near[axis][0], high[axis]
    following = {"x": ("y", "z"), "y": ("z", "x"), "z": ("x", "y")}
    tail = [(8, DK)]

    def second(axis, after):
        a2 = following[axis][0]
        width = COLS * len(KINDS[axis])
        kernel = functools.partial(second_kernel, axis, AXES.index(a2))
        outs = [(64, width)] * 4 + tail
        *pieces, t = small_call(kernel, where, held[axis], outs, [(256, width)], after, "second")
        return around(pieces, a2), [t]

    def third(axis, arrived, after):
        a3 = following[axis][1]
        width = COLS * len(KINDS[axis])
        kernel = functools.partial(third_kernel, AXES.index(a3))
        outs = [(16, width)] * 4 + tail
        *pieces, t = small_call(kernel, where, arrived, outs, [(64, width)], after, "third")
        return around(pieces, a3), [t]

    rounds["x"], _ = second("x", ())
    rounds["x"], _ = third("x", rounds["x"], ())
    rounds["y"], token = second("y", ())
    rounds["z"], token = second("z", token)
    rounds["y"], token = third("y", rounds["y"], token)
    rounds["z"], token = third("z", rounds["z"], token)
    (mine,) = small_call(
        last_kernel, where, [r for axis in KINDS for r in rounds[axis]], [(16, D)], name="last"
    )
    pieces = around([mine] * 4, "x")
    weight_grad = pl.pallas_call(
        assemble_kernel,
        in_specs=[pl.BlockSpec(memory_space=pltpu.SMEM)]
        + [pl.BlockSpec(memory_space=pltpu.VMEM)] * len(pieces),
        out_specs=pl.BlockSpec(memory_space=pltpu.VMEM),
        out_shape=jax.ShapeDtypeStruct((64, D), F32),
        compiler_params=pltpu.CompilerParams(vmem_limit_bytes=SMALL_LIMIT),
        cost_estimate=cost(64 * D, 8 * 64 * D),
        name="assemble",
    )(where, *pieces)
    return hidden[None], weight_grad


def solution(mesh):
    fine = Mesh(mesh.devices.reshape(SIZES), AXES)
    rows = P("x", ("y", "z", "c"), None)
    return jax.shard_map(
        shards,
        mesh=fine,
        in_specs=(rows,) * 6,
        out_specs=(rows, P(("y", "z", "c"), None)),
        check_vma=False,
    )
```

profile of v0, /device:TPU:0, one launch (start us, length us, event | category | flops | bytes accessed | tf_op | source)
XLA Modules:
  0.0 234.6 jit_solution(14514925063382090481)
XLA Ops:
  1.2 13.5 %local_state.1 = (f32[16,72,128]{2,1,0:T(8,128)}, f32[16,72,128]{2,1,0:T(8,128)}, f32[512,2048]{1,0:T(8,128)}, f32[512,4096]{1,0:T(8,128)}) custom-call(s32[4]{0:T(128)} %pad_add_fusion.where_ref.refs_0_, bf16[512,2048]{1,0:T(8,128)(2,1)} %bitcast.13, bf16[512,2048]{1,0:T(8,128)(2,1)} %bitcast.18, f32[512,2048]{1,0:T(8,128)} %bitcast.29, ...), custom_call_target="tpu_custom_call" | custom-call | flops 268435456 | bytes 26000000 | tf_op jit(solution)/shard_map/local_state/pallas_call | solution.py:138
  14.8 2.2 collective-permute-done.got_ref.refs_2_
  17.8 2.3 chip_total.1
  20.2 4.1 %collective-permute-start.2 = (f32[4,72,128]{2,1,0:T(8,128)}, f32[4,72,128]{2,1,0:T(8,128)S(1)}, u32[]{:S(2)}, u32[]{:S(2)}) collective-permute-start(f32[4,72,128]{2,1,0:T(8,128)} %get-tuple-element.105), channel_id=1, source_target_pairs={{0,6},{1,7},{2,0},{3,1},{4,2},{5,3},{6,4},{7,5},{8,14},{9,15},{10,... | collective-permute-start | bytes 442376 | tf_op jit(solution)/shard_map/ppermute | solution.py:53
  25.6 2.2 copy-done
  27.8 1.6 copy-done.2
  29.4 1.6 copy-done.3
  31.9 4.5 %local_core.4 = (f32[512,2048]{1,0:T(8,128)S(1)}, bf16[512,2048]{1,0:T(8,128)(2,1)S(1)}, bf16[512,2048]{1,0:T(8,128)(2,1)S(1)}, f32[8,128]{1,0:T(8,128)S(1)}) custom-call(bf16[512,2048]{1,0:T(8,128)(2,1)S(1)} %bitcast.23, bf16[512,2048]{1,0:T(8,128)(2,1)S(1)} %bitcast.14, bf16[512,2048]{1,0:T(8,128)(2,1)S(1)} %bitcast.19, f32[512,2048]{1,0:T(8,128)S(1)} %copy-done, ...), custom_call_target="tpu_custom_call" | custom-call | flops 536870912 | bytes 20000000 | tf_op jit(solution)/shard_map/local_core/pallas_call | solution.py:206
  37.1 3.3 %collective-permute-start.6 = (f32[4,72,128]{2,1,0:T(8,128)S(1)}, f32[4,72,128]{2,1,0:T(8,128)S(1)}, u32[]{:S(2)}, u32[]{:S(2)}) collective-permute-start(f32[4,72,128]{2,1,0:T(8,128)S(1)} %get-tuple-element.108.rest_3_.refs_2_), channel_id=1, source_target_pairs={{0,16},{1,17},{2,18},{3,19},{4,20},{5,21},{6,22},{7,23},{8,24},{9,... | collective-permute-start | bytes 442376 | tf_op jit(solution)/shard_map/ppermute | solution.py:53
  42.4 4.5 %local_core.5 = (f32[512,2048]{1,0:T(8,128)S(1)}, bf16[512,2048]{1,0:T(8,128)(2,1)S(1)}, bf16[512,2048]{1,0:T(8,128)(2,1)S(1)}, f32[8,128]{1,0:T(8,128)S(1)}) custom-call(bf16[512,2048]{1,0:T(8,128)(2,1)S(1)} %bitcast.24, bf16[512,2048]{1,0:T(8,128)(2,1)S(1)} %bitcast.15, ...), custom_call_target="tpu_custom_call", output_to_operand_aliasing={{0}: (4, {}), {1}: (5, {}), {2}: (6, {})} | custom-call | flops 536870912 | bytes 20000000 | tf_op jit(solution)/shard_map/local_core/pallas_call | solution.py:206
  48.5 2.3 collective-permute-start.8
  50.8 2.1 collective-permute-start.9
  52.8 4.5 %local_core.6 = (f32[512,2048]{1,0:T(8,128)S(1)}, bf16[512,2048]{1,0:T(8,128)(2,1)S(1)}, bf16[512,2048]{1,0:T(8,128)(2,1)S(1)}, f32[8,128]{1,0:T(8,128)S(1)}) custom-call(bf16[512,2048]{1,0:T(8,128)(2,1)S(1)} %bitcast.25, bf16[512,2048]{1,0:T(8,128)(2,1)S(1)} %bitcast.16, ...), custom_call_target="tpu_custom_call", output_to_operand_aliasing={{0}: (4, {}), {1}: (5, {}), {2}: (6, {})} | custom-call | flops 536870912 | bytes 20000000 | tf_op jit(solution)/shard_map/local_core/pallas_call | solution.py:206
  59.8 5.1 %local_core.7 = (f32[512,2048]{1,0:T(8,128)S(1)}, bf16[512,2048]{1,0:T(8,128)(2,1)S(1)}, bf16[512,2048]{1,0:T(8,128)(2,1)S(1)}, f32[8,128]{1,0:T(8,128)}) custom-call(bf16[512,2048]{1,0:T(8,128)(2,1)S(1)} %bitcast.26, bf16[512,2048]{1,0:T(8,128)(2,1)S(1)} %bitcast.17, ...), custom_call_target="tpu_custom_call", output_to_operand_aliasing={{0}: (4, {}), {1}: (5, {}), {2}: (6, {})} | custom-call | flops 536870912 | bytes 20000000 | tf_op jit(solution)/shard_map/local_core/pallas_call | solution.py:206
  64.9 8.0 %gated_hidden.1 = (bf16[512,2048]{1,0:T(8,128)(2,1)}, bf16[1024,512]{1,0:T(8,128)(2,1)S(1)}, f32[1024,512]{1,0:T(8,128)S(1)}) custom-call(s32[4]{0:T(128)S(1)} %copy-done.12, f32[512,2048]{1,0:T(8,128)S(1)} %get-tuple-element.123.out_ref, bf16[512,2048]{1,0:T(8,128)(2,1)S(1)} %get-tuple-element.124.high_ref, ...), custom_call_target="tpu_custom_call" | custom-call | flops 805306368 | bytes 17000000 | tf_op jit(solution)/shard_map/gated_hidden/pallas_call | solution.py:372
  74.3 3.8 %collective-permute-done.11 = f32[1024,512]{1,0:T(8,128)S(1)} collective-permute-done((f32[1024,512]{1,0:T(8,128)S(1)}, f32[1024,512]{1,0:T(8,128)S(1)}, u32[]{:S(2)}, u32[]{:S(2)}) %collective-permute-start.11) | collective-permute-done | bytes 2097184 | tf_op jit(solution)/shard_map/ppermute | solution.py:53
  78.1 3.4 %copy-done.14 = f32[512,4096]{1,0:T(8,128)} copy-done((f32[512,4096]{1,0:T(8,128)}, f32[512,4096]{1,0:T(8,128)S(1)}, u32[]{:S(2)}) %copy-start.14) | copy-done | bytes 8388632
  82.1 17.3 %products.1 = (f32[128,1536]{1,0:T(8,128)S(1)}, f32[128,1536]{1,0:T(8,128)S(1)}, f32[128,1536]{1,0:T(8,128)S(1)}, f32[128,1536]{1,0:T(8,128)S(1)}, f32[128,1536]...) custom-call(s32[4]{0:T(128)S(1)} %copy-done.12, ...), custom_call_target="tpu_custom_call" | custom-call | flops 8589934592 | bytes 32000000 | tf_op jit(solution)/shard_map/products/pallas_call | solution.py:450
  101.0 1.7 collective-permute-start.19
  102.7 2.2 collective-permute-start.14
  107.9 5.7 %collective-permute-done.15.b = f32[128,1024]{1,0:T(8,128)S(1)} collective-permute-done((f32[128,1024]{1,0:T(8,128)S(1)}, f32[128,1024]{1,0:T(8,128)S(1)}, u32[]{:S(2)}, u32[]{:S(2)}) %collective-permute-start.15) | collective-permute-done | bytes 524320 | tf_op jit(solution)/shard_map/ppermute | solution.py:53
  113.9 3.6 %collective-permute-start.13 = (f32[128,1536]{1,0:T(8,128)S(1)}, f32[128,1536]{1,0:T(8,128)S(1)}, u32[]{:S(2)}, u32[]{:S(2)}) collective-permute-start(f32[128,1536]{1,0:T(8,128)S(1)} %get-tuple-element.132), channel_id=1, source_target_pairs={{0,24},{1,9},{2,26},{3,11},{4,28},{5,13},{6,30},{7,15},{8,0},{9,17... | collective-permute-start | bytes 2359304 | tf_op jit(solution)/shard_map/ppermute | solution.py:53
  117.5 2.0 collective-permute-done.39.refs_2_
  120.8 2.1 collective-permute-done.14.b
  122.8 2.2 collective-permute-start.17
  128.8 1.6 collective-permute-done.41.refs_4_
  130.4 2.2 collective-permute-start.16
  132.6 3.9 %collective-permute-done.13.refs_2_ = f32[128,1536]{1,0:T(8,128)S(1)} collective-permute-done((f32[128,1536]{1,0:T(8,128)S(1)}, f32[128,1536]{1,0:T(8,128)S(1)}, u32[]{:S(2)}, u32[]{:S(2)}) %collective-permute-start.13) | collective-permute-done | bytes 786464 | tf_op jit(solution)/shard_map/ppermute | solution.py:53
  136.4 3.7 %collective-permute-start.21 = (f32[128,1536]{1,0:T(8,128)S(1)}, f32[128,1536]{1,0:T(8,128)S(1)}, u32[]{:S(2)}, u32[]{:S(2)}) collective-permute-start(f32[128,1536]{1,0:T(8,128)S(1)} %get-tuple-element.149), channel_id=1, source_target_pairs={{0,24},{1,9},{2,26},{3,11},{4,28},{5,13},{6,30},{7,15},{8,0},{9,17... | collective-permute-start | bytes 2359304 | tf_op jit(solution)/shard_map/ppermute | solution.py:53
  143.2 5.1 %collective-permute-done.28.b = f32[128,1536]{1,0:T(8,128)S(1)} collective-permute-done((f32[128,1536]{1,0:T(8,128)S(1)}, f32[128,1536]{1,0:T(8,128)S(1)}, u32[]{:S(2)}, u32[]{:S(2)}) %collective-permute-start.28) | collective-permute-done | bytes 786464 | tf_op jit(solution)/shard_map/ppermute | solution.py:53
  149.2 8.8 %collective-permute-done.16.refs_3_ = f32[128,1536]{1,0:T(8,128)S(1)} collective-permute-done((f32[128,1536]{1,0:T(8,128)S(1)}, f32[128,1536]{1,0:T(8,128)S(1)}, u32[]{:S(2)}, u32[]{:S(2)}) %collective-permute-start.16) | collective-permute-done | bytes 786464 | tf_op jit(solution)/shard_map/ppermute | solution.py:53
  162.4 1.8 collective-permute-start.23
  164.1 4.4 %collective-permute-done.42.refs_5_ = f32[128,1024]{1,0:T(8,128)S(1)} collective-permute-done((f32[128,1024]{1,0:T(8,128)S(1)}, f32[128,1024]{1,0:T(8,128)S(1)}, u32[]{:S(2)}, u32[]{:S(2)}) %collective-permute-start.42) | collective-permute-done | bytes 524320 | tf_op jit(solution)/shard_map/ppermute | solution.py:53
  171.9 6.5 %collective-permute-done.29.refs_5_ = f32[128,1536]{1,0:T(8,128)S(1)} collective-permute-done((f32[128,1536]{1,0:T(8,128)S(1)}, f32[128,1536]{1,0:T(8,128)S(1)}, u32[]{:S(2)}, u32[]{:S(2)}) %collective-permute-start.29) | collective-permute-done | bytes 786464 | tf_op jit(solution)/shard_map/ppermute | solution.py:53
  179.9 2.8 %collective-permute-start.34 = (f32[64,1536]{1,0:T(8,128)S(1)}, f32[64,1536]{1,0:T(8,128)S(1)}, u32[]{:S(2)}, u32[]{:S(2)}) collective-permute-start(f32[64,1536]{1,0:T(8,128)S(1)} %get-tuple-element.170), channel_id=1, source_target_pairs={{0,96},{1,97},{2,98},{3,99},{4,100},{5,101},{6,102},{7,103},{8,104... | collective-permute-start | bytes 1179656 | tf_op jit(solution)/shard_map/ppermute | solution.py:53
  183.3 1.7 collective-permute-start.44
  185.0 2.1 collective-permute-start.45
  187.8 1.9 collective-permute-done.44.refs_3_
  189.7 3.4 %collective-permute-start.30 = (f32[16,1536]{1,0:T(8,128)S(1)}, f32[16,1536]{1,0:T(8,128)S(1)}, u32[]{:S(2)}, u32[]{:S(2)}) collective-permute-start(f32[16,1536]{1,0:T(8,128)S(1)} %get-tuple-element.165), channel_id=1, source_target_pairs={{0,32},{1,33},{2,34},{3,35},{4,36},{5,37},{6,38},{7,39},{8,40},{9,... | collective-permute-start | bytes 294920 | tf_op jit(solution)/shard_map/ppermute | solution.py:53
  194.2 3.9 %collective-permute-start.46 = (f32[16,1024]{1,0:T(8,128)S(1)}, f32[16,1024]{1,0:T(8,128)S(1)}, u32[]{:S(2)}, u32[]{:S(2)}) collective-permute-start(f32[16,1024]{1,0:T(8,128)S(1)} %get-tuple-element.187), channel_id=1, source_target_pairs={{0,2},{1,3},{2,4},{3,5},{4,6},{5,7},{6,0},{7,1},{8,10},{9,11},{10,... | collective-permute-start | bytes 196616 | tf_op jit(solution)/shard_map/ppermute | solution.py:53
  198.2 2.9 %collective-permute-start.47 = (f32[16,1024]{1,0:T(8,128)S(1)}, f32[16,1024]{1,0:T(8,128)S(1)}, u32[]{:S(2)}, u32[]{:S(2)}) collective-permute-start(f32[16,1024]{1,0:T(8,128)S(1)} %get-tuple-element.188), channel_id=1, source_target_pairs={{0,6},{1,7},{2,0},{3,1},{4,2},{5,3},{6,4},{7,5},{8,14},{9,15},{10,... | collective-permute-start | bytes 196616 | tf_op jit(solution)/shard_map/ppermute | solution.py:53
  201.1 1.6 collective-permute-start.48
  202.7 2.0 collective-permute-start.31
  208.6 2.4 %collective-permute-start.37 = (f32[16,1536]{1,0:T(8,128)S(1)}, f32[16,1536]{1,0:T(8,128)S(1)}, u32[]{:S(2)}, u32[]{:S(2)}) collective-permute-start(f32[16,1536]{1,0:T(8,128)S(1)} %get-tuple-element.175), channel_id=1, source_target_pairs={{0,24},{1,25},{2,26},{3,27},{4,28},{5,29},{6,30},{7,31},{8,0},{9,1... | collective-permute-start | bytes 294920 | tf_op jit(solution)/shard_map/ppermute | solution.py:53
  214.2 2.9 %collective-permute-done.38.refs_8_ = f32[16,1536]{1,0:T(8,128)S(1)} collective-permute-done((f32[16,1536]{1,0:T(8,128)S(1)}, f32[16,1536]{1,0:T(8,128)S(1)}, u32[]{:S(2)}, u32[]{:S(2)}) %collective-permute-start.38) | collective-permute-done | bytes 98336 | tf_op jit(solution)/shard_map/ppermute | solution.py:53
  217.7 2.9 %collective-permute-start.51 = (f32[16,4096]{1,0:T(8,128)S(1)}, f32[16,4096]{1,0:T(8,128)S(1)}, u32[]{:S(2)}, u32[]{:S(2)}) collective-permute-start(f32[16,4096]{1,0:T(8,128)S(1)} %last.1.refs_0_), channel_id=1, source_target_pairs={{0,64},{1,65},{2,66},{3,67},{4,68},{5,69},{6,70},{7,71},{8,72},{9,... | collective-permute-start | bytes 786440 | tf_op jit(solution)/shard_map/ppermute | solution.py:53
  222.6 5.9 %collective-permute-done.51.refs_3_ = f32[16,4096]{1,0:T(8,128)S(1)} collective-permute-done((f32[16,4096]{1,0:T(8,128)S(1)}, f32[16,4096]{1,0:T(8,128)S(1)}, u32[]{:S(2)}, u32[]{:S(2)}) %collective-permute-start.51) | collective-permute-done | bytes 262176 | tf_op jit(solution)/shard_map/ppermute | solution.py:53
  228.6 4.5 %collective-permute-done.50.refs_2_ = f32[16,4096]{1,0:T(8,128)S(1)} collective-permute-done((f32[16,4096]{1,0:T(8,128)S(1)}, f32[16,4096]{1,0:T(8,128)S(1)}, u32[]{:S(2)}, u32[]{:S(2)}) %collective-permute-start.50) | collective-permute-done | bytes 262176 | tf_op jit(solution)/shard_map/ppermute | solution.py:53
  (114 shorter events, 49.3 us)
Async XLA Ops:
  20.1 58.1 %collective-permute-start.12 = (f32[512,4096]{1,0:T(8,128)}, f32[512,4096]{1,0:T(8,128)S(1)}, u32[]{:S(2)}, u32[]{:S(2)}) collective-permute-start(f32[512,4096]{1,0:T(8,128)} %get-tuple-element.130), channel_id=1, source_target_pairs={{0,1},{1,0},{2,3},{3,2},{4,5},{5,4},{6,7},{7,6},{8,9},{9,8},{10,11... | collective-permute-start | bytes 25165832 | tf_op jit(solution)/shard_map/ppermute | solution.py:53
  20.2 16.2 %collective-permute-start.2 = (f32[4,72,128]{2,1,0:T(8,128)}, f32[4,72,128]{2,1,0:T(8,128)S(1)}, u32[]{:S(2)}, u32[]{:S(2)}) collective-permute-start(f32[4,72,128]{2,1,0:T(8,128)} %get-tuple-element.105), channel_id=1, source_target_pairs={{0,6},{1,7},{2,0},{3,1},{4,2},{5,3},{6,4},{7,5},{8,14},{9,15},{10,... | collective-permute-start | bytes 442376 | tf_op jit(solution)/shard_map/ppermute | solution.py:53
  24.3 12.0 %collective-permute-start.3 = (f32[4,72,128]{2,1,0:T(8,128)}, f32[4,72,128]{2,1,0:T(8,128)S(1)}, u32[]{:S(2)}, u32[]{:S(2)}) collective-permute-start(f32[4,72,128]{2,1,0:T(8,128)} %get-tuple-element.106), channel_id=1, source_target_pairs={{0,4},{1,5},{2,6},{3,7},{4,0},{5,1},{6,2},{7,3},{8,12},{9,13},{10,... | collective-permute-start | bytes 442376 | tf_op jit(solution)/shard_map/ppermute | solution.py:53
  24.3 12.0 %collective-permute-start.1 = (f32[4,72,128]{2,1,0:T(8,128)}, f32[4,72,128]{2,1,0:T(8,128)S(1)}, u32[]{:S(2)}, u32[]{:S(2)}) collective-permute-start(f32[4,72,128]{2,1,0:T(8,128)} %get-tuple-element.100.rest_0_), channel_id=1, source_target_pairs={{0,2},{1,3},{2,4},{3,5},{4,6},{5,7},{6,0},{7,1},{8,10},{9,11},{10,... | collective-permute-start | bytes 442376 | tf_op jit(solution)/shard_map/ppermute | solution.py:53
  37.1 9.8 %collective-permute-start.6 = (f32[4,72,128]{2,1,0:T(8,128)S(1)}, f32[4,72,128]{2,1,0:T(8,128)S(1)}, u32[]{:S(2)}, u32[]{:S(2)}) collective-permute-start(f32[4,72,128]{2,1,0:T(8,128)S(1)} %get-tuple-element.108.rest_3_.refs_2_), channel_id=1, source_target_pairs={{0,16},{1,17},{2,18},{3,19},{4,20},{5,21},{6,22},{7,23},{8,24},{9,... | collective-permute-start | bytes 442376 | tf_op jit(solution)/shard_map/ppermute | solution.py:53
  40.3 7.1 %collective-permute-start.5 = (f32[4,72,128]{2,1,0:T(8,128)S(1)}, f32[4,72,128]{2,1,0:T(8,128)S(1)}, u32[]{:S(2)}, u32[]{:S(2)}) collective-permute-start(f32[4,72,128]{2,1,0:T(8,128)S(1)} %get-tuple-element.108.rest_3_.refs_2_), channel_id=1, source_target_pairs={{0,24},{1,25},{2,26},{3,27},{4,28},{5,29},{6,30},{7,31},{8,0},{9,1... | collective-permute-start | bytes 442376 | tf_op jit(solution)/shard_map/ppermute | solution.py:53
  41.4 6.4 %collective-permute-start.4 = (f32[4,72,128]{2,1,0:T(8,128)S(1)}, f32[4,72,128]{2,1,0:T(8,128)S(1)}, u32[]{:S(2)}, u32[]{:S(2)}) collective-permute-start(f32[4,72,128]{2,1,0:T(8,128)S(1)} %get-tuple-element.108.rest_3_.refs_2_), channel_id=1, source_target_pairs={{0,8},{1,9},{2,10},{3,11},{4,12},{5,13},{6,14},{7,15},{8,16},{9,17... | collective-permute-start | bytes 442376 | tf_op jit(solution)/shard_map/ppermute | solution.py:53
  48.5 8.9 %collective-permute-start.8 = (f32[4,64,128]{2,1,0:T(8,128)S(1)}, f32[4,64,128]{2,1,0:T(8,128)S(1)}, u32[]{:S(2)}, u32[]{:S(2)}) collective-permute-start(f32[4,64,128]{2,1,0:T(8,128)S(1)} %get-tuple-element.119), channel_id=1, source_target_pairs={{0,6},{1,7},{2,0},{3,1},{4,2},{5,3},{6,4},{7,5},{8,14},{9,15},{10,... | collective-permute-start | bytes 393224 | tf_op jit(solution)/shard_map/ppermute | solution.py:53
  50.8 6.7 %collective-permute-start.9 = (f32[4,64,128]{2,1,0:T(8,128)S(1)}, f32[4,64,128]{2,1,0:T(8,128)S(1)}, u32[]{:S(2)}, u32[]{:S(2)}) collective-permute-start(f32[4,64,128]{2,1,0:T(8,128)S(1)} %get-tuple-element.120), channel_id=1, source_target_pairs={{0,4},{1,5},{2,6},{3,7},{4,0},{5,1},{6,2},{7,3},{8,12},{9,13},{10,... | collective-permute-start | bytes 393224 | tf_op jit(solution)/shard_map/ppermute | solution.py:53
  52.8 6.2 %collective-permute-start.7 = (f32[4,64,128]{2,1,0:T(8,128)S(1)}, f32[4,64,128]{2,1,0:T(8,128)S(1)}, u32[]{:S(2)}, u32[]{:S(2)}) collective-permute-start(f32[4,64,128]{2,1,0:T(8,128)S(1)} %get-tuple-element.114.rest_3_), channel_id=1, source_target_pairs={{0,2},{1,3},{2,4},{3,5},{4,6},{5,7},{6,0},{7,1},{8,10},{9,11},{10,... | collective-permute-start | bytes 393224 | tf_op jit(solution)/shard_map/ppermute | solution.py:53
  99.5 14.1 %collective-permute-start.15 = (f32[128,1024]{1,0:T(8,128)S(1)}, f32[128,1024]{1,0:T(8,128)S(1)}, u32[]{:S(2)}, u32[]{:S(2)}) collective-permute-start(f32[128,1024]{1,0:T(8,128)S(1)} %get-tuple-element.136), channel_id=1, source_target_pairs={{0,32},{1,97},{2,34},{3,99},{4,36},{5,101},{6,38},{7,103},{8,40},{... | collective-permute-start | bytes 1572872 | tf_op jit(solution)/shard_map/ppermute | solution.py:53
  101.0 13.0 %collective-permute-start.19 = (f32[128,1024]{1,0:T(8,128)S(1)}, f32[128,1024]{1,0:T(8,128)S(1)}, u32[]{:S(2)}, u32[]{:S(2)}) collective-permute-start(f32[128,1024]{1,0:T(8,128)S(1)} %get-tuple-element.143), channel_id=1, source_target_pairs={{0,96},{1,33},{2,98},{3,35},{4,100},{5,37},{6,102},{7,39},{8,104},... | collective-permute-start | bytes 1572872 | tf_op jit(solution)/shard_map/ppermute | solution.py:53
  102.7 20.1 %collective-permute-start.14 = (f32[128,1536]{1,0:T(8,128)S(1)}, f32[128,1536]{1,0:T(8,128)S(1)}, u32[]{:S(2)}, u32[]{:S(2)}) collective-permute-start(f32[128,1536]{1,0:T(8,128)S(1)} %get-tuple-element.134), channel_id=1, source_target_pairs={{0,8},{1,25},{2,10},{3,27},{4,12},{5,29},{6,14},{7,31},{8,16},{9,1... | collective-permute-start | bytes 2359304 | tf_op jit(solution)/shard_map/ppermute | solution.py:53
  104.9 14.7 %collective-permute-start.39 = (f32[128,1024]{1,0:T(8,128)S(1)}, f32[128,1024]{1,0:T(8,128)S(1)}, u32[]{:S(2)}, u32[]{:S(2)}) collective-permute-start(f32[128,1024]{1,0:T(8,128)S(1)} %get-tuple-element.178), channel_id=1, source_target_pairs={{0,96},{1,33},{2,98},{3,35},{4,100},{5,37},{6,102},{7,39},{8,104},... | collective-permute-start | bytes 1572872 | tf_op jit(solution)/shard_map/ppermute | solution.py:53
  106.4 18.6 %collective-permute-start.18 = (f32[128,1536]{1,0:T(8,128)S(1)}, f32[128,1536]{1,0:T(8,128)S(1)}, u32[]{:S(2)}, u32[]{:S(2)}) collective-permute-start(f32[128,1536]{1,0:T(8,128)S(1)} %get-tuple-element.141), channel_id=1, source_target_pairs={{0,24},{1,9},{2,26},{3,11},{4,28},{5,13},{6,30},{7,15},{8,0},{9,17... | collective-permute-start | bytes 2359304 | tf_op jit(solution)/shard_map/ppermute | solution.py:53
  113.5 13.2 %collective-permute-start.20 = (f32[128,1536]{1,0:T(8,128)S(1)}, f32[128,1536]{1,0:T(8,128)S(1)}, u32[]{:S(2)}, u32[]{:S(2)}) collective-permute-start(f32[128,1536]{1,0:T(8,128)S(1)} %get-tuple-element.145), channel_id=1, source_target_pairs={{0,2},{1,7},{2,4},{3,1},{4,6},{5,3},{6,0},{7,5},{8,10},{9,15},{10,... | collective-permute-start | bytes 2359304 | tf_op jit(solution)/shard_map/ppermute | solution.py:53
  113.9 22.5 %collective-permute-start.13 = (f32[128,1536]{1,0:T(8,128)S(1)}, f32[128,1536]{1,0:T(8,128)S(1)}, u32[]{:S(2)}, u32[]{:S(2)}) collective-permute-start(f32[128,1536]{1,0:T(8,128)S(1)} %get-tuple-element.132), channel_id=1, source_target_pairs={{0,24},{1,9},{2,26},{3,11},{4,28},{5,13},{6,30},{7,15},{8,0},{9,17... | collective-permute-start | bytes 2359304 | tf_op jit(solution)/shard_map/ppermute | solution.py:53
  119.6 10.8 %collective-permute-start.41 = (f32[128,1024]{1,0:T(8,128)S(1)}, f32[128,1024]{1,0:T(8,128)S(1)}, u32[]{:S(2)}, u32[]{:S(2)}) collective-permute-start(f32[128,1024]{1,0:T(8,128)S(1)} %get-tuple-element.180), channel_id=1, source_target_pairs={{0,32},{1,97},{2,34},{3,99},{4,36},{5,101},{6,38},{7,103},{8,40},{... | collective-permute-start | bytes 1572872 | tf_op jit(solution)/shard_map/ppermute | solution.py:53
  122.8 18.7 %collective-permute-start.17 = (f32[128,1536]{1,0:T(8,128)S(1)}, f32[128,1536]{1,0:T(8,128)S(1)}, u32[]{:S(2)}, u32[]{:S(2)}) collective-permute-start(f32[128,1536]{1,0:T(8,128)S(1)} %get-tuple-element.139), channel_id=1, source_target_pairs={{0,8},{1,25},{2,10},{3,27},{4,12},{5,29},{6,14},{7,31},{8,16},{9,1... | collective-permute-start | bytes 2359304 | tf_op jit(solution)/shard_map/ppermute | solution.py:53
  125.0 16.7 %collective-permute-start.25 = (f32[128,1536]{1,0:T(8,128)S(1)}, f32[128,1536]{1,0:T(8,128)S(1)}, u32[]{:S(2)}, u32[]{:S(2)}) collective-permute-start(f32[128,1536]{1,0:T(8,128)S(1)} %get-tuple-element.155), channel_id=1, source_target_pairs={{0,6},{1,3},{2,0},{3,5},{4,2},{5,7},{6,4},{7,1},{8,14},{9,11},{10,... | collective-permute-start | bytes 2359304 | tf_op jit(solution)/shard_map/ppermute | solution.py:53
  126.7 21.6 %collective-permute-start.28 = (f32[128,1536]{1,0:T(8,128)S(1)}, f32[128,1536]{1,0:T(8,128)S(1)}, u32[]{:S(2)}, u32[]{:S(2)}) collective-permute-start(f32[128,1536]{1,0:T(8,128)S(1)} %get-tuple-element.159), channel_id=1, source_target_pairs={{0,6},{1,3},{2,0},{3,5},{4,2},{5,7},{6,4},{7,1},{8,14},{9,11},{10,... | collective-permute-start | bytes 2359304 | tf_op jit(solution)/shard_map/ppermute | solution.py:53
  130.4 27.6 %collective-permute-start.16 = (f32[128,1536]{1,0:T(8,128)S(1)}, f32[128,1536]{1,0:T(8,128)S(1)}, u32[]{:S(2)}, u32[]{:S(2)}) collective-permute-start(f32[128,1536]{1,0:T(8,128)S(1)} %get-tuple-element.138), channel_id=1, source_target_pairs={{0,8},{1,25},{2,10},{3,27},{4,12},{5,29},{6,14},{7,31},{8,16},{9,1... | collective-permute-start | bytes 2359304 | tf_op jit(solution)/shard_map/ppermute | solution.py:53
  136.4 22.9 %collective-permute-start.21 = (f32[128,1536]{1,0:T(8,128)S(1)}, f32[128,1536]{1,0:T(8,128)S(1)}, u32[]{:S(2)}, u32[]{:S(2)}) collective-permute-start(f32[128,1536]{1,0:T(8,128)S(1)} %get-tuple-element.149), channel_id=1, source_target_pairs={{0,24},{1,9},{2,26},{3,11},{4,28},{5,13},{6,30},{7,15},{8,0},{9,17... | collective-permute-start | bytes 2359304 | tf_op jit(solution)/shard_map/ppermute | solution.py:53
  141.5 19.3 %collective-permute-start.27 = (f32[128,1536]{1,0:T(8,128)S(1)}, f32[128,1536]{1,0:T(8,128)S(1)}, u32[]{:S(2)}, u32[]{:S(2)}) collective-permute-start(f32[128,1536]{1,0:T(8,128)S(1)} %get-tuple-element.157), channel_id=1, source_target_pairs={{0,2},{1,7},{2,4},{3,1},{4,6},{5,3},{6,0},{7,5},{8,10},{9,15},{10,... | collective-permute-start | bytes 2359304 | tf_op jit(solution)/shard_map/ppermute | solution.py:53
  141.7 29.1 %collective-permute-start.26 = (f32[128,1536]{1,0:T(8,128)S(1)}, f32[128,1536]{1,0:T(8,128)S(1)}, u32[]{:S(2)}, u32[]{:S(2)}) collective-permute-start(f32[128,1536]{1,0:T(8,128)S(1)} %get-tuple-element.156), channel_id=1, source_target_pairs={{0,2},{1,7},{2,4},{3,1},{4,6},{5,3},{6,0},{7,5},{8,10},{9,15},{10,... | collective-permute-start | bytes 2359304 | tf_op jit(solution)/shard_map/ppermute | solution.py:53
  148.3 14.0 %collective-permute-start.40 = (f32[128,1024]{1,0:T(8,128)S(1)}, f32[128,1024]{1,0:T(8,128)S(1)}, u32[]{:S(2)}, u32[]{:S(2)}) collective-permute-start(f32[128,1024]{1,0:T(8,128)S(1)} %get-tuple-element.179), channel_id=1, source_target_pairs={{0,32},{1,97},{2,34},{3,99},{4,36},{5,101},{6,38},{7,103},{8,40},{... | collective-permute-start | bytes 1572872 | tf_op jit(solution)/shard_map/ppermute | solution.py:53
  158.0 20.5 %collective-permute-start.29 = (f32[128,1536]{1,0:T(8,128)S(1)}, f32[128,1536]{1,0:T(8,128)S(1)}, u32[]{:S(2)}, u32[]{:S(2)}) collective-permute-start(f32[128,1536]{1,0:T(8,128)S(1)} %get-tuple-element.161), channel_id=1, source_target_pairs={{0,6},{1,3},{2,0},{3,5},{4,2},{5,7},{6,4},{7,1},{8,14},{9,11},{10,... | collective-permute-start | bytes 2359304 | tf_op jit(solution)/shard_map/ppermute | solution.py:53
  159.3 9.2 %collective-permute-start.42 = (f32[128,1024]{1,0:T(8,128)S(1)}, f32[128,1024]{1,0:T(8,128)S(1)}, u32[]{:S(2)}, u32[]{:S(2)}) collective-permute-start(f32[128,1024]{1,0:T(8,128)S(1)} %get-tuple-element.181), channel_id=1, source_target_pairs={{0,96},{1,33},{2,98},{3,35},{4,100},{5,37},{6,102},{7,39},{8,104},... | collective-permute-start | bytes 1572872 | tf_op jit(solution)/shard_map/ppermute | solution.py:53
  160.8 21.9 %collective-permute-start.22 = (f32[64,1536]{1,0:T(8,128)S(1)}, f32[64,1536]{1,0:T(8,128)S(1)}, u32[]{:S(2)}, u32[]{:S(2)}) collective-permute-start(f32[64,1536]{1,0:T(8,128)S(1)} %get-tuple-element.151), channel_id=1, source_target_pairs={{0,2},{1,3},{2,4},{3,5},{4,6},{5,7},{6,0},{7,1},{8,10},{9,11},{10,... | collective-permute-start | bytes 1179656 | tf_op jit(solution)/shard_map/ppermute | solution.py:53
  162.4 21.0 %collective-permute-start.23 = (f32[64,1536]{1,0:T(8,128)S(1)}, f32[64,1536]{1,0:T(8,128)S(1)}, u32[]{:S(2)}, u32[]{:S(2)}) collective-permute-start(f32[64,1536]{1,0:T(8,128)S(1)} %get-tuple-element.152), channel_id=1, source_target_pairs={{0,6},{1,7},{2,0},{3,1},{4,2},{5,3},{6,4},{7,5},{8,14},{9,15},{10,... | collective-permute-start | bytes 1179656 | tf_op jit(solution)/shard_map/ppermute | solution.py:53
  168.5 16.5 %collective-permute-start.24 = (f32[64,1536]{1,0:T(8,128)S(1)}, f32[64,1536]{1,0:T(8,128)S(1)}, u32[]{:S(2)}, u32[]{:S(2)}) collective-permute-start(f32[64,1536]{1,0:T(8,128)S(1)} %get-tuple-element.153), channel_id=1, source_target_pairs={{0,4},{1,5},{2,6},{3,7},{4,0},{5,1},{6,2},{7,3},{8,12},{9,13},{10,... | collective-permute-start | bytes 1179656 | tf_op jit(solution)/shard_map/ppermute | solution.py:53
  170.8 9.1 %collective-permute-start.43 = (f32[64,1024]{1,0:T(8,128)S(1)}, f32[64,1024]{1,0:T(8,128)S(1)}, u32[]{:S(2)}, u32[]{:S(2)}) collective-permute-start(f32[64,1024]{1,0:T(8,128)S(1)} %get-tuple-element.183), channel_id=1, source_target_pairs={{0,8},{1,9},{2,10},{3,11},{4,12},{5,13},{6,14},{7,15},{8,16},{9,17... | collective-permute-start | bytes 786440 | tf_op jit(solution)/shard_map/ppermute | solution.py:53
  179.4 18.7 %collective-permute-start.33 = (f32[64,1536]{1,0:T(8,128)S(1)}, f32[64,1536]{1,0:T(8,128)S(1)}, u32[]{:S(2)}, u32[]{:S(2)}) collective-permute-start(f32[64,1536]{1,0:T(8,128)S(1)} %get-tuple-element.169), channel_id=1, source_target_pairs={{0,32},{1,33},{2,34},{3,35},{4,36},{5,37},{6,38},{7,39},{8,40},{9,... | collective-permute-start | bytes 1179656 | tf_op jit(solution)/shard_map/ppermute | solution.py:53
  179.9 21.2 %collective-permute-start.34 = (f32[64,1536]{1,0:T(8,128)S(1)}, f32[64,1536]{1,0:T(8,128)S(1)}, u32[]{:S(2)}, u32[]{:S(2)}) collective-permute-start(f32[64,1536]{1,0:T(8,128)S(1)} %get-tuple-element.170), channel_id=1, source_target_pairs={{0,96},{1,97},{2,98},{3,99},{4,100},{5,101},{6,102},{7,103},{8,104... | collective-permute-start | bytes 1179656 | tf_op jit(solution)/shard_map/ppermute | solution.py:53
  182.8 19.9 %collective-permute-start.35 = (f32[64,1536]{1,0:T(8,128)S(1)}, f32[64,1536]{1,0:T(8,128)S(1)}, u32[]{:S(2)}, u32[]{:S(2)}) collective-permute-start(f32[64,1536]{1,0:T(8,128)S(1)} %get-tuple-element.171), channel_id=1, source_target_pairs={{0,64},{1,65},{2,66},{3,67},{4,68},{5,69},{6,70},{7,71},{8,72},{9,... | collective-permute-start | bytes 1179656 | tf_op jit(solution)/shard_map/ppermute | solution.py:53
  183.3 6.4 %collective-permute-start.44 = (f32[64,1024]{1,0:T(8,128)S(1)}, f32[64,1024]{1,0:T(8,128)S(1)}, u32[]{:S(2)}, u32[]{:S(2)}) collective-permute-start(f32[64,1024]{1,0:T(8,128)S(1)} %get-tuple-element.184), channel_id=1, source_target_pairs={{0,24},{1,25},{2,26},{3,27},{4,28},{5,29},{6,30},{7,31},{8,0},{9,1... | collective-permute-start | bytes 786440 | tf_op jit(solution)/shard_map/ppermute | solution.py:53
  185.0 8.1 %collective-permute-start.45 = (f32[64,1024]{1,0:T(8,128)S(1)}, f32[64,1024]{1,0:T(8,128)S(1)}, u32[]{:S(2)}, u32[]{:S(2)}) collective-permute-start(f32[64,1024]{1,0:T(8,128)S(1)} %get-tuple-element.185), channel_id=1, source_target_pairs={{0,16},{1,17},{2,18},{3,19},{4,20},{5,21},{6,22},{7,23},{8,24},{9,... | collective-permute-start | bytes 786440 | tf_op jit(solution)/shard_map/ppermute | solution.py:53
  189.7 21.3 %collective-permute-start.30 = (f32[16,1536]{1,0:T(8,128)S(1)}, f32[16,1536]{1,0:T(8,128)S(1)}, u32[]{:S(2)}, u32[]{:S(2)}) collective-permute-start(f32[16,1536]{1,0:T(8,128)S(1)} %get-tuple-element.165), channel_id=1, source_target_pairs={{0,32},{1,33},{2,34},{3,35},{4,36},{5,37},{6,38},{7,39},{8,40},{9,... | collective-permute-start | bytes 294920 | tf_op jit(solution)/shard_map/ppermute | solution.py:53
  194.2 11.6 %collective-permute-start.46 = (f32[16,1024]{1,0:T(8,128)S(1)}, f32[16,1024]{1,0:T(8,128)S(1)}, u32[]{:S(2)}, u32[]{:S(2)}) collective-permute-start(f32[16,1024]{1,0:T(8,128)S(1)} %get-tuple-element.187), channel_id=1, source_target_pairs={{0,2},{1,3},{2,4},{3,5},{4,6},{5,7},{6,0},{7,1},{8,10},{9,11},{10,... | collective-permute-start | bytes 196616 | tf_op jit(solution)/shard_map/ppermute | solution.py:53
  198.2 9.1 %collective-permute-start.47 = (f32[16,1024]{1,0:T(8,128)S(1)}, f32[16,1024]{1,0:T(8,128)S(1)}, u32[]{:S(2)}, u32[]{:S(2)}) collective-permute-start(f32[16,1024]{1,0:T(8,128)S(1)} %get-tuple-element.188), channel_id=1, source_target_pairs={{0,6},{1,7},{2,0},{3,1},{4,2},{5,3},{6,4},{7,5},{8,14},{9,15},{10,... | collective-permute-start | bytes 196616 | tf_op jit(solution)/shard_map/ppermute | solution.py:53
  201.1 7.5 %collective-permute-start.48 = (f32[16,1024]{1,0:T(8,128)S(1)}, f32[16,1024]{1,0:T(8,128)S(1)}, u32[]{:S(2)}, u32[]{:S(2)}) collective-permute-start(f32[16,1024]{1,0:T(8,128)S(1)} %get-tuple-element.189), channel_id=1, source_target_pairs={{0,4},{1,5},{2,6},{3,7},{4,0},{5,1},{6,2},{7,3},{8,12},{9,13},{10,... | collective-permute-start | bytes 196616 | tf_op jit(solution)/shard_map/ppermute | solution.py:53
  202.7 9.8 %collective-permute-start.31 = (f32[16,1536]{1,0:T(8,128)S(1)}, f32[16,1536]{1,0:T(8,128)S(1)}, u32[]{:S(2)}, u32[]{:S(2)}) collective-permute-start(f32[16,1536]{1,0:T(8,128)S(1)} %get-tuple-element.166), channel_id=1, source_target_pairs={{0,96},{1,97},{2,98},{3,99},{4,100},{5,101},{6,102},{7,103},{8,104... | collective-permute-start | bytes 294920 | tf_op jit(solution)/shard_map/ppermute | solution.py:53
  205.8 6.9 %collective-permute-start.32 = (f32[16,1536]{1,0:T(8,128)S(1)}, f32[16,1536]{1,0:T(8,128)S(1)}, u32[]{:S(2)}, u32[]{:S(2)}) collective-permute-start(f32[16,1536]{1,0:T(8,128)S(1)} %get-tuple-element.167), channel_id=1, source_target_pairs={{0,64},{1,65},{2,66},{3,67},{4,68},{5,69},{6,70},{7,71},{8,72},{9,... | collective-permute-start | bytes 294920 | tf_op jit(solution)/shard_map/ppermute | solution.py:53
  207.3 6.4 %collective-permute-start.36 = (f32[16,1536]{1,0:T(8,128)S(1)}, f32[16,1536]{1,0:T(8,128)S(1)}, u32[]{:S(2)}, u32[]{:S(2)}) collective-permute-start(f32[16,1536]{1,0:T(8,128)S(1)} %get-tuple-element.174), channel_id=1, source_target_pairs={{0,8},{1,9},{2,10},{3,11},{4,12},{5,13},{6,14},{7,15},{8,16},{9,17... | collective-permute-start | bytes 294920 | tf_op jit(solution)/shard_map/ppermute | solution.py:53
  211.0 6.1 %collective-permute-start.38 = (f32[16,1536]{1,0:T(8,128)S(1)}, f32[16,1536]{1,0:T(8,128)S(1)}, u32[]{:S(2)}, u32[]{:S(2)}) collective-permute-start(f32[16,1536]{1,0:T(8,128)S(1)} %get-tuple-element.176), channel_id=1, source_target_pairs={{0,16},{1,17},{2,18},{3,19},{4,20},{5,21},{6,22},{7,23},{8,24},{9,... | collective-permute-start | bytes 294920 | tf_op jit(solution)/shard_map/ppermute | solution.py:53
  217.7 10.8 %collective-permute-start.51 = (f32[16,4096]{1,0:T(8,128)S(1)}, f32[16,4096]{1,0:T(8,128)S(1)}, u32[]{:S(2)}, u32[]{:S(2)}) collective-permute-start(f32[16,4096]{1,0:T(8,128)S(1)} %last.1.refs_0_), channel_id=1, source_target_pairs={{0,64},{1,65},{2,66},{3,67},{4,68},{5,69},{6,70},{7,71},{8,72},{9,... | collective-permute-start | bytes 786440 | tf_op jit(solution)/shard_map/ppermute | solution.py:53
  220.6 12.4 %collective-permute-start.50 = (f32[16,4096]{1,0:T(8,128)S(1)}, f32[16,4096]{1,0:T(8,128)S(1)}, u32[]{:S(2)}, u32[]{:S(2)}) collective-permute-start(f32[16,4096]{1,0:T(8,128)S(1)} %last.1.refs_0_), channel_id=1, source_target_pairs={{0,96},{1,97},{2,98},{3,99},{4,100},{5,101},{6,102},{7,103},{8,104... | collective-permute-start | bytes 786440 | tf_op jit(solution)/shard_map/ppermute | solution.py:53
  221.9 11.1 %collective-permute-start.49 = (f32[16,4096]{1,0:T(8,128)S(1)}, f32[16,4096]{1,0:T(8,128)S(1)}, u32[]{:S(2)}, u32[]{:S(2)}) collective-permute-start(f32[16,4096]{1,0:T(8,128)S(1)} %last.1.refs_0_), channel_id=1, source_target_pairs={{0,32},{1,33},{2,34},{3,35},{4,36},{5,37},{6,38},{7,39},{8,40},{9,... | collective-permute-start | bytes 786440 | tf_op jit(solution)/shard_map/ppermute | solution.py:53
  (20 other events, 116.3 us)
where the time goes:
time: 235 us
  starting transfers between devices  79.7 us (34%)
  Pallas kernels  72.3 us (31%)
  waiting for transfers between devices  69 us (29%)
  local copies, waits for them, and re-layouts  12.1 us (5%)
    ppermute x52, starting transfers between devices, send(): return lax.ppermute(array, AXES, shift_pairs(axis, by))  79.7 us
    ppermute x52, waiting for transfers between devices, send(): return lax.ppermute(array, AXES, shift_pairs(axis, by))  69 us
    pallas_call x4, Pallas kernels, local_core(): pl.pallas_call(core_kernel, grid=(steps,), in_specs=[spec] * 4 + [pl.Bloc...  18.5 us
    pallas_call x1, Pallas kernels, products(): pl.pallas_call(product_kernel, grid_spec=pltpu.PrefetchScalarGridSpec(num...  17.3 us
    pallas_call x1, Pallas kernels, local_state(): pl.pallas_call(state_kernel, grid_spec=pltpu.PrefetchScalarGridSpec(num_s...  13.5 us
    unnamed x32, local copies, waits for them, and re-layouts  12.1 us
    pallas_call x10, Pallas kernels, small_call(): pl.pallas_call(body, in_specs=[pl.BlockSpec(memory_space=pltpu.SMEM)] + w...  8.77 us
    pallas_call x1, Pallas kernels, gated(): pl.pallas_call(hidden_kernel, grid_spec=pltpu.PrefetchScalarGridSpec(num_...  8.02 us
  transfers between devices with their start and end apart: 52, of which 27 were waited for; matrix products, arithmetic and copies ran while one was open for 0% of the time, Pallas kernels for 16%

commit v1 on v0

--- a/solution.py
+++ b/solution.py
@@ -22,7 +22,7 @@
 BF16 = jnp.bfloat16
 VMEM_LIMIT = 60 * 1024 * 1024
 PIECE_LIMIT = 24 * 1024 * 1024
-PRODUCT_LIMIT = 40 * 1024 * 1024
+PRODUCT_LIMIT = 28 * 1024 * 1024
 SMALL_LIMIT = 16 * 1024 * 1024
 
 KINDS = {"y": (0, 1, 2), "z": (3, 4, 5), "x": (6, 7)}
@@ -47,6 +47,16 @@
         q[at] = (q[at] + step) % SIZES[at]
         pairs.append((linear(p), linear(q)))
     return pairs
+
+
+def swap(array, axis, distance):
+    at = AXES.index(axis)
+    pairs = []
+    for p in places():
+        q = list(p)
+        q[at] ^= distance
+        pairs.append((linear(p), linear(q)))
+    return lax.ppermute(array, AXES, pairs)
 
 
 def send(array, axis, by):
@@ -146,7 +156,7 @@
         ),
         out_shape=[out, out]
         + [jax.ShapeDtypeStruct((TOK, n), F32) for n in (H * DK, D)],
-        compiler_params=params(),
+        compiler_params=params(PIECE_LIMIT),
         cost_estimate=cost(2 * TOK * DK * DK * H, 26e6, TOK * DK * H),
         name="local_state",
     )(where, k, v, g, cotan)
@@ -307,7 +317,7 @@
         out_shape=[jax.ShapeDtypeStruct((4, MSG, DK), F32)] * 4
         + [jax.ShapeDtypeStruct(wide.shape, F32)],
         input_output_aliases={3: 4},
-        compiler_params=pltpu.CompilerParams(vmem_limit_bytes=VMEM_LIMIT),
+        compiler_params=pltpu.CompilerParams(vmem_limit_bytes=SMALL_LIMIT),
         cost_estimate=cost(H * MSG * DK * 4, 16 * H * MSG * DK),
         name="chip_total",
     )(where, keep, got, wide)
@@ -391,77 +401,67 @@
 CHUNK = {"x": (4, 4, 1, 16, TOK), "y": (1, 4, 4, 16, TOK), "z": (4, 1, 4, 16, TOK)}
 
 
-def product_kernel(where_ref, keep_ref, got_ref, own_ref, other_ref, *refs):
-    outs, left_ref, right_ref = refs[:-2], refs[-2], refs[-1]
-    block = pl.program_id(0)
+def product_kernel(axis, where_ref, keep_ref, got_ref, own_ref, other_ref, *refs):
+    outs, token_ref, left_ref, right_ref = refs[-8:-3], refs[-3], refs[-2], refs[-1]
     core = where_ref[3]
-
-    def chunk(ref, axis, j):
+    token_ref[...] = jnp.zeros_like(token_ref)
+
+    def chunk(ref, j):
         if axis == "y":
             return ref[j]
         if axis == "z":
             return ref[:, j]
         return ref[:, :, j]
 
-    for axis, blocks in KINDS.items():
-
-        @pl.when(block == blocks[0])
-        def _():
-            me = where_ref[AXES.index(axis)]
-            for t, d in enumerate((2, 1 + 2 * core, 3 - 2 * core, 0)):
-                j = lax.rem(me + d, 4)
-                for part, ref in enumerate((keep_ref, got_ref)):
-                    both = chunk(ref, axis, j).reshape(256, TOK).astype(BF16)
-                    lanes = slice(part * TOK, (part + 1) * TOK)
-                    low, high = both[:128], both[128:]
-                    left_ref[256 * t : 256 * t + 128, lanes] = jnp.where(core == 0, low, high)
-                    left_ref[256 * t + 128 : 256 * t + 256, lanes] = jnp.where(core == 0, high, low)
+    @pl.when(pl.program_id(0) == 0)
+    def _():
+        me = where_ref[AXES.index(axis)]
+        for t, d in enumerate((2, 1 + 2 * core, 3 - 2 * core, 0)):
+            j = lax.rem(me + d, 4)
+            for part, ref in enumerate((keep_ref, got_ref)):
+                both = chunk(ref, j).reshape(256, TOK).astype(BF16)
+                lanes = slice(part * TOK, (part + 1) * TOK)
+                low, high = both[:128], both[128:]
+                left_ref[256 * t : 256 * t + 128, lanes] = jnp.where(core == 0, low, high)
+                left_ref[256 * t + 128 : 256 * t + 256, lanes] = jnp.where(core == 0, high, low)
 
     right_ref[:TOK, :] = own_ref[...]
     right_ref[TOK:, :] = other_ref[...].astype(BF16)
     total = jnp.dot(left_ref[...], right_ref[...], preferred_element_type=F32)
     opposite, after, before, mine = (total[256 * t : 256 * (t + 1)] for t in range(4))
-    for n, blocks in enumerate(KINDS.values()):
-        out = outs[7 * n : 7 * (n + 1)]
-
-        @pl.when((block >= blocks[0]) & (block <= blocks[-1]))
-        def _():
-            out[0][...] = opposite[:128]
-            out[1][...] = opposite[128:]
-            out[2][...] = after[128:]
-            out[3][...] = before[:128]
-            out[4][...] = after[:128]
-            out[5][...] = before[128:]
-            out[6][...] = mine
-
-
-def products(where, keep, got, own, other):
-    rows = (128,) * 6 + (256,)
-    out_specs, out_shape = [], []
-    for blocks in KINDS.values():
-
-        def column(i, w, low=blocks[0], high=blocks[-1]):
-            return 0, jnp.clip(i, low, high) - low
-
-        out_specs += [pl.BlockSpec((r, COLS), column) for r in rows]
-        out_shape += [jax.ShapeDtypeStruct((r, COLS * len(blocks)), F32) for r in rows]
-    cotan = pl.BlockSpec((TOK, COLS), lambda i, w: (0, i))
+    outs[0][...] = opposite[:128]
+    outs[1][...] = opposite[128:]
+    outs[2][...] = after
+    outs[3][...] = before
+    outs[4][...] = mine
+
+
+def products(axis, where, keep, got, own, other, after):
+    blocks = KINDS[axis]
+    rows = (128,) * 2 + (256,) * 3
+    cotan = pl.BlockSpec((TOK, COLS), lambda i, w: (0, blocks[0] + i))
     whole = pl.BlockSpec((4, 4, 4, 16, TOK), lambda i, w: (0, 0, 0, 0, 0))
-    outs = pl.pallas_call(
-        product_kernel,
+    width = COLS * len(blocks)
+    return pl.pallas_call(
+        functools.partial(product_kernel, axis),
         grid_spec=pltpu.PrefetchScalarGridSpec(
             num_scalar_prefetch=1,
-            grid=(D // COLS,),
-            in_specs=[whole, whole, cotan, cotan],
-            out_specs=out_specs,
-            scratch_shapes=[pltpu.VMEM((1024, 2 * TOK), BF16), pltpu.VMEM((2 * TOK, COLS), BF16)],
+            grid=(len(blocks),),
+            in_specs=[whole, whole, cotan, cotan]
+            + [pl.BlockSpec(memory_space=pl.ANY)] * len(after),
+            out_specs=[pl.BlockSpec((r, COLS), lambda i, w: (0, i)) for r in rows]
+            + [pl.BlockSpec((8, DK), lambda i, w: (0, 0))],
+            scratch_shapes=[
+                pltpu.VMEM((1024, 2 * TOK), BF16),
+                pltpu.VMEM((2 * TOK, COLS), BF16),
+            ],
         ),
-        out_shape=out_shape,
+        out_shape=[jax.ShapeDtypeStruct((r, width), F32) for r in rows]
+        + [jax.ShapeDtypeStruct((8, DK), F32)],
         compiler_params=params(PRODUCT_LIMIT),
-        cost_estimate=cost(4 * 1024 * TOK * D, 32e6),
-        name="products",
-    )(where, keep, got, own, other)
-    return {axis: outs[7 * n : 7 * (n + 1)] for n, axis in enumerate(KINDS)}
+        cost_estimate=cost(4 * 1024 * TOK * width, 8000 * width),
+        name="products_" + axis,
+    )(where, keep, got, own, other, *after)
 
 
 def relay_kernel(a, b, *rest):
@@ -470,56 +470,63 @@
     token[...] = jnp.zeros_like(token)
 
 
-def relay(term, arrived, after):
-    rows, width = term.shape
-    spec = pl.BlockSpec((rows, COLS), lambda i: (0, i))
+def relay(term, arrived, half, after):
+    width = term.shape[1]
+    spec = pl.BlockSpec((128, COLS), lambda i: (half, i))
+    came = pl.BlockSpec((128, COLS), lambda i: (0, i))
     return pl.pallas_call(
         relay_kernel,
         grid=(width // COLS,),
-        in_specs=[spec] * 2 + [pl.BlockSpec(memory_space=pl.ANY)] * len(after),
+        in_specs=[spec, came] + [pl.BlockSpec(memory_space=pl.ANY)] * len(after),
         out_specs=[spec, pl.BlockSpec((8, DK), lambda i: (0, 0))],
         out_shape=[
-            jax.ShapeDtypeStruct((rows, width), F32),
+            jax.ShapeDtypeStruct(term.shape, F32),
             jax.ShapeDtypeStruct((8, DK), F32),
         ],
+        input_output_aliases={0: 0},
         compiler_params=params(SMALL_LIMIT),
-        cost_estimate=cost(rows * width, 12 * rows * width),
+        cost_estimate=cost(128 * width, 12 * 128 * width),
         name="relay",
     )(term, arrived, *after)
 
 
-def second_kernel(axis, me, where_ref, mine, a, b, c, d, *rest):
+def second_kernel(axis, me, where_ref, mine, a, b, *rest):
     outs, token, total = rest[:4], rest[4], rest[5]
-    start = pl.multiple_of(128 * where_ref[3], 128)
-    total[pl.ds(start, 128), :] = mine[:128] + (a[...] + b[...])
-    total[pl.ds(128 - start, 128), :] = mine[128:] + (c[...] + d[...])
-    for d in range(4):
-        j = lax.rem(where_ref[me] + d, 4)
+    core = where_ref[3]
+    start = pl.multiple_of(128 * core, 128)
+    total[pl.ds(start, 128), :] = mine[:128] + (a[:128] + b[:128])
+    total[pl.ds(128 - start, 128), :] = mine[128:] + (a[128:] + b[128:])
+    for t in range(4):
+        j = lax.rem(where_ref[me] + jnp.where(core == 0, 7 - t, 1 + t), 4)
         if axis == "z":
             for y in range(4):
                 row = pl.multiple_of(64 * y + 16 * j, 16)
-                outs[d][16 * y : 16 * (y + 1), :] = total[pl.ds(row, 16), :]
+                outs[t][16 * y : 16 * (y + 1), :] = total[pl.ds(row, 16), :]
         else:
-            outs[d][...] = total[pl.ds(pl.multiple_of(64 * j, 64), 64), :]
+            outs[t][...] = total[pl.ds(pl.multiple_of(64 * j, 64), 64), :]
     token[...] = jnp.zeros_like(token)
 
 
-def third_kernel(me, where_ref, a, b, c, d, *rest):
-    outs, token, total = rest[:4], rest[4], rest[5]
-    total[...] = a[...] + (b[...] + c[...]) + d[...]
-    for i in range(4):
-        row = pl.multiple_of(16 * lax.rem(where_ref[me] + i, 4), 16)
-        outs[i][...] = total[pl.ds(row, 16), :]
+def add_kernel(where_ref, a, b, out, token):
+    out[...] = a[...] + b[...]
+    token[...] = jnp.zeros_like(token)
+
+
+def halves_kernel(me, place, where_ref, a, b, keep, away, token, total):
+    total[...] = a[...] + b[...]
+    rows = keep.shape[0]
+    row = rows * place(where_ref[me])
+    keep[...] = total[pl.ds(pl.multiple_of(row, rows), rows), :]
+    away[...] = total[pl.ds(pl.multiple_of(rows - row, rows), rows), :]
     token[...] = jnp.zeros_like(token)
 
 
 def last_kernel(where_ref, *refs):
     out = refs[-1]
     col = 0
-    for n in range(3):
-        a, b, c, d = refs[4 * n : 4 * (n + 1)]
+    for a, b in zip(refs[0:6:2], refs[1:6:2]):
         width = a.shape[1]
-        out[:, col : col + width] = a[...] + (b[...] + c[...]) + d[...]
+        out[:, col : col + width] = a[...] + b[...]
         col += width
 
 
@@ -544,52 +551,71 @@
     theirs = send(away, "c", 1).reshape(4, 4, 4, 16, TOK)
     keep = keep.reshape(4, 4, 4, 16, TOK)
 
-    terms = products(where, keep, theirs, own, other)
     forward = lambda c: 1 - 2 * c
     back = lambda c: 2 * c - 1
-    ahead = {axis: send(terms[axis][0], axis, forward) for axis in KINDS}
-    behind = {axis: send(terms[axis][1], axis, back) for axis in KINDS}
-    near = {
-        axis: (send(terms[axis][2], axis, forward), send(terms[axis][3], axis, back))
-        for axis in KINDS
-    }
-    order = ("x", "y", "z")
-    token = ()
-    low, high = {}, {}
-    for axis in order:
-        term, *token = relay(terms[axis][4], ahead[axis], token)
+    terms, ahead, behind, low, high = {}, {}, {}, {}, {}
+
+    def start(axis, after):
+        *t, token = products(axis, where, keep, theirs, own, other, after)
+        terms[axis] = t
+        ahead[axis] = send(t[0], axis, forward)
+        behind[axis] = send(t[1], axis, back)
+        return [token]
+
+    def relay_low(axis, after):
+        term, *token = relay(terms[axis][2], ahead[axis], 0, after)
         low[axis] = send(term, axis, forward)
-    for axis in order:
-        term, *token = relay(terms[axis][5], behind[axis], token)
+        return token
+
+    def relay_high(axis, after):
+        term, *token = relay(terms[axis][3], behind[axis], 1, after)
         high[axis] = send(term, axis, back)
-    held, rounds = {}, {}
-    for axis in KINDS:
-        held[axis] = terms[axis][6], near[axis][1], low[axis], near[axis][0], high[axis]
+        return token
+
+    token = start("y", ())
+    token = start("z", token)
+    token = start("x", token)
+    token = relay_low("y", token)
+    token = relay_low("z", token)
+    token = relay_high("y", token)
+    token = relay_high("z", token)
+    token = relay_low("x", token)
+    token = relay_high("x", token)
+
     following = {"x": ("y", "z"), "y": ("z", "x"), "z": ("x", "y")}
     tail = [(8, DK)]
-
-    def second(axis, after):
+    order = ("y", "x", "z")
+    parts, came, rounds = {}, {}, {}
+    for axis in order:
         a2 = following[axis][0]
         width = COLS * len(KINDS[axis])
         kernel = functools.partial(second_kernel, axis, AXES.index(a2))
         outs = [(64, width)] * 4 + tail
-        *pieces, t = small_call(kernel, where, held[axis], outs, [(256, width)], after, "second")
-        return around(pieces, a2), [t]
-
-    def third(axis, arrived, after):
-        a3 = following[axis][1]
-        width = COLS * len(KINDS[axis])
-        kernel = functools.partial(third_kernel, AXES.index(a3))
-        outs = [(16, width)] * 4 + tail
-        *pieces, t = small_call(kernel, where, arrived, outs, [(64, width)], after, "third")
-        return around(pieces, a3), [t]
-
-    rounds["x"], _ = second("x", ())
-    rounds["x"], _ = third("x", rounds["x"], ())
-    rounds["y"], token = second("y", ())
-    rounds["z"], token = second("z", token)
-    rounds["y"], token = third("y", rounds["y"], token)
-    rounds["z"], token = third("z", rounds["z"], token)
+        ins = [terms[axis][4], low[axis], high[axis]]
+        *parts[axis], t = small_call(kernel, where, ins, outs, [(256, width)], token, "second")
+        came[axis] = send(parts[axis][0], a2, forward)
+        token = [t]
+    for step in (1, 2):
+        for axis in order:
+            part = parts[axis][step]
+            ins = [part, came[axis]]
+            part, t = small_call(add_kernel, where, ins, [part.shape] + tail, (), token, "add")
+            came[axis] = send(part, following[axis][0], forward)
+            token = [t]
+    for axis in order:
+        rounds[axis] = parts[axis][3], came[axis]
+    upper, odd = (lambda p: lax.div(p, 2)), (lambda p: lax.rem(p, 2))
+    for rows, distance, place_of in ((32, 2, upper), (16, 1, odd)):
+        for axis in order:
+            a3 = following[axis][1]
+            width = COLS * len(KINDS[axis])
+            kernel = functools.partial(halves_kernel, AXES.index(a3), place_of)
+            outs = [(rows, width)] * 2 + tail
+            keep, away, t = small_call(
+                kernel, where, rounds[axis], outs, [(2 * rows, width)], token, "halves"
+            )
+            rounds[axis] = keep, swap(away, a3, distance)
+            token = [t]
     (mine,) = small_call(
         last_kernel, where, [r for axis in KINDS for r in rounds[axis]], [(16, D)], name="last"
     )

time: 235 us -> 216 us (0.919)
  starting transfers between devices: 79.7 us -> 48.8 us
  waiting for transfers between devices: 69 us -> 92.7 us
  Pallas kernels: 72.3 us -> 65.8 us
  local copies, waits for them, and re-layouts: 12.1 us -> 7.58 us
    ppermute x52 -> x37, starting transfers between devices: 79.7 us -> 41.8 us  [send(): return lax.ppermute(array, AXES, shift_pairs(axis, by))]
    ppermute x52 -> x37, waiting for transfers between devices: 69 us -> 84 us  [send(): return lax.ppermute(array, AXES, shift_pairs(axis, by))]
    ppermute x0 -> x6, waiting for transfers between devices: none -> 8.64 us  [swap(): return lax.ppermute(array, AXES, pairs)]
    ppermute x0 -> x6, starting transfers between devices: none -> 6.96 us  [swap(): return lax.ppermute(array, AXES, pairs)]
    pallas_call x1, Pallas kernels: 13.5 us -> 8.19 us  [local_state(): pl.pallas_call(state_kernel, grid_spec=pltpu.PrefetchScalarGridSpec(num_s...]
    unnamed x32 -> x16, local copies, waits for them, and re-layouts: 12.1 us -> 7.58 us
    pallas_call x10 -> x19, Pallas kernels: 8.77 us -> 13 us  [small_call(): pl.pallas_call(body, in_specs=[pl.BlockSpec(memory_space=pltpu.SMEM)] + w...]
    pallas_call x7 -> x9, Pallas kernels: 19.6 us -> 16 us  [the longest x3 14.3 us: products(): pl.pallas_call(functools.partial(product_kernel, axis), grid_spec=pltpu.P...]
  transfers between devices with their start and end apart: 52 -> 43, of which waited for: 27 -> 23; matrix products, arithmetic and copies ran while one was open for 0% -> 0% of each run, Pallas kernels for 16% -> 23%
where the time goes in v1:
time: 216 us
  waiting for transfers between devices  92.7 us (43%)
  Pallas kernels  65.8 us (30%)
  starting transfers between devices  48.8 us (23%)
  local copies, waits for them, and re-layouts  7.58 us (4%)
    ppermute x37, waiting for transfers between devices, send(): return lax.ppermute(array, AXES, shift_pairs(axis, by))  84 us
    ppermute x37, starting transfers between devices, send(): return lax.ppermute(array, AXES, shift_pairs(axis, by))  41.8 us
    pallas_call x4, Pallas kernels, local_core(): pl.pallas_call(core_kernel, grid=(steps,), in_specs=[spec] * 4 + [pl.Bloc...  18.5 us
    pallas_call x3, Pallas kernels, products(): pl.pallas_call(functools.partial(product_kernel, axis), grid_spec=pltpu.P...  14.3 us
    pallas_call x19, Pallas kernels, small_call(): pl.pallas_call(body, in_specs=[pl.BlockSpec(memory_space=pltpu.SMEM)] + w...  13 us
    ppermute x6, waiting for transfers between devices, swap(): return lax.ppermute(array, AXES, pairs)  8.64 us
    pallas_call x1, Pallas kernels, local_state(): pl.pallas_call(state_kernel, grid_spec=pltpu.PrefetchScalarGridSpec(num_s...  8.19 us
    pallas_call x1, Pallas kernels, gated(): pl.pallas_call(hidden_kernel, grid_spec=pltpu.PrefetchScalarGridSpec(num_...  7.98 us
  transfers between devices with their start and end apart: 43, of which 23 were waited for; matrix products, arithmetic and copies ran while one was open for 0% of the time, Pallas kernels for 23%

profile of v1, /device:TPU:0, one launch (start us, length us, event | category | flops | bytes accessed | tf_op | source)
XLA Modules:
  0.0 215.9 jit_solution(6840443921468890251)
XLA Ops:
  0.7 2.2 %copy-done = bf16[1,512,4096]{2,1,0:T(8,128)(2,1)S(1)} copy-done((bf16[1,512,4096]{2,1,0:T(8,128)(2,1)S(1)}, bf16[1,512,4096]{2,1,0:T(8,128)(2,1)}, u32[]{:S(2)}) %copy-start) | copy-done | bytes 4194328
  2.9 1.6 copy-done.2
  4.5 1.6 copy-done.4
  6.1 2.2 %copy-done.6 = f32[1,512,2048]{2,1,0:T(8,128)S(1)} copy-done((f32[1,512,2048]{2,1,0:T(8,128)S(1)}, f32[1,512,2048]{2,1,0:T(8,128)}, u32[]{:S(2)}) %copy-start.6) | copy-done | bytes 4194328
  8.3 8.2 %local_state.1 = (f32[16,72,128]{2,1,0:T(8,128)S(1)}, f32[16,72,128]{2,1,0:T(8,128)S(1)}, f32[512,2048]{1,0:T(8,128)S(1)}, f32[512,4096]{1,0:T(8,128)}) custom-call(s32[4]{0:T(128)S(1)} %pad_add_fusion.where_ref.refs_0_, bf16[512,2048]{1,0:T(8,128)(2,1)S(1)} %bitcast.17, bf16[512,2048]{1,0:T(8,128)(2,1)S(1)} %bitcast.22, f32[512,2048]{1,0:T(8,128)S(1)} %bitcast.37, ...), custom_call_target="tpu_custom_call" | custom-call | flops 268435456 | bytes 26000000 | tf_op jit(solution)/shard_map/local_state/pallas_call | solution.py:148
  16.5 2.0 collective-permute-done.got_ref.refs_2_
  19.3 4.1 %collective-permute-start.2 = (f32[4,72,128]{2,1,0:T(8,128)S(1)}, f32[4,72,128]{2,1,0:T(8,128)S(1)}, u32[]{:S(2)}, u32[]{:S(2)}) collective-permute-start(f32[4,72,128]{2,1,0:T(8,128)S(1)} %get-tuple-element.120), channel_id=1, source_target_pairs={{0,6},{1,7},{2,0},{3,1},{4,2},{5,3},{6,4},{7,5},{8,14},{9,15},{10,... | collective-permute-start | bytes 442376 | tf_op jit(solution)/shard_map/ppermute | solution.py:63
  23.5 1.3 collective-permute-start.1
  24.7 4.5 %local_core.4 = (f32[512,2048]{1,0:T(8,128)S(1)}, bf16[512,2048]{1,0:T(8,128)(2,1)S(1)}, bf16[512,2048]{1,0:T(8,128)(2,1)S(1)}, f32[8,128]{1,0:T(8,128)S(1)}) custom-call(bf16[512,2048]{1,0:T(8,128)(2,1)S(1)} %bitcast.27, bf16[512,2048]{1,0:T(8,128)(2,1)S(1)} %bitcast.18, bf16[512,2048]{1,0:T(8,128)(2,1)S(1)} %bitcast.23, ...), custom_call_target="tpu_custom_call" | custom-call | flops 536870912 | bytes 20000000 | tf_op jit(solution)/shard_map/local_core/pallas_call | solution.py:216
  30.3 1.5 collective-permute-done.3.refs_4_
  31.7 2.0 collective-permute-done.1.refs_2_
  34.3 3.3 %collective-permute-start.6 = (f32[4,72,128]{2,1,0:T(8,128)S(1)}, f32[4,72,128]{2,1,0:T(8,128)S(1)}, u32[]{:S(2)}, u32[]{:S(2)}) collective-permute-start(f32[4,72,128]{2,1,0:T(8,128)S(1)} %get-tuple-element.123.rest_3_.refs_2_), channel_id=1, source_target_pairs={{0,16},{1,17},{2,18},{3,19},{4,20},{5,21},{6,22},{7,23},{8,24},{9,... | collective-permute-start | bytes 442376 | tf_op jit(solution)/shard_map/ppermute | solution.py:63
  39.6 4.5 %local_core.5 = (f32[512,2048]{1,0:T(8,128)S(1)}, bf16[512,2048]{1,0:T(8,128)(2,1)S(1)}, bf16[512,2048]{1,0:T(8,128)(2,1)S(1)}, f32[8,128]{1,0:T(8,128)S(1)}) custom-call(bf16[512,2048]{1,0:T(8,128)(2,1)S(1)} %bitcast.28, bf16[512,2048]{1,0:T(8,128)(2,1)S(1)} %bitcast.19, ...), custom_call_target="tpu_custom_call", output_to_operand_aliasing={{0}: (4, {}), {1}: (5, {}), {2}: (6, {})} | custom-call | flops 536870912 | bytes 20000000 | tf_op jit(solution)/shard_map/local_core/pallas_call | solution.py:216
  46.9 1.3 collective-permute-start.7
  48.2 4.5 %local_core.6 = (f32[512,2048]{1,0:T(8,128)S(1)}, bf16[512,2048]{1,0:T(8,128)(2,1)S(1)}, bf16[512,2048]{1,0:T(8,128)(2,1)S(1)}, f32[8,128]{1,0:T(8,128)S(1)}) custom-call(bf16[512,2048]{1,0:T(8,128)(2,1)S(1)} %bitcast.29, bf16[512,2048]{1,0:T(8,128)(2,1)S(1)} %bitcast.20, ...), custom_call_target="tpu_custom_call", output_to_operand_aliasing={{0}: (4, {}), {1}: (5, {}), {2}: (6, {})} | custom-call | flops 536870912 | bytes 20000000 | tf_op jit(solution)/shard_map/local_core/pallas_call | solution.py:216
  55.7 5.1 %local_core.7 = (f32[512,2048]{1,0:T(8,128)S(1)}, bf16[512,2048]{1,0:T(8,128)(2,1)S(1)}, bf16[512,2048]{1,0:T(8,128)(2,1)S(1)}, f32[8,128]{1,0:T(8,128)}) custom-call(bf16[512,2048]{1,0:T(8,128)(2,1)S(1)} %bitcast.30, bf16[512,2048]{1,0:T(8,128)(2,1)S(1)} %bitcast.21, ...), custom_call_target="tpu_custom_call", output_to_operand_aliasing={{0}: (4, {}), {1}: (5, {}), {2}: (6, {})} | custom-call | flops 536870912 | bytes 20000000 | tf_op jit(solution)/shard_map/local_core/pallas_call | solution.py:216
  60.8 8.0 %gated_hidden.1 = (bf16[512,2048]{1,0:T(8,128)(2,1)}, bf16[1024,512]{1,0:T(8,128)(2,1)S(1)}, f32[1024,512]{1,0:T(8,128)S(1)}) custom-call(s32[4]{0:T(128)S(1)} %pad_add_fusion.where_ref.refs_0_, f32[512,2048]{1,0:T(8,128)S(1)} %get-tuple-element.138.out_ref, bf16[512,2048]{1,0:T(8,128)(2,1)S(1)} %get-tuple-element.139.high_ref, ...), custom_call_target="tpu_custom_call" | custom-call | flops 805306368 | bytes 17000000 | tf_op jit(solution)/shard_map/gated_hidden/pallas_call | solution.py:382
  69.3 3.8 %collective-permute-done.11 = f32[1024,512]{1,0:T(8,128)S(1)} collective-permute-done((f32[1024,512]{1,0:T(8,128)S(1)}, f32[1024,512]{1,0:T(8,128)S(1)}, u32[]{:S(2)}, u32[]{:S(2)}) %collective-permute-start.11) | collective-permute-done | bytes 2097184 | tf_op jit(solution)/shard_map/ppermute | solution.py:63
  73.1 5.3 %products_y.1 = (f32[128,1536]{1,0:T(8,128)S(1)}, f32[128,1536]{1,0:T(8,128)S(1)}, f32[256,1536]{1,0:T(8,128)S(1)}, f32[256,1536]{1,0:T(8,128)S(1)}, f32[256,1536]{1,0:T(8,128)S(1)}, /*index=5*/f32[8,128]{1,0:T(8,128)S(1)}) custom-call(s32[4]{0:T(128)S(1)} %pad_add_fusion.where_ref.refs_0_, bf16[4,4,4,16,512]{4,3,2,1,0:T(8,128)(2,1)S(1)} %bitcast.34, ...), custom_call_target="tpu_custom_call" | custom-call | flops 3221225472 | bytes 12288000 | tf_op jit(solution)/shard_map/products_y/pallas_call | solution.py:445
  78.3 2.0 collective-permute-start.13
  80.3 5.3 %products_z.1 = (f32[128,1536]{1,0:T(8,128)S(1)}, f32[128,1536]{1,0:T(8,128)S(1)}, f32[256,1536]{1,0:T(8,128)S(1)}, f32[256,1536]{1,0:T(8,128)S(1)}, f32[256,1536]{1,0:T(8,128)S(1)}, /*index=5*/f32[8,128]{1,0:T(8,128)S(1)}) custom-call(s32[4]{0:T(128)S(1)} %pad_add_fusion.where_ref.refs_0_, bf16[4,4,4,16,512]{4,3,2,1,0:T(8,128)(2,1)S(1)} %bitcast.35, ...), custom_call_target="tpu_custom_call" | custom-call | flops 3221225472 | bytes 12288000 | tf_op jit(solution)/shard_map/products_z/pallas_call | solution.py:445
  85.7 1.5 collective-permute-start.15
  87.2 3.8 %products_x.1 = (f32[128,1024]{1,0:T(8,128)S(1)}, f32[128,1024]{1,0:T(8,128)S(1)}, f32[256,1024]{1,0:T(8,128)S(1)}, f32[256,1024]{1,0:T(8,128)S(1)}, f32[256,1024]{1,0:T(8,128)S(1)}, /*index=5*/f32[8,128]{1,0:T(8,128)S(1)}) custom-call(s32[4]{0:T(128)S(1)} %pad_add_fusion.where_ref.refs_0_, bf16[4,4,4,16,512]{4,3,2,1,0:T(8,128)(2,1)S(1)} %bitcast.36, ...), custom_call_target="tpu_custom_call" | custom-call | flops 2147483648 | bytes 8192000 | tf_op jit(solution)/shard_map/products_x/pallas_call | solution.py:445
  92.1 6.8 %collective-permute-done.16.b = f32[128,1536]{1,0:T(8,128)S(1)} collective-permute-done((f32[128,1536]{1,0:T(8,128)S(1)}, f32[128,1536]{1,0:T(8,128)S(1)}, u32[]{:S(2)}, u32[]{:S(2)}) %collective-permute-start.16) | collective-permute-done | bytes 786464 | tf_op jit(solution)/shard_map/ppermute | solution.py:63
  99.6 3.6 %collective-permute-start.17 = (f32[256,1536]{1,0:T(8,128)S(1)}, f32[256,1536]{1,0:T(8,128)S(1)}, u32[]{:S(2)}, u32[]{:S(2)}) collective-permute-start(f32[256,1536]{1,0:T(8,128)S(1)} %get-tuple-element.159), channel_id=1, source_target_pairs={{0,24},{1,9},{2,26},{3,11},{4,28},{5,13},{6,30},{7,15},{8,0},{9,17... | collective-permute-start | bytes 4718600 | tf_op jit(solution)/shard_map/ppermute | solution.py:63
  104.3 1.5 collective-permute-start.19
  105.7 1.7 collective-permute-start.18
  107.5 7.7 %collective-permute-done.20.b = f32[128,1536]{1,0:T(8,128)S(1)} collective-permute-done((f32[128,1536]{1,0:T(8,128)S(1)}, f32[128,1536]{1,0:T(8,128)S(1)}, u32[]{:S(2)}, u32[]{:S(2)}) %collective-permute-start.20) | collective-permute-done | bytes 786464 | tf_op jit(solution)/shard_map/ppermute | solution.py:63
  115.5 2.3 %collective-permute-start.23 = (f32[256,1536]{1,0:T(8,128)S(1)}, f32[256,1536]{1,0:T(8,128)S(1)}, u32[]{:S(2)}, u32[]{:S(2)}) collective-permute-start(f32[256,1536]{1,0:T(8,128)S(1)} %get-tuple-element.176), channel_id=1, source_target_pairs={{0,6},{1,3},{2,0},{3,5},{4,2},{5,7},{6,4},{7,1},{8,14},{9,11},{10,... | collective-permute-start | bytes 4718600 | tf_op jit(solution)/shard_map/ppermute | solution.py:63
  117.8 1.4 collective-permute-done.19.b
  119.2 1.3 collective-permute-start.22
  122.1 13.4 %collective-permute-done.17.refs_3_ = f32[256,1536]{1,0:T(8,128)S(1)} collective-permute-done((f32[256,1536]{1,0:T(8,128)S(1)}, f32[256,1536]{1,0:T(8,128)S(1)}, u32[]{:S(2)}, u32[]{:S(2)}) %collective-permute-start.17) | collective-permute-done | bytes 1572896 | tf_op jit(solution)/shard_map/ppermute | solution.py:63
  135.5 3.7 %collective-permute-start.24 = (f32[256,1024]{1,0:T(8,128)S(1)}, f32[256,1024]{1,0:T(8,128)S(1)}, u32[]{:S(2)}, u32[]{:S(2)}) collective-permute-start(f32[256,1024]{1,0:T(8,128)S(1)} %get-tuple-element.178), channel_id=1, source_target_pairs={{0,32},{1,97},{2,34},{3,99},{4,36},{5,101},{6,38},{7,103},{8,40},{... | collective-permute-start | bytes 3145736 | tf_op jit(solution)/shard_map/ppermute | solution.py:63
  140.6 12.5 %collective-permute-done.24.refs_2_ = f32[256,1024]{1,0:T(8,128)S(1)} collective-permute-done((f32[256,1024]{1,0:T(8,128)S(1)}, f32[256,1024]{1,0:T(8,128)S(1)}, u32[]{:S(2)}, u32[]{:S(2)}) %collective-permute-start.24) | collective-permute-done | bytes 1048608 | tf_op jit(solution)/shard_map/ppermute | solution.py:63
  156.9 7.1 %collective-permute-done.28.refs_2_ = f32[64,1024]{1,0:T(8,128)S(1)} collective-permute-done((f32[64,1024]{1,0:T(8,128)S(1)}, f32[64,1024]{1,0:T(8,128)S(1)}, u32[]{:S(2)}, u32[]{:S(2)}) %collective-permute-start.28) | collective-permute-done | bytes 262176 | tf_op jit(solution)/shard_map/ppermute | solution.py:63
  165.1 1.6 collective-permute-start.30
  167.4 6.9 %collective-permute-done.31.refs_2_ = f32[64,1024]{1,0:T(8,128)S(1)} collective-permute-done((f32[64,1024]{1,0:T(8,128)S(1)}, f32[64,1024]{1,0:T(8,128)S(1)}, u32[]{:S(2)}, u32[]{:S(2)}) %collective-permute-start.31) | collective-permute-done | bytes 262176 | tf_op jit(solution)/shard_map/ppermute | solution.py:63
  177.1 2.3 %collective-permute-start.32 = (f32[32,1536]{1,0:T(8,128)S(1)}, f32[32,1536]{1,0:T(8,128)S(1)}, u32[]{:S(2)}, u32[]{:S(2)}) collective-permute-start(f32[32,1536]{1,0:T(8,128)S(1)} %get-tuple-element.200), channel_id=1, source_target_pairs={{0,64},{1,65},{2,66},{3,67},{4,68},{5,69},{6,70},{7,71},{8,72},{9,... | collective-permute-start | bytes 589832 | tf_op jit(solution)/shard_map/ppermute | solution.py:59
  179.4 6.8 %collective-permute-done.34.refs_2_ = f32[64,1024]{1,0:T(8,128)S(1)} collective-permute-done((f32[64,1024]{1,0:T(8,128)S(1)}, f32[64,1024]{1,0:T(8,128)S(1)}, u32[]{:S(2)}, u32[]{:S(2)}) %collective-permute-start.34) | collective-permute-done | bytes 262176 | tf_op jit(solution)/shard_map/ppermute | solution.py:63
  189.7 4.3 %collective-permute-done.37.refs_2_ = f32[32,1024]{1,0:T(8,128)S(1)} collective-permute-done((f32[32,1024]{1,0:T(8,128)S(1)}, f32[32,1024]{1,0:T(8,128)S(1)}, u32[]{:S(2)}, u32[]{:S(2)}) %collective-permute-start.37) | collective-permute-done | bytes 131104 | tf_op jit(solution)/shard_map/ppermute | solution.py:59
  194.7 1.1 halves.11
  195.8 2.9 %collective-permute-start.38 = (f32[16,1536]{1,0:T(8,128)S(1)}, f32[16,1536]{1,0:T(8,128)S(1)}, u32[]{:S(2)}, u32[]{:S(2)}) collective-permute-start(f32[16,1536]{1,0:T(8,128)S(1)} %get-tuple-element.217), channel_id=1, source_target_pairs={{0,8},{1,9},{2,10},{3,11},{4,12},{5,13},{6,14},{7,15},{8,0},{9,1},... | collective-permute-start | bytes 294920 | tf_op jit(solution)/shard_map/ppermute | solution.py:59
  198.7 4.3 %collective-permute-done.39.refs_6_ = f32[16,1024]{1,0:T(8,128)S(1)} collective-permute-done((f32[16,1024]{1,0:T(8,128)S(1)}, f32[16,1024]{1,0:T(8,128)S(1)}, u32[]{:S(2)}, u32[]{:S(2)}) %collective-permute-start.39) | collective-permute-done | bytes 65568 | tf_op jit(solution)/shard_map/ppermute | solution.py:59
  203.6 1.5 collective-permute-start.42
  205.3 1.8 collective-permute-start.40
  207.1 4.6 %collective-permute-done.42.refs_3_ = f32[16,4096]{1,0:T(8,128)S(1)} collective-permute-done((f32[16,4096]{1,0:T(8,128)S(1)}, f32[16,4096]{1,0:T(8,128)S(1)}, u32[]{:S(2)}, u32[]{:S(2)}) %collective-permute-start.42) | collective-permute-done | bytes 262176 | tf_op jit(solution)/shard_map/ppermute | solution.py:63
  211.7 1.6 collective-permute-done.41.refs_2_
  214.4 1.6 assemble.1
  (91 shorter events, 31.4 us)
Async XLA Ops:
  0.7 2.2 %copy-start = (bf16[1,512,4096]{2,1,0:T(8,128)(2,1)S(1)}, bf16[1,512,4096]{2,1,0:T(8,128)(2,1)}, u32[]{:S(2)}) copy-start(bf16[1,512,4096]{2,1,0:T(8,128)(2,1)} %param.11) | copy-start | bytes 12582916
  16.5 2.0 collective-permute-start
  18.5 6.3 %copy-start.3 = (bf16[1,512,2048]{2,1,0:T(8,128)(2,1)S(1)}, bf16[1,512,2048]{2,1,0:T(8,128)(2,1)}, u32[]{:S(2)}) copy-start(bf16[1,512,2048]{2,1,0:T(8,128)(2,1)} %param.7) | copy-start | bytes 6291460
  18.5 6.3 %copy-start.5 = (bf16[1,512,2048]{2,1,0:T(8,128)(2,1)S(1)}, bf16[1,512,2048]{2,1,0:T(8,128)(2,1)}, u32[]{:S(2)}) copy-start(bf16[1,512,2048]{2,1,0:T(8,128)(2,1)} %param.6) | copy-start | bytes 6291460
  19.1 53.9 %collective-permute-start.12 = (f32[512,4096]{1,0:T(8,128)}, f32[512,4096]{1,0:T(8,128)S(1)}, u32[]{:S(2)}, u32[]{:S(2)}) collective-permute-start(f32[512,4096]{1,0:T(8,128)} %get-tuple-element.145), channel_id=1, source_target_pairs={{0,1},{1,0},{2,3},{3,2},{4,5},{5,4},{6,7},{7,6},{8,9},{9,8},{10,11... | collective-permute-start | bytes 25165832 | tf_op jit(solution)/shard_map/ppermute | solution.py:63
  19.3 10.9 %collective-permute-start.2 = (f32[4,72,128]{2,1,0:T(8,128)S(1)}, f32[4,72,128]{2,1,0:T(8,128)S(1)}, u32[]{:S(2)}, u32[]{:S(2)}) collective-permute-start(f32[4,72,128]{2,1,0:T(8,128)S(1)} %get-tuple-element.120), channel_id=1, source_target_pairs={{0,6},{1,7},{2,0},{3,1},{4,2},{5,3},{6,4},{7,5},{8,14},{9,15},{10,... | collective-permute-start | bytes 442376 | tf_op jit(solution)/shard_map/ppermute | solution.py:63
  23.5 8.3 %collective-permute-start.3 = (f32[4,72,128]{2,1,0:T(8,128)S(1)}, f32[4,72,128]{2,1,0:T(8,128)S(1)}, u32[]{:S(2)}, u32[]{:S(2)}) collective-permute-start(f32[4,72,128]{2,1,0:T(8,128)S(1)} %get-tuple-element.121), channel_id=1, source_target_pairs={{0,4},{1,5},{2,6},{3,7},{4,0},{5,1},{6,2},{7,3},{8,12},{9,13},{10,... | collective-permute-start | bytes 442376 | tf_op jit(solution)/shard_map/ppermute | solution.py:63
  23.5 10.2 %collective-permute-start.1 = (f32[4,72,128]{2,1,0:T(8,128)S(1)}, f32[4,72,128]{2,1,0:T(8,128)S(1)}, u32[]{:S(2)}, u32[]{:S(2)}) collective-permute-start(f32[4,72,128]{2,1,0:T(8,128)S(1)} %get-tuple-element.115.rest_0_), channel_id=1, source_target_pairs={{0,2},{1,3},{2,4},{3,5},{4,6},{5,7},{6,0},{7,1},{8,10},{9,11},{10,... | collective-permute-start | bytes 442376 | tf_op jit(solution)/shard_map/ppermute | solution.py:63
  34.3 9.8 %collective-permute-start.6 = (f32[4,72,128]{2,1,0:T(8,128)S(1)}, f32[4,72,128]{2,1,0:T(8,128)S(1)}, u32[]{:S(2)}, u32[]{:S(2)}) collective-permute-start(f32[4,72,128]{2,1,0:T(8,128)S(1)} %get-tuple-element.123.rest_3_.refs_2_), channel_id=1, source_target_pairs={{0,16},{1,17},{2,18},{3,19},{4,20},{5,21},{6,22},{7,23},{8,24},{9,... | collective-permute-start | bytes 442376 | tf_op jit(solution)/shard_map/ppermute | solution.py:63
  37.6 7.3 %collective-permute-start.5 = (f32[4,72,128]{2,1,0:T(8,128)S(1)}, f32[4,72,128]{2,1,0:T(8,128)S(1)}, u32[]{:S(2)}, u32[]{:S(2)}) collective-permute-start(f32[4,72,128]{2,1,0:T(8,128)S(1)} %get-tuple-element.123.rest_3_.refs_2_), channel_id=1, source_target_pairs={{0,24},{1,25},{2,26},{3,27},{4,28},{5,29},{6,30},{7,31},{8,0},{9,1... | collective-permute-start | bytes 442376 | tf_op jit(solution)/shard_map/ppermute | solution.py:63
  38.6 6.6 %collective-permute-start.4 = (f32[4,72,128]{2,1,0:T(8,128)S(1)}, f32[4,72,128]{2,1,0:T(8,128)S(1)}, u32[]{:S(2)}, u32[]{:S(2)}) collective-permute-start(f32[4,72,128]{2,1,0:T(8,128)S(1)} %get-tuple-element.123.rest_3_.refs_2_), channel_id=1, source_target_pairs={{0,8},{1,9},{2,10},{3,11},{4,12},{5,13},{6,14},{7,15},{8,16},{9,17... | collective-permute-start | bytes 442376 | tf_op jit(solution)/shard_map/ppermute | solution.py:63
  45.9 6.8 %collective-permute-start.8 = (f32[4,64,128]{2,1,0:T(8,128)S(1)}, f32[4,64,128]{2,1,0:T(8,128)S(1)}, u32[]{:S(2)}, u32[]{:S(2)}) collective-permute-start(f32[4,64,128]{2,1,0:T(8,128)S(1)} %get-tuple-element.134), channel_id=1, source_target_pairs={{0,6},{1,7},{2,0},{3,1},{4,2},{5,3},{6,4},{7,5},{8,14},{9,15},{10,... | collective-permute-start | bytes 393224 | tf_op jit(solution)/shard_map/ppermute | solution.py:63
  46.7 7.1 %collective-permute-start.9 = (f32[4,64,128]{2,1,0:T(8,128)S(1)}, f32[4,64,128]{2,1,0:T(8,128)S(1)}, u32[]{:S(2)}, u32[]{:S(2)}) collective-permute-start(f32[4,64,128]{2,1,0:T(8,128)S(1)} %get-tuple-element.135), channel_id=1, source_target_pairs={{0,4},{1,5},{2,6},{3,7},{4,0},{5,1},{6,2},{7,3},{8,12},{9,13},{10,... | collective-permute-start | bytes 393224 | tf_op jit(solution)/shard_map/ppermute | solution.py:63
  46.9 7.8 %collective-permute-start.7 = (f32[4,64,128]{2,1,0:T(8,128)S(1)}, f32[4,64,128]{2,1,0:T(8,128)S(1)}, u32[]{:S(2)}, u32[]{:S(2)}) collective-permute-start(f32[4,64,128]{2,1,0:T(8,128)S(1)} %get-tuple-element.129.rest_3_), channel_id=1, source_target_pairs={{0,2},{1,3},{2,4},{3,5},{4,6},{5,7},{6,0},{7,1},{8,10},{9,11},{10,... | collective-permute-start | bytes 393224 | tf_op jit(solution)/shard_map/ppermute | solution.py:63
  55.5 5.4 %collective-permute-start.10 = (f32[16,64,128]{2,1,0:T(8,128)S(1)}, f32[16,64,128]{2,1,0:T(8,128)S(1)}, u32[]{:S(2)}, u32[]{:S(2)}) collective-permute-start(f32[16,64,128]{2,1,0:T(8,128)S(1)} %get-tuple-element.137.rest_3_), channel_id=1, source_target_pairs={{0,1},{1,0},{2,3},{3,2},{4,5},{5,4},{6,7},{7,6},{8,9},{9,8},{10,11... | collective-permute-start | bytes 1572872 | tf_op jit(solution)/shard_map/ppermute | solution.py:63
  55.7 5.1 %copy-start.7 = (bf16[1,512,2048]{2,1,0:T(8,128)(2,1)S(1)}, bf16[1,512,2048]{2,1,0:T(8,128)(2,1)}, u32[]{:S(2)}) copy-start(bf16[1,512,2048]{2,1,0:T(8,128)(2,1)} %param.10) | copy-start | bytes 6291460
  60.8 12.2 %copy-start.1 = (bf16[1,512,4096]{2,1,0:T(8,128)(2,1)S(1)}, bf16[1,512,4096]{2,1,0:T(8,128)(2,1)}, u32[]{:S(2)}) copy-start(bf16[1,512,4096]{2,1,0:T(8,128)(2,1)} %param.11) | copy-start | bytes 12582916
  68.8 4.2 %collective-permute-start.11 = (f32[1024,512]{1,0:T(8,128)S(1)}, f32[1024,512]{1,0:T(8,128)S(1)}, u32[]{:S(2)}, u32[]{:S(2)}) collective-permute-start(f32[1024,512]{1,0:T(8,128)S(1)} %get-tuple-element.144), channel_id=1, source_target_pairs={{0,1},{1,0},{2,3},{3,2},{4,5},{5,4},{6,7},{7,6},{8,9},{9,8},{10,11... | collective-permute-start | bytes 6291464 | tf_op jit(solution)/shard_map/ppermute | solution.py:63
  78.3 13.4 %collective-permute-start.13 = (f32[128,1536]{1,0:T(8,128)S(1)}, f32[128,1536]{1,0:T(8,128)S(1)}, u32[]{:S(2)}, u32[]{:S(2)}) collective-permute-start(f32[128,1536]{1,0:T(8,128)S(1)} %get-tuple-element.148), channel_id=1, source_target_pairs={{0,8},{1,25},{2,10},{3,27},{4,12},{5,29},{6,14},{7,31},{8,16},{9,1... | collective-permute-start | bytes 2359304 | tf_op jit(solution)/shard_map/ppermute | solution.py:63
  85.6 13.3 %collective-permute-start.16 = (f32[128,1536]{1,0:T(8,128)S(1)}, f32[128,1536]{1,0:T(8,128)S(1)}, u32[]{:S(2)}, u32[]{:S(2)}) collective-permute-start(f32[128,1536]{1,0:T(8,128)S(1)} %get-tuple-element.156), channel_id=1, source_target_pairs={{0,2},{1,7},{2,4},{3,1},{4,6},{5,3},{6,0},{7,5},{8,10},{9,15},{10,... | collective-permute-start | bytes 2359304 | tf_op jit(solution)/shard_map/ppermute | solution.py:63
  85.7 13.5 %collective-permute-start.15 = (f32[128,1536]{1,0:T(8,128)S(1)}, f32[128,1536]{1,0:T(8,128)S(1)}, u32[]{:S(2)}, u32[]{:S(2)}) collective-permute-start(f32[128,1536]{1,0:T(8,128)S(1)} %get-tuple-element.154), channel_id=1, source_target_pairs={{0,24},{1,9},{2,26},{3,11},{4,28},{5,13},{6,30},{7,15},{8,0},{9,17... | collective-permute-start | bytes 2359304 | tf_op jit(solution)/shard_map/ppermute | solution.py:63
  99.6 36.0 %collective-permute-start.17 = (f32[256,1536]{1,0:T(8,128)S(1)}, f32[256,1536]{1,0:T(8,128)S(1)}, u32[]{:S(2)}, u32[]{:S(2)}) collective-permute-start(f32[256,1536]{1,0:T(8,128)S(1)} %get-tuple-element.159), channel_id=1, source_target_pairs={{0,24},{1,9},{2,26},{3,11},{4,28},{5,13},{6,30},{7,15},{8,0},{9,17... | collective-permute-start | bytes 4718600 | tf_op jit(solution)/shard_map/ppermute | solution.py:63
  103.2 12.0 %collective-permute-start.20 = (f32[128,1536]{1,0:T(8,128)S(1)}, f32[128,1536]{1,0:T(8,128)S(1)}, u32[]{:S(2)}, u32[]{:S(2)}) collective-permute-start(f32[128,1536]{1,0:T(8,128)S(1)} %get-tuple-element.165), channel_id=1, source_target_pairs={{0,6},{1,3},{2,0},{3,5},{4,2},{5,7},{6,4},{7,1},{8,14},{9,11},{10,... | collective-permute-start | bytes 2359304 | tf_op jit(solution)/shard_map/ppermute | solution.py:63
  104.3 15.0 %collective-permute-start.19 = (f32[128,1024]{1,0:T(8,128)S(1)}, f32[128,1024]{1,0:T(8,128)S(1)}, u32[]{:S(2)}, u32[]{:S(2)}) collective-permute-start(f32[128,1024]{1,0:T(8,128)S(1)} %get-tuple-element.163), channel_id=1, source_target_pairs={{0,32},{1,97},{2,34},{3,99},{4,36},{5,101},{6,38},{7,103},{8,40},{... | collective-permute-start | bytes 1572872 | tf_op jit(solution)/shard_map/ppermute | solution.py:63
  105.7 33.5 %collective-permute-start.14 = (f32[256,1536]{1,0:T(8,128)S(1)}, f32[256,1536]{1,0:T(8,128)S(1)}, u32[]{:S(2)}, u32[]{:S(2)}) collective-permute-start(f32[256,1536]{1,0:T(8,128)S(1)} %get-tuple-element.152), channel_id=1, source_target_pairs={{0,8},{1,25},{2,10},{3,27},{4,12},{5,29},{6,14},{7,31},{8,16},{9,1... | collective-permute-start | bytes 4718600 | tf_op jit(solution)/shard_map/ppermute | solution.py:63
  105.7 15.0 %collective-permute-start.18 = (f32[128,1024]{1,0:T(8,128)S(1)}, f32[128,1024]{1,0:T(8,128)S(1)}, u32[]{:S(2)}, u32[]{:S(2)}) collective-permute-start(f32[128,1024]{1,0:T(8,128)S(1)} %get-tuple-element.161), channel_id=1, source_target_pairs={{0,96},{1,33},{2,98},{3,35},{4,100},{5,37},{6,102},{7,39},{8,104},... | collective-permute-start | bytes 1572872 | tf_op jit(solution)/shard_map/ppermute | solution.py:63
  115.5 38.4 %collective-permute-start.23 = (f32[256,1536]{1,0:T(8,128)S(1)}, f32[256,1536]{1,0:T(8,128)S(1)}, u32[]{:S(2)}, u32[]{:S(2)}) collective-permute-start(f32[256,1536]{1,0:T(8,128)S(1)} %get-tuple-element.176), channel_id=1, source_target_pairs={{0,6},{1,3},{2,0},{3,5},{4,2},{5,7},{6,4},{7,1},{8,14},{9,11},{10,... | collective-permute-start | bytes 4718600 | tf_op jit(solution)/shard_map/ppermute | solution.py:63
  119.2 34.7 %collective-permute-start.22 = (f32[256,1536]{1,0:T(8,128)S(1)}, f32[256,1536]{1,0:T(8,128)S(1)}, u32[]{:S(2)}, u32[]{:S(2)}) collective-permute-start(f32[256,1536]{1,0:T(8,128)S(1)} %get-tuple-element.175), channel_id=1, source_target_pairs={{0,2},{1,7},{2,4},{3,1},{4,6},{5,3},{6,0},{7,5},{8,10},{9,15},{10,... | collective-permute-start | bytes 4718600 | tf_op jit(solution)/shard_map/ppermute | solution.py:63
  121.0 19.6 %collective-permute-start.25 = (f32[256,1024]{1,0:T(8,128)S(1)}, f32[256,1024]{1,0:T(8,128)S(1)}, u32[]{:S(2)}, u32[]{:S(2)}) collective-permute-start(f32[256,1024]{1,0:T(8,128)S(1)} %get-tuple-element.179), channel_id=1, source_target_pairs={{0,96},{1,33},{2,98},{3,35},{4,100},{5,37},{6,102},{7,39},{8,104},... | collective-permute-start | bytes 3145736 | tf_op jit(solution)/shard_map/ppermute | solution.py:63
  135.5 17.5 %collective-permute-start.24 = (f32[256,1024]{1,0:T(8,128)S(1)}, f32[256,1024]{1,0:T(8,128)S(1)}, u32[]{:S(2)}, u32[]{:S(2)}) collective-permute-start(f32[256,1024]{1,0:T(8,128)S(1)} %get-tuple-element.178), channel_id=1, source_target_pairs={{0,32},{1,97},{2,34},{3,99},{4,36},{5,101},{6,38},{7,103},{8,40},{... | collective-permute-start | bytes 3145736 | tf_op jit(solution)/shard_map/ppermute | solution.py:63
  140.3 15.9 %collective-permute-start.21 = (f32[64,1536]{1,0:T(8,128)S(1)}, f32[64,1536]{1,0:T(8,128)S(1)}, u32[]{:S(2)}, u32[]{:S(2)}) collective-permute-start(f32[64,1536]{1,0:T(8,128)S(1)} %get-tuple-element.173), channel_id=1, source_target_pairs={{0,2},{1,7},{2,4},{3,1},{4,6},{5,3},{6,0},{7,5},{8,10},{9,15},{10,... | collective-permute-start | bytes 1179656 | tf_op jit(solution)/shard_map/ppermute | solution.py:63
  154.9 9.7 %collective-permute-start.27 = (f32[64,1536]{1,0:T(8,128)S(1)}, f32[64,1536]{1,0:T(8,128)S(1)}, u32[]{:S(2)}, u32[]{:S(2)}) collective-permute-start(f32[64,1536]{1,0:T(8,128)S(1)} %get-tuple-element.185), channel_id=1, source_target_pairs={{0,32},{1,97},{2,34},{3,99},{4,36},{5,101},{6,38},{7,103},{8,40},{... | collective-permute-start | bytes 1179656 | tf_op jit(solution)/shard_map/ppermute | solution.py:63
  155.9 8.0 %collective-permute-start.28 = (f32[64,1024]{1,0:T(8,128)S(1)}, f32[64,1024]{1,0:T(8,128)S(1)}, u32[]{:S(2)}, u32[]{:S(2)}) collective-permute-start(f32[64,1024]{1,0:T(8,128)S(1)} %get-tuple-element.187), channel_id=1, source_target_pairs={{0,8},{1,25},{2,10},{3,27},{4,12},{5,29},{6,14},{7,31},{8,16},{9,1... | collective-permute-start | bytes 786440 | tf_op jit(solution)/shard_map/ppermute | solution.py:63
  156.8 10.0 %collective-permute-start.26 = (f32[64,1536]{1,0:T(8,128)S(1)}, f32[64,1536]{1,0:T(8,128)S(1)}, u32[]{:S(2)}, u32[]{:S(2)}) collective-permute-start(f32[64,1536]{1,0:T(8,128)S(1)} %get-tuple-element.183), channel_id=1, source_target_pairs={{0,2},{1,7},{2,4},{3,1},{4,6},{5,3},{6,0},{7,5},{8,10},{9,15},{10,... | collective-permute-start | bytes 1179656 | tf_op jit(solution)/shard_map/ppermute | solution.py:63
  165.1 9.8 %collective-permute-start.30 = (f32[64,1536]{1,0:T(8,128)S(1)}, f32[64,1536]{1,0:T(8,128)S(1)}, u32[]{:S(2)}, u32[]{:S(2)}) collective-permute-start(f32[64,1536]{1,0:T(8,128)S(1)} %get-tuple-element.193), channel_id=1, source_target_pairs={{0,32},{1,97},{2,34},{3,99},{4,36},{5,101},{6,38},{7,103},{8,40},{... | collective-permute-start | bytes 1179656 | tf_op jit(solution)/shard_map/ppermute | solution.py:63
  166.8 7.6 %collective-permute-start.31 = (f32[64,1024]{1,0:T(8,128)S(1)}, f32[64,1024]{1,0:T(8,128)S(1)}, u32[]{:S(2)}, u32[]{:S(2)}) collective-permute-start(f32[64,1024]{1,0:T(8,128)S(1)} %get-tuple-element.195), channel_id=1, source_target_pairs={{0,8},{1,25},{2,10},{3,27},{4,12},{5,29},{6,14},{7,31},{8,16},{9,1... | collective-permute-start | bytes 786440 | tf_op jit(solution)/shard_map/ppermute | solution.py:63
  167.4 9.2 %collective-permute-start.29 = (f32[64,1536]{1,0:T(8,128)S(1)}, f32[64,1536]{1,0:T(8,128)S(1)}, u32[]{:S(2)}, u32[]{:S(2)}) collective-permute-start(f32[64,1536]{1,0:T(8,128)S(1)} %get-tuple-element.191), channel_id=1, source_target_pairs={{0,2},{1,7},{2,4},{3,1},{4,6},{5,3},{6,0},{7,5},{8,10},{9,15},{10,... | collective-permute-start | bytes 1179656 | tf_op jit(solution)/shard_map/ppermute | solution.py:63
  175.5 11.3 %collective-permute-start.33 = (f32[64,1536]{1,0:T(8,128)S(1)}, f32[64,1536]{1,0:T(8,128)S(1)}, u32[]{:S(2)}, u32[]{:S(2)}) collective-permute-start(f32[64,1536]{1,0:T(8,128)S(1)} %get-tuple-element.202), channel_id=1, source_target_pairs={{0,32},{1,97},{2,34},{3,99},{4,36},{5,101},{6,38},{7,103},{8,40},{... | collective-permute-start | bytes 1179656 | tf_op jit(solution)/shard_map/ppermute | solution.py:63
  176.5 9.7 %collective-permute-start.34 = (f32[64,1024]{1,0:T(8,128)S(1)}, f32[64,1024]{1,0:T(8,128)S(1)}, u32[]{:S(2)}, u32[]{:S(2)}) collective-permute-start(f32[64,1024]{1,0:T(8,128)S(1)} %get-tuple-element.204), channel_id=1, source_target_pairs={{0,8},{1,25},{2,10},{3,27},{4,12},{5,29},{6,14},{7,31},{8,16},{9,1... | collective-permute-start | bytes 786440 | tf_op jit(solution)/shard_map/ppermute | solution.py:63
  177.1 11.5 %collective-permute-start.32 = (f32[32,1536]{1,0:T(8,128)S(1)}, f32[32,1536]{1,0:T(8,128)S(1)}, u32[]{:S(2)}, u32[]{:S(2)}) collective-permute-start(f32[32,1536]{1,0:T(8,128)S(1)} %get-tuple-element.200), channel_id=1, source_target_pairs={{0,64},{1,65},{2,66},{3,67},{4,68},{5,69},{6,70},{7,71},{8,72},{9,... | collective-permute-start | bytes 589832 | tf_op jit(solution)/shard_map/ppermute | solution.py:59
  187.4 7.3 %collective-permute-start.36 = (f32[32,1536]{1,0:T(8,128)S(1)}, f32[32,1536]{1,0:T(8,128)S(1)}, u32[]{:S(2)}, u32[]{:S(2)}) collective-permute-start(f32[32,1536]{1,0:T(8,128)S(1)} %get-tuple-element.211), channel_id=1, source_target_pairs={{0,16},{1,17},{2,18},{3,19},{4,20},{5,21},{6,22},{7,23},{8,24},{9,... | collective-permute-start | bytes 589832 | tf_op jit(solution)/shard_map/ppermute | solution.py:59
  187.5 6.6 %collective-permute-start.37 = (f32[32,1024]{1,0:T(8,128)S(1)}, f32[32,1024]{1,0:T(8,128)S(1)}, u32[]{:S(2)}, u32[]{:S(2)}) collective-permute-start(f32[32,1024]{1,0:T(8,128)S(1)} %get-tuple-element.213), channel_id=1, source_target_pairs={{0,4},{1,5},{2,6},{3,7},{4,0},{5,1},{6,2},{7,3},{8,12},{9,13},{10,... | collective-permute-start | bytes 393224 | tf_op jit(solution)/shard_map/ppermute | solution.py:59
  189.2 13.8 %collective-permute-start.35 = (f32[16,1536]{1,0:T(8,128)S(1)}, f32[16,1536]{1,0:T(8,128)S(1)}, u32[]{:S(2)}, u32[]{:S(2)}) collective-permute-start(f32[16,1536]{1,0:T(8,128)S(1)} %get-tuple-element.209), channel_id=1, source_target_pairs={{0,32},{1,33},{2,34},{3,35},{4,36},{5,37},{6,38},{7,39},{8,40},{9,... | collective-permute-start | bytes 294920 | tf_op jit(solution)/shard_map/ppermute | solution.py:59
  195.8 7.2 %collective-permute-start.38 = (f32[16,1536]{1,0:T(8,128)S(1)}, f32[16,1536]{1,0:T(8,128)S(1)}, u32[]{:S(2)}, u32[]{:S(2)}) collective-permute-start(f32[16,1536]{1,0:T(8,128)S(1)} %get-tuple-element.217), channel_id=1, source_target_pairs={{0,8},{1,9},{2,10},{3,11},{4,12},{5,13},{6,14},{7,15},{8,0},{9,1},... | collective-permute-start | bytes 294920 | tf_op jit(solution)/shard_map/ppermute | solution.py:59
  198.7 4.3 %collective-permute-start.39 = (f32[16,1024]{1,0:T(8,128)S(1)}, f32[16,1024]{1,0:T(8,128)S(1)}, u32[]{:S(2)}, u32[]{:S(2)}) collective-permute-start(f32[16,1024]{1,0:T(8,128)S(1)} %get-tuple-element.219), channel_id=1, source_target_pairs={{0,2},{1,3},{2,0},{3,1},{4,6},{5,7},{6,4},{7,5},{8,10},{9,11},{10,... | collective-permute-start | bytes 196616 | tf_op jit(solution)/shard_map/ppermute | solution.py:59
  203.6 8.1 %collective-permute-start.42 = (f32[16,4096]{1,0:T(8,128)S(1)}, f32[16,4096]{1,0:T(8,128)S(1)}, u32[]{:S(2)}, u32[]{:S(2)}) collective-permute-start(f32[16,4096]{1,0:T(8,128)S(1)} %last.1.refs_0_), channel_id=1, source_target_pairs={{0,64},{1,65},{2,66},{3,67},{4,68},{5,69},{6,70},{7,71},{8,72},{9,... | collective-permute-start | bytes 786440 | tf_op jit(solution)/shard_map/ppermute | solution.py:63
  205.1 8.2 %collective-permute-start.41 = (f32[16,4096]{1,0:T(8,128)S(1)}, f32[16,4096]{1,0:T(8,128)S(1)}, u32[]{:S(2)}, u32[]{:S(2)}) collective-permute-start(f32[16,4096]{1,0:T(8,128)S(1)} %last.1.refs_0_), channel_id=1, source_target_pairs={{0,96},{1,97},{2,98},{3,99},{4,100},{5,101},{6,102},{7,103},{8,104... | collective-permute-start | bytes 786440 | tf_op jit(solution)/shard_map/ppermute | solution.py:63
  205.3 9.1 %collective-permute-start.40 = (f32[16,4096]{1,0:T(8,128)S(1)}, f32[16,4096]{1,0:T(8,128)S(1)}, u32[]{:S(2)}, u32[]{:S(2)}) collective-permute-start(f32[16,4096]{1,0:T(8,128)S(1)} %last.1.refs_0_), channel_id=1, source_target_pairs={{0,32},{1,33},{2,34},{3,35},{4,36},{5,37},{6,38},{7,39},{8,40},{9,... | collective-permute-start | bytes 786440 | tf_op jit(solution)/shard_map/ppermute | solution.py:63
  (3 other events, 5.4 us)

commit v2 on v1

--- a/solution.py
+++ b/solution.py
@@ -27,7 +27,6 @@
 
 KINDS = {"y": (0, 1, 2), "z": (3, 4, 5), "x": (6, 7)}
 GROUP = 2
-PIECE = 4
 
 
 def linear(p):
@@ -208,9 +207,8 @@
                     state = term if state is None else state * decay[j] + term
 
 
-def local_core(piece, q, k, v, cum, after, earlier):
-    steps = PIECE // GROUP
-    spec = pl.BlockSpec((TOK, GROUP * DK), lambda h: (0, h + piece * steps))
+def local_core(first, steps, q, k, v, cum, after, earlier):
+    spec = pl.BlockSpec((TOK, GROUP * DK), lambda h: (0, h + first))
     extra = list(earlier) + [after]
     shape = (TOK, H * DK)
     return pl.pallas_call(
@@ -222,7 +220,7 @@
         + [jax.ShapeDtypeStruct((8, DK), F32)],
         input_output_aliases={4 + i: i for i in range(len(earlier))},
         compiler_params=params(PIECE_LIMIT),
-        cost_estimate=cost(2 * TOK * DK * DK * PIECE * 8, 20e6, 4 * TOK * DK * PIECE),
+        cost_estimate=cost(64 * TOK * DK * DK, 20e6, 16 * TOK * DK),
         name="local_core",
     )(q, k, v, cum, *extra)
 
@@ -330,18 +328,18 @@
     *parts, wide = chip_total(where, keep, got, wide)
     other = send(wide, "c", 1)
     arrived = around(parts, "z")
-    *local, token = local_core(0, q, k, v, cum, parts[1], ())
+    *local, token = local_core(0, 3, q, k, v, cum, parts[1], ())
     prefix, total = small_call(
         row_kernel, where, arrived, [(4,) + msg, msg], [(4,) + msg], [token], "row_total"
     )
     rows = around([total] * 4, "y")
-    *local, token = local_core(1, q, k, v, cum, total, local)
+    *local, token = local_core(3, 2, q, k, v, cum, total, local)
     out = (4, HALF, DK)
     back = small_call(
         back_kernel, where, [prefix] + rows, [out] * 4, [(4,) + msg], [token], "row_start"
     )
     arrived = around(back, "z")
-    *local, token = local_core(2, q, k, v, cum, back[1], local)
+    *local, token = local_core(5, 2, q, k, v, cum, back[1], local)
     mine, theirs = small_call(
         core_start_kernel,
         where,
@@ -350,7 +348,7 @@
         after=[token],
         name="core_start",
     )
-    *local, token = local_core(3, q, k, v, cum, theirs, local)
+    *local, token = local_core(7, 1, q, k, v, cum, theirs, local)
     return mine, send(theirs, "c", 1), local, other
 
 
@@ -401,8 +399,8 @@
 CHUNK = {"x": (4, 4, 1, 16, TOK), "y": (1, 4, 4, 16, TOK), "z": (4, 1, 4, 16, TOK)}
 
 
-def product_kernel(axis, where_ref, keep_ref, got_ref, own_ref, other_ref, *refs):
-    outs, token_ref, left_ref, right_ref = refs[-8:-3], refs[-3], refs[-2], refs[-1]
+def product_kernel(axis, steps, where_ref, keep_ref, got_ref, own_ref, other_ref, *refs):
+    *outs, token_ref, left_ref, right_ref = refs[-3 - len(steps) :]
     core = where_ref[3]
     token_ref[...] = jnp.zeros_like(token_ref)
 
@@ -416,34 +414,32 @@
     @pl.when(pl.program_id(0) == 0)
     def _():
         me = where_ref[AXES.index(axis)]
-        for t, d in enumerate((2, 1 + 2 * core, 3 - 2 * core, 0)):
-            j = lax.rem(me + d, 4)
+        for t, step in enumerate(steps):
+            j = lax.rem(me + step(core), 4)
             for part, ref in enumerate((keep_ref, got_ref)):
-                both = chunk(ref, j).reshape(256, TOK).astype(BF16)
                 lanes = slice(part * TOK, (part + 1) * TOK)
-                low, high = both[:128], both[128:]
-                left_ref[256 * t : 256 * t + 128, lanes] = jnp.where(core == 0, low, high)
-                left_ref[256 * t + 128 : 256 * t + 256, lanes] = jnp.where(core == 0, high, low)
+                rows = chunk(ref, j).reshape(256, TOK)
+                left_ref[256 * t : 256 * (t + 1), lanes] = rows.astype(BF16)
 
     right_ref[:TOK, :] = own_ref[...]
     right_ref[TOK:, :] = other_ref[...].astype(BF16)
     total = jnp.dot(left_ref[...], right_ref[...], preferred_element_type=F32)
-    opposite, after, before, mine = (total[256 * t : 256 * (t + 1)] for t in range(4))
-    outs[0][...] = opposite[:128]
-    outs[1][...] = opposite[128:]
-    outs[2][...] = after
-    outs[3][...] = before
-    outs[4][...] = mine
-
-
-def products(axis, where, keep, got, own, other, after):
+    for t, out in enumerate(outs):
+        out[...] = total[256 * t : 256 * (t + 1)]
+
+
+BEFORE, OPPOSITE = (lambda core: 3 - 2 * core), (lambda core: 2)
+AFTER, MINE = (lambda core: 1 + 2 * core), (lambda core: 0)
+
+
+def products(axis, steps, where, keep, got, own, other, after):
     blocks = KINDS[axis]
-    rows = (128,) * 2 + (256,) * 3
+    rows = (256,) * len(steps)
     cotan = pl.BlockSpec((TOK, COLS), lambda i, w: (0, blocks[0] + i))
     whole = pl.BlockSpec((4, 4, 4, 16, TOK), lambda i, w: (0, 0, 0, 0, 0))
     width = COLS * len(blocks)
     return pl.pallas_call(
-        functools.partial(product_kernel, axis),
+        functools.partial(product_kernel, axis, steps),
         grid_spec=pltpu.PrefetchScalarGridSpec(
             num_scalar_prefetch=1,
             grid=(len(blocks),),
@@ -452,14 +448,14 @@
             out_specs=[pl.BlockSpec((r, COLS), lambda i, w: (0, i)) for r in rows]
             + [pl.BlockSpec((8, DK), lambda i, w: (0, 0))],
             scratch_shapes=[
-                pltpu.VMEM((1024, 2 * TOK), BF16),
+                pltpu.VMEM((256 * len(steps), 2 * TOK), BF16),
                 pltpu.VMEM((2 * TOK, COLS), BF16),
             ],
         ),
         out_shape=[jax.ShapeDtypeStruct((r, width), F32) for r in rows]
         + [jax.ShapeDtypeStruct((8, DK), F32)],
         compiler_params=params(PRODUCT_LIMIT),
-        cost_estimate=cost(4 * 1024 * TOK * width, 8000 * width),
+        cost_estimate=cost(1e6, 1e6),
         name="products_" + axis,
     )(where, keep, got, own, other, *after)
 
@@ -470,14 +466,13 @@
     token[...] = jnp.zeros_like(token)
 
 
-def relay(term, arrived, half, after):
-    width = term.shape[1]
-    spec = pl.BlockSpec((128, COLS), lambda i: (half, i))
-    came = pl.BlockSpec((128, COLS), lambda i: (0, i))
+def relay(term, arrived, after):
+    rows, width = term.shape
+    spec = pl.BlockSpec((rows, COLS), lambda i: (0, i))
     return pl.pallas_call(
         relay_kernel,
         grid=(width // COLS,),
-        in_specs=[spec, came] + [pl.BlockSpec(memory_space=pl.ANY)] * len(after),
+        in_specs=[spec] * 2 + [pl.BlockSpec(memory_space=pl.ANY)] * len(after),
         out_specs=[spec, pl.BlockSpec((8, DK), lambda i: (0, 0))],
         out_shape=[
             jax.ShapeDtypeStruct(term.shape, F32),
@@ -485,17 +480,15 @@
         ],
         input_output_aliases={0: 0},
         compiler_params=params(SMALL_LIMIT),
-        cost_estimate=cost(128 * width, 12 * 128 * width),
+        cost_estimate=cost(rows * width, 12 * rows * width),
         name="relay",
     )(term, arrived, *after)
 
 
-def second_kernel(axis, me, where_ref, mine, a, b, *rest):
-    outs, token, total = rest[:4], rest[4], rest[5]
+def second_kernel(axis, me, where_ref, mine, *rest):
+    came, outs, total = rest[:-5], rest[-5:-1], rest[-1]
     core = where_ref[3]
-    start = pl.multiple_of(128 * core, 128)
-    total[pl.ds(start, 128), :] = mine[:128] + (a[:128] + b[:128])
-    total[pl.ds(128 - start, 128), :] = mine[128:] + (a[128:] + b[128:])
+    total[...] = sum((ref[...] for ref in came), mine[...])
     for t in range(4):
         j = lax.rem(where_ref[me] + jnp.where(core == 0, 7 - t, 1 + t), 4)
         if axis == "z":
@@ -504,21 +497,18 @@
                 outs[t][16 * y : 16 * (y + 1), :] = total[pl.ds(row, 16), :]
         else:
             outs[t][...] = total[pl.ds(pl.multiple_of(64 * j, 64), 64), :]
-    token[...] = jnp.zeros_like(token)
-
-
-def add_kernel(where_ref, a, b, out, token):
+
+
+def add_kernel(where_ref, a, b, out):
     out[...] = a[...] + b[...]
-    token[...] = jnp.zeros_like(token)
-
-
-def halves_kernel(me, place, where_ref, a, b, keep, away, token, total):
+
+
+def halves_kernel(me, place, where_ref, a, b, keep, away, total):
     total[...] = a[...] + b[...]
     rows = keep.shape[0]
     row = rows * place(where_ref[me])
     keep[...] = total[pl.ds(pl.multiple_of(row, rows), rows), :]
     away[...] = total[pl.ds(pl.multiple_of(rows - row, rows), rows), :]
-    token[...] = jnp.zeros_like(token)
 
 
 def last_kernel(where_ref, *refs):
@@ -530,6 +520,22 @@
         col += width
 
 
+def together(kernels, where, ins, outs, scratch, name):
+    def body(where_ref, *refs):
+        sets = [[] for _ in kernels]
+        at = 0
+        for lists in (ins, outs, scratch):
+            for mine, part in zip(sets, lists):
+                mine += refs[at : at + len(part)]
+                at += len(part)
+        for kernel, mine in zip(kernels, sets):
+            kernel(where_ref, *mine)
+
+    flat = lambda lists: [item for part in lists for item in part]
+    results = iter(small_call(body, where, flat(ins), flat(outs), flat(scratch), (), name))
+    return [[next(results) for _ in part] for part in outs]
+
+
 def around(pieces, axis):
     return [pieces[0]] + [send(pieces[d], axis, d) for d in (1, 3, 2)]
 
@@ -551,71 +557,73 @@
     theirs = send(away, "c", 1).reshape(4, 4, 4, 16, TOK)
     keep = keep.reshape(4, 4, 4, 16, TOK)
 
-    forward = lambda c: 1 - 2 * c
-    back = lambda c: 2 * c - 1
-    terms, ahead, behind, low, high = {}, {}, {}, {}, {}
-
-    def start(axis, after):
-        *t, token = products(axis, where, keep, theirs, own, other, after)
-        terms[axis] = t
-        ahead[axis] = send(t[0], axis, forward)
-        behind[axis] = send(t[1], axis, back)
-        return [token]
-
-    def relay_low(axis, after):
-        term, *token = relay(terms[axis][2], ahead[axis], 0, after)
-        low[axis] = send(term, axis, forward)
-        return token
-
-    def relay_high(axis, after):
-        term, *token = relay(terms[axis][3], behind[axis], 1, after)
-        high[axis] = send(term, axis, back)
-        return token
-
-    token = start("y", ())
-    token = start("z", token)
-    token = start("x", token)
-    token = relay_low("y", token)
-    token = relay_low("z", token)
-    token = relay_high("y", token)
-    token = relay_high("z", token)
-    token = relay_low("x", token)
-    token = relay_high("x", token)
+    forward, backward = (lambda c: 1 - 2 * c), (lambda c: 2 * c - 1)
+    order = ("x", "y", "z")
+    terms, came = {}, {}
+    token = ()
+    for axis in ("y", "z", "x"):
+        first = (BEFORE,) if axis == "x" else (OPPOSITE,)
+        term, *token = products(axis, first, where, keep, theirs, own, other, token)
+        came[axis] = send(term, axis, forward)
+    for axis in ("x", "y", "z"):
+        others = (OPPOSITE, AFTER, MINE) if axis == "x" else (BEFORE, AFTER, MINE)
+        *terms[axis], t = products(axis, others, where, keep, theirs, own, other, token)
+        token = [t]
+
+    def pass_on(axis, n, after):
+        term, *after = relay(terms[axis][n], came[axis], after)
+        came[axis] = send(term, axis, forward)
+        return after
+
+    direct = {axis: (send(terms[axis][0], axis, backward),) for axis in ("y", "z")}
+    direct["x"] = ()
+    token = pass_on("x", 0, token)
+    token = pass_on("y", 1, token)
+    token = pass_on("z", 1, token)
+    token = pass_on("x", 1, token)
 
     following = {"x": ("y", "z"), "y": ("z", "x"), "z": ("x", "y")}
-    tail = [(8, DK)]
-    order = ("y", "x", "z")
-    parts, came, rounds = {}, {}, {}
-    for axis in order:
-        a2 = following[axis][0]
-        width = COLS * len(KINDS[axis])
-        kernel = functools.partial(second_kernel, axis, AXES.index(a2))
-        outs = [(64, width)] * 4 + tail
-        ins = [terms[axis][4], low[axis], high[axis]]
-        *parts[axis], t = small_call(kernel, where, ins, outs, [(256, width)], token, "second")
-        came[axis] = send(parts[axis][0], a2, forward)
-        token = [t]
+    width = {axis: COLS * len(KINDS[axis]) for axis in order}
+    parts = together(
+        [functools.partial(second_kernel, a, AXES.index(following[a][0])) for a in order],
+        where,
+        [[terms[a][2], came[a], *direct[a]] for a in order],
+        [[(64, width[a])] * 4 for a in order],
+        [[(256, width[a])] for a in order],
+        "second",
+    )
+    held = [part[0] for part in parts]
     for step in (1, 2):
-        for axis in order:
-            part = parts[axis][step]
-            ins = [part, came[axis]]
-            part, t = small_call(add_kernel, where, ins, [part.shape] + tail, (), token, "add")
-            came[axis] = send(part, following[axis][0], forward)
-            token = [t]
-    for axis in order:
-        rounds[axis] = parts[axis][3], came[axis]
+        came = [send(h, following[a][0], forward) for h, a in zip(held, order)]
+        held = together(
+            [add_kernel] * 3,
+            where,
+            [[part[step], c] for part, c in zip(parts, came)],
+            [[(64, width[a])] for a in order],
+            [[]] * 3,
+            "add",
+        )
+        held = [h[0] for h in held]
+    came = [send(h, following[a][0], forward) for h, a in zip(held, order)]
+    pairs = [[part[3], c] for part, c in zip(parts, came)]
     upper, odd = (lambda p: lax.div(p, 2)), (lambda p: lax.rem(p, 2))
     for rows, distance, place_of in ((32, 2, upper), (16, 1, odd)):
-        for axis in order:
-            a3 = following[axis][1]
-            width = COLS * len(KINDS[axis])
-            kernel = functools.partial(halves_kernel, AXES.index(a3), place_of)
-            outs = [(rows, width)] * 2 + tail
-            keep, away, t = small_call(
-                kernel, where, rounds[axis], outs, [(2 * rows, width)], token, "halves"
-            )
-            rounds[axis] = keep, swap(away, a3, distance)
-            token = [t]
+        pairs = together(
+            [
+                functools.partial(halves_kernel, AXES.index(following[a][1]), place_of)
+                for a in order
+            ],
+            where,
+            pairs,
+            [[(rows, width[a])] * 2 for a in order],
+            [[(2 * rows, width[a])] for a in order],
+            "halves",
+        )
+        pairs = [
+            [keep, swap(away, following[a][1], distance)]
+            for (keep, away), a in zip(pairs, order)
+        ]
+    rounds = dict(zip(order, pairs))
     (mine,) = small_call(
         last_kernel, where, [r for axis in KINDS for r in rounds[axis]], [(16, D)], name="last"
     )

time: 216 us -> 201 us (0.931)
  waiting for transfers between devices: 92.7 us -> 77.5 us
    ppermute x37 -> x34, waiting for transfers between devices: 84 us -> 72.2 us  [send(): return lax.ppermute(array, AXES, shift_pairs(axis, by))]
    pallas_call x19 -> x9, Pallas kernels: 13 us -> 6.92 us  [small_call(): pl.pallas_call(body, in_specs=[pl.BlockSpec(memory_space=pltpu.SMEM)] + w...]
    pallas_call x9 -> x10, Pallas kernels: 16 us -> 20.7 us  [the longest x6 18.3 us: products(): pl.pallas_call(functools.partial(product_kernel, axis, steps), grid_spec=...]
    ppermute x6, starting transfers between devices: 6.96 us -> 11.4 us  [swap(): return lax.ppermute(array, AXES, pairs)]
    ppermute x6, waiting for transfers between devices: 8.64 us -> 5.26 us  [swap(): return lax.ppermute(array, AXES, pairs)]
    ppermute x37 -> x34, starting transfers between devices: 41.8 us -> 39.4 us  [send(): return lax.ppermute(array, AXES, shift_pairs(axis, by))]
  transfers between devices with their start and end apart: 43 -> 40, of which waited for: 23 -> 24; matrix products, arithmetic and copies ran while one was open for 0% -> 0% of each run, Pallas kernels for 23% -> 21%
where the time goes in v2:
time: 201 us
  waiting for transfers between devices  77.5 us (39%)
  Pallas kernels  64.1 us (32%)
  starting transfers between devices  50.8 us (25%)
  local copies, waits for them, and re-layouts  7.58 us (4%)
    ppermute x34, waiting for transfers between devices, send(): return lax.ppermute(array, AXES, shift_pairs(axis, by))  72.2 us
    ppermute x34, starting transfers between devices, send(): return lax.ppermute(array, AXES, shift_pairs(axis, by))  39.4 us
    pallas_call x6, Pallas kernels, products(): pl.pallas_call(functools.partial(product_kernel, axis, steps), grid_spec=...  18.3 us
    pallas_call x4, Pallas kernels, local_core(): pl.pallas_call(core_kernel, grid=(steps,), in_specs=[spec] * 4 + [pl.Bloc...  18.1 us
    ppermute x6, starting transfers between devices, swap(): return lax.ppermute(array, AXES, pairs)  11.4 us
    pallas_call x1, Pallas kernels, local_state(): pl.pallas_call(state_kernel, grid_spec=pltpu.PrefetchScalarGridSpec(num_s...  8.21 us
    pallas_call x1, Pallas kernels, gated(): pl.pallas_call(hidden_kernel, grid_spec=pltpu.PrefetchScalarGridSpec(num_...  7.96 us
    unnamed x16, local copies, waits for them, and re-layouts  7.58 us
  transfers between devices with their start and end apart: 40, of which 24 were waited for; matrix products, arithmetic and copies ran while one was open for 0% of the time, Pallas kernels for 21%

profile of v2, /device:TPU:0, one launch (start us, length us, event | category | flops | bytes accessed | tf_op | source)
XLA Modules:
  0.0 201.0 jit_solution(5339823367005596754)
XLA Ops:
  0.7 2.2 %copy-done = bf16[1,512,4096]{2,1,0:T(8,128)(2,1)S(1)} copy-done((bf16[1,512,4096]{2,1,0:T(8,128)(2,1)S(1)}, bf16[1,512,4096]{2,1,0:T(8,128)(2,1)}, u32[]{:S(2)}) %copy-start) | copy-done | bytes 4194328
  2.9 1.6 copy-done.2
  4.5 1.6 copy-done.4
  6.1 2.2 %copy-done.6 = f32[1,512,2048]{2,1,0:T(8,128)S(1)} copy-done((f32[1,512,2048]{2,1,0:T(8,128)S(1)}, f32[1,512,2048]{2,1,0:T(8,128)}, u32[]{:S(2)}) %copy-start.6) | copy-done | bytes 4194328
  8.3 8.2 %local_state.1 = (f32[16,72,128]{2,1,0:T(8,128)S(1)}, f32[16,72,128]{2,1,0:T(8,128)S(1)}, f32[512,2048]{1,0:T(8,128)S(1)}, f32[512,4096]{1,0:T(8,128)}) custom-call(s32[4]{0:T(128)S(1)} %pad_add_fusion.where_ref.refs_0_, bf16[512,2048]{1,0:T(8,128)(2,1)S(1)} %bitcast.26, bf16[512,2048]{1,0:T(8,128)(2,1)S(1)} %bitcast.31, f32[512,2048]{1,0:T(8,128)S(1)} %bitcast.46, ...), custom_call_target="tpu_custom_call" | custom-call | flops 268435456 | bytes 26000000 | tf_op jit(solution)/shard_map/local_state/pallas_call | solution.py:147
  16.5 2.0 collective-permute-done.got_ref.refs_2_
  19.4 4.1 %collective-permute-start.2 = (f32[4,72,128]{2,1,0:T(8,128)S(1)}, f32[4,72,128]{2,1,0:T(8,128)S(1)}, u32[]{:S(2)}, u32[]{:S(2)}) collective-permute-start(f32[4,72,128]{2,1,0:T(8,128)S(1)} %get-tuple-element.101), channel_id=1, source_target_pairs={{0,6},{1,7},{2,0},{3,1},{4,2},{5,3},{6,4},{7,5},{8,14},{9,15},{10,... | collective-permute-start | bytes 442376 | tf_op jit(solution)/shard_map/ppermute | solution.py:62
  24.8 6.7 %local_core.4 = (f32[512,2048]{1,0:T(8,128)S(1)}, bf16[512,2048]{1,0:T(8,128)(2,1)S(1)}, bf16[512,2048]{1,0:T(8,128)(2,1)S(1)}, f32[8,128]{1,0:T(8,128)S(1)}) custom-call(bf16[512,2048]{1,0:T(8,128)(2,1)S(1)} %bitcast.42, bf16[512,2048]{1,0:T(8,128)(2,1)S(1)} %bitcast.27, bf16[512,2048]{1,0:T(8,128)(2,1)S(1)} %bitcast.32, ...), custom_call_target="tpu_custom_call" | custom-call | flops 536870912 | bytes 20000000 | tf_op jit(solution)/shard_map/local_core/pallas_call | solution.py:214
  31.7 2.0 collective-permute-done.1.refs_2_
  34.3 3.3 %collective-permute-start.6 = (f32[4,72,128]{2,1,0:T(8,128)S(1)}, f32[4,72,128]{2,1,0:T(8,128)S(1)}, u32[]{:S(2)}, u32[]{:S(2)}) collective-permute-start(f32[4,72,128]{2,1,0:T(8,128)S(1)} %get-tuple-element.104.rest_3_.refs_2_), channel_id=1, source_target_pairs={{0,16},{1,17},{2,18},{3,19},{4,20},{5,21},{6,22},{7,23},{8,24},{9,... | collective-permute-start | bytes 442376 | tf_op jit(solution)/shard_map/ppermute | solution.py:62
  39.6 4.5 %local_core.5 = (f32[512,2048]{1,0:T(8,128)S(1)}, bf16[512,2048]{1,0:T(8,128)(2,1)S(1)}, bf16[512,2048]{1,0:T(8,128)(2,1)S(1)}, f32[8,128]{1,0:T(8,128)S(1)}) custom-call(bf16[512,2048]{1,0:T(8,128)(2,1)S(1)} %bitcast.43, bf16[512,2048]{1,0:T(8,128)(2,1)S(1)} %bitcast.28, ...), custom_call_target="tpu_custom_call", output_to_operand_aliasing={{0}: (4, {}), {1}: (5, {}), {2}: (6, {})} | custom-call | flops 536870912 | bytes 20000000 | tf_op jit(solution)/shard_map/local_core/pallas_call | solution.py:214
  48.2 4.5 %local_core.6 = (f32[512,2048]{1,0:T(8,128)S(1)}, bf16[512,2048]{1,0:T(8,128)(2,1)S(1)}, bf16[512,2048]{1,0:T(8,128)(2,1)S(1)}, f32[8,128]{1,0:T(8,128)S(1)}) custom-call(bf16[512,2048]{1,0:T(8,128)(2,1)S(1)} %bitcast.44, bf16[512,2048]{1,0:T(8,128)(2,1)S(1)} %bitcast.29, ...), custom_call_target="tpu_custom_call", output_to_operand_aliasing={{0}: (4, {}), {1}: (5, {}), {2}: (6, {})} | custom-call | flops 536870912 | bytes 20000000 | tf_op jit(solution)/shard_map/local_core/pallas_call | solution.py:214
  55.8 2.5 %local_core.7 = (f32[512,2048]{1,0:T(8,128)S(1)}, bf16[512,2048]{1,0:T(8,128)(2,1)S(1)}, bf16[512,2048]{1,0:T(8,128)(2,1)S(1)}, f32[8,128]{1,0:T(8,128)}) custom-call(bf16[512,2048]{1,0:T(8,128)(2,1)S(1)} %bitcast.45, bf16[512,2048]{1,0:T(8,128)(2,1)S(1)} %bitcast.30, ...), custom_call_target="tpu_custom_call", output_to_operand_aliasing={{0}: (4, {}), {1}: (5, {}), {2}: (6, {})} | custom-call | flops 536870912 | bytes 20000000 | tf_op jit(solution)/shard_map/local_core/pallas_call | solution.py:214
  58.3 8.0 %gated_hidden.1 = (bf16[512,2048]{1,0:T(8,128)(2,1)}, bf16[1024,512]{1,0:T(8,128)(2,1)S(1)}, f32[1024,512]{1,0:T(8,128)S(1)}) custom-call(s32[4]{0:T(128)S(1)} %pad_add_fusion.where_ref.refs_0_, f32[512,2048]{1,0:T(8,128)S(1)} %get-tuple-element.119.out_ref, bf16[512,2048]{1,0:T(8,128)(2,1)S(1)} %get-tuple-element.120.high_ref, ...), custom_call_target="tpu_custom_call" | custom-call | flops 805306368 | bytes 17000000 | tf_op jit(solution)/shard_map/gated_hidden/pallas_call | solution.py:380
  66.8 3.8 %collective-permute-done.11 = f32[1024,512]{1,0:T(8,128)S(1)} collective-permute-done((f32[1024,512]{1,0:T(8,128)S(1)}, f32[1024,512]{1,0:T(8,128)S(1)}, u32[]{:S(2)}, u32[]{:S(2)}) %collective-permute-start.11) | collective-permute-done | bytes 2097184 | tf_op jit(solution)/shard_map/ppermute | solution.py:62
  70.6 2.4 %products_y.2 = (f32[256,1536]{1,0:T(8,128)S(1)}, f32[8,128]{1,0:T(8,128)S(1)}) custom-call(s32[4]{0:T(128)S(1)} %pad_add_fusion.where_ref.refs_0_, bf16[4,4,4,16,512]{4,3,2,1,0:T(8,128)(2,1)S(1)} %bitcast.36, f32[4,4,4,16,512]{4,3,2,1,0:T(8,128)S(1)} %bitcast.20, bf16[512,4096]{1,0:T(8,128)(2,1)S(1)} %bitcast.14, ...), custom_call_target="tpu_custom_call" | custom-call | flops 1000000 | bytes 1000000 | tf_op jit(solution)/shard_map/products_y/pallas_call | solution.py:441
  73.0 2.4 %products_z.2 = (f32[256,1536]{1,0:T(8,128)S(1)}, f32[8,128]{1,0:T(8,128)S(1)}) custom-call(s32[4]{0:T(128)S(1)} %pad_add_fusion.where_ref.refs_0_, bf16[4,4,4,16,512]{4,3,2,1,0:T(8,128)(2,1)S(1)} %bitcast.37, f32[4,4,4,16,512]{4,3,2,1,0:T(8,128)S(1)} %bitcast.21, bf16[512,4096]{1,0:T(8,128)(2,1)S(1)} %bitcast.15, ...), custom_call_target="tpu_custom_call" | custom-call | flops 1000000 | bytes 1000000 | tf_op jit(solution)/shard_map/products_z/pallas_call | solution.py:441
  75.4 1.8 products_x.2
  77.2 1.6 collective-permute-start.13
  78.8 1.7 collective-permute-start.16
  80.5 3.1 %products_x.3 = (f32[256,1024]{1,0:T(8,128)S(1)}, f32[256,1024]{1,0:T(8,128)S(1)}, f32[256,1024]{1,0:T(8,128)S(1)}, f32[8,128]{1,0:T(8,128)S(1)}) custom-call(s32[4]{0:T(128)S(1)} %pad_add_fusion.where_ref.refs_0_, bf16[4,4,4,16,512]{4,3,2,1,0:T(8,128)(2,1)S(1)} %bitcast.39, f32[4,4,4,16,512]{4,3,2,1,0:T(8,128)S(1)} %bitcast.23, ...), custom_call_target="tpu_custom_call" | custom-call | flops 1000000 | bytes 1000000 | tf_op jit(solution)/shard_map/products_x/pallas_call | solution.py:441
  83.6 4.3 %products_y.3 = (f32[256,1536]{1,0:T(8,128)S(1)}, f32[256,1536]{1,0:T(8,128)S(1)}, f32[256,1536]{1,0:T(8,128)S(1)}, f32[8,128]{1,0:T(8,128)S(1)}) custom-call(s32[4]{0:T(128)S(1)} %pad_add_fusion.where_ref.refs_0_, bf16[4,4,4,16,512]{4,3,2,1,0:T(8,128)(2,1)S(1)} %bitcast.40, f32[4,4,4,16,512]{4,3,2,1,0:T(8,128)S(1)} %bitcast.24, ...), custom_call_target="tpu_custom_call" | custom-call | flops 1000000 | bytes 1000000 | tf_op jit(solution)/shard_map/products_y/pallas_call | solution.py:441
  87.9 4.3 %products_z.3 = (f32[256,1536]{1,0:T(8,128)S(1)}, f32[256,1536]{1,0:T(8,128)S(1)}, f32[256,1536]{1,0:T(8,128)S(1)}, f32[8,128]{1,0:T(8,128)S(1)}) custom-call(s32[4]{0:T(128)S(1)} %pad_add_fusion.where_ref.refs_0_, bf16[4,4,4,16,512]{4,3,2,1,0:T(8,128)(2,1)S(1)} %bitcast.41, f32[4,4,4,16,512]{4,3,2,1,0:T(8,128)S(1)} %bitcast.25, ...), custom_call_target="tpu_custom_call" | custom-call | flops 1000000 | bytes 1000000 | tf_op jit(solution)/shard_map/products_z/pallas_call | solution.py:441
  94.2 3.2 %collective-permute-start.21 = (f32[256,1536]{1,0:T(8,128)S(1)}, f32[256,1536]{1,0:T(8,128)S(1)}, u32[]{:S(2)}, u32[]{:S(2)}) collective-permute-start(f32[256,1536]{1,0:T(8,128)S(1)} %get-tuple-element.151), channel_id=1, source_target_pairs={{0,6},{1,3},{2,0},{3,5},{4,2},{5,7},{6,4},{7,1},{8,14},{9,11},{10,... | collective-permute-start | bytes 4718600 | tf_op jit(solution)/shard_map/ppermute | solution.py:62
  97.4 1.5 collective-permute-start.19
  98.9 1.5 collective-permute-done.16.b
  100.9 2.9 %collective-permute-done.15.b = f32[256,1536]{1,0:T(8,128)S(1)} collective-permute-done((f32[256,1536]{1,0:T(8,128)S(1)}, f32[256,1536]{1,0:T(8,128)S(1)}, u32[]{:S(2)}, u32[]{:S(2)}) %collective-permute-start.15) | collective-permute-done | bytes 1572896 | tf_op jit(solution)/shard_map/ppermute | solution.py:62
  104.5 1.9 collective-permute-start.18
  106.4 3.3 %collective-permute-done.14.b = f32[256,1024]{1,0:T(8,128)S(1)} collective-permute-done((f32[256,1024]{1,0:T(8,128)S(1)}, f32[256,1024]{1,0:T(8,128)S(1)}, u32[]{:S(2)}, u32[]{:S(2)}) %collective-permute-start.14) | collective-permute-done | bytes 1048608 | tf_op jit(solution)/shard_map/ppermute | solution.py:62
  111.2 16.9 %collective-permute-done.21.refs_8_ = f32[256,1536]{1,0:T(8,128)S(1)} collective-permute-done((f32[256,1536]{1,0:T(8,128)S(1)}, f32[256,1536]{1,0:T(8,128)S(1)}, u32[]{:S(2)}, u32[]{:S(2)}) %collective-permute-start.21) | collective-permute-done | bytes 1572896 | tf_op jit(solution)/shard_map/ppermute | solution.py:62
  128.1 7.7 %collective-permute-done.20.refs_7_ = f32[256,1536]{1,0:T(8,128)S(1)} collective-permute-done((f32[256,1536]{1,0:T(8,128)S(1)}, f32[256,1536]{1,0:T(8,128)S(1)}, u32[]{:S(2)}, u32[]{:S(2)}) %collective-permute-start.20) | collective-permute-done | bytes 1572896 | tf_op jit(solution)/shard_map/ppermute | solution.py:62
  135.8 1.7 second.1
  137.6 1.6 collective-permute-start.24
  140.5 6.2 %collective-permute-done.22.refs_2_ = f32[64,1024]{1,0:T(8,128)S(1)} collective-permute-done((f32[64,1024]{1,0:T(8,128)S(1)}, f32[64,1024]{1,0:T(8,128)S(1)}, u32[]{:S(2)}, u32[]{:S(2)}) %collective-permute-start.22) | collective-permute-done | bytes 262176 | tf_op jit(solution)/shard_map/ppermute | solution.py:62
  147.5 1.4 collective-permute-start.27
  150.3 6.2 %collective-permute-done.25.refs_2_ = f32[64,1024]{1,0:T(8,128)S(1)} collective-permute-done((f32[64,1024]{1,0:T(8,128)S(1)}, f32[64,1024]{1,0:T(8,128)S(1)}, u32[]{:S(2)}, u32[]{:S(2)}) %collective-permute-start.25) | collective-permute-done | bytes 262176 | tf_op jit(solution)/shard_map/ppermute | solution.py:62
  157.2 2.6 %collective-permute-start.29 = (f32[64,1536]{1,0:T(8,128)S(1)}, f32[64,1536]{1,0:T(8,128)S(1)}, u32[]{:S(2)}, u32[]{:S(2)}) collective-permute-start(f32[64,1536]{1,0:T(8,128)S(1)} %get-tuple-element.167), channel_id=1, source_target_pairs={{0,2},{1,7},{2,4},{3,1},{4,6},{5,3},{6,0},{7,5},{8,10},{9,15},{10,... | collective-permute-start | bytes 1179656 | tf_op jit(solution)/shard_map/ppermute | solution.py:62
  160.2 7.2 %collective-permute-done.28.refs_2_ = f32[64,1024]{1,0:T(8,128)S(1)} collective-permute-done((f32[64,1024]{1,0:T(8,128)S(1)}, f32[64,1024]{1,0:T(8,128)S(1)}, u32[]{:S(2)}, u32[]{:S(2)}) %collective-permute-start.28) | collective-permute-done | bytes 262176 | tf_op jit(solution)/shard_map/ppermute | solution.py:62
  167.4 1.4 collective-permute-done.30.refs_6_
  169.5 2.0 collective-permute-start.32
  172.6 4.2 %collective-permute-start.31 = (f32[32,1024]{1,0:T(8,128)S(1)}, f32[32,1024]{1,0:T(8,128)S(1)}, u32[]{:S(2)}, u32[]{:S(2)}) collective-permute-start(f32[32,1024]{1,0:T(8,128)S(1)} %get-tuple-element.171), channel_id=1, source_target_pairs={{0,4},{1,5},{2,6},{3,7},{4,0},{5,1},{6,2},{7,3},{8,12},{9,13},{10,... | collective-permute-start | bytes 393224 | tf_op jit(solution)/shard_map/ppermute | solution.py:58
  176.9 3.0 %collective-permute-done.31.refs_2_ = f32[32,1024]{1,0:T(8,128)S(1)} collective-permute-done((f32[32,1024]{1,0:T(8,128)S(1)}, f32[32,1024]{1,0:T(8,128)S(1)}, u32[]{:S(2)}, u32[]{:S(2)}) %collective-permute-start.31) | collective-permute-done | bytes 131104 | tf_op jit(solution)/shard_map/ppermute | solution.py:58
  180.9 3.6 %collective-permute-start.36 = (f32[16,1024]{1,0:T(8,128)S(1)}, f32[16,1024]{1,0:T(8,128)S(1)}, u32[]{:S(2)}, u32[]{:S(2)}) collective-permute-start(f32[16,1024]{1,0:T(8,128)S(1)} %get-tuple-element.181), channel_id=1, source_target_pairs={{0,2},{1,3},{2,0},{3,1},{4,6},{5,7},{6,4},{7,5},{8,10},{9,11},{10,... | collective-permute-start | bytes 196616 | tf_op jit(solution)/shard_map/ppermute | solution.py:58
  184.6 2.2 %collective-permute-done.36.refs_6_ = f32[16,1024]{1,0:T(8,128)S(1)} collective-permute-done((f32[16,1024]{1,0:T(8,128)S(1)}, f32[16,1024]{1,0:T(8,128)S(1)}, u32[]{:S(2)}, u32[]{:S(2)}) %collective-permute-start.36) | collective-permute-done | bytes 65568 | tf_op jit(solution)/shard_map/ppermute | solution.py:58
  187.4 3.7 %collective-permute-start.39 = (f32[16,4096]{1,0:T(8,128)S(1)}, f32[16,4096]{1,0:T(8,128)S(1)}, u32[]{:S(2)}, u32[]{:S(2)}) collective-permute-start(f32[16,4096]{1,0:T(8,128)S(1)} %last.1.refs_0_), channel_id=1, source_target_pairs={{0,64},{1,65},{2,66},{3,67},{4,68},{5,69},{6,70},{7,71},{8,72},{9,... | collective-permute-start | bytes 786440 | tf_op jit(solution)/shard_map/ppermute | solution.py:62
  193.1 2.3 %collective-permute-done.39.refs_3_ = f32[16,4096]{1,0:T(8,128)S(1)} collective-permute-done((f32[16,4096]{1,0:T(8,128)S(1)}, f32[16,4096]{1,0:T(8,128)S(1)}, u32[]{:S(2)}, u32[]{:S(2)}) %collective-permute-start.39) | collective-permute-done | bytes 262176 | tf_op jit(solution)/shard_map/ppermute | solution.py:62
  195.4 3.5 %collective-permute-done.38.refs_2_ = f32[16,4096]{1,0:T(8,128)S(1)} collective-permute-done((f32[16,4096]{1,0:T(8,128)S(1)}, f32[16,4096]{1,0:T(8,128)S(1)}, u32[]{:S(2)}, u32[]{:S(2)}) %collective-permute-start.38) | collective-permute-done | bytes 262176 | tf_op jit(solution)/shard_map/ppermute | solution.py:62
  199.4 1.6 assemble.1
  (76 shorter events, 28.1 us)
Async XLA Ops:
  0.7 2.2 %copy-start = (bf16[1,512,4096]{2,1,0:T(8,128)(2,1)S(1)}, bf16[1,512,4096]{2,1,0:T(8,128)(2,1)}, u32[]{:S(2)}) copy-start(bf16[1,512,4096]{2,1,0:T(8,128)(2,1)} %param.11) | copy-start | bytes 12582916
  2.9 1.6 copy-start.2
  4.5 1.6 copy-start.4
  6.1 2.2 %copy-start.6 = (f32[1,512,2048]{2,1,0:T(8,128)S(1)}, f32[1,512,2048]{2,1,0:T(8,128)}, u32[]{:S(2)}) copy-start(f32[1,512,2048]{2,1,0:T(8,128)} %param.9) | copy-start | bytes 12582916
  16.5 2.0 collective-permute-start
  18.5 6.3 %copy-start.3 = (bf16[1,512,2048]{2,1,0:T(8,128)(2,1)S(1)}, bf16[1,512,2048]{2,1,0:T(8,128)(2,1)}, u32[]{:S(2)}) copy-start(bf16[1,512,2048]{2,1,0:T(8,128)(2,1)} %param.7) | copy-start | bytes 6291460
  18.5 6.3 %copy-start.5 = (bf16[1,512,2048]{2,1,0:T(8,128)(2,1)S(1)}, bf16[1,512,2048]{2,1,0:T(8,128)(2,1)}, u32[]{:S(2)}) copy-start(bf16[1,512,2048]{2,1,0:T(8,128)(2,1)} %param.6) | copy-start | bytes 6291460
  19.1 51.4 %collective-permute-start.12 = (f32[512,4096]{1,0:T(8,128)}, f32[512,4096]{1,0:T(8,128)S(1)}, u32[]{:S(2)}, u32[]{:S(2)}) collective-permute-start(f32[512,4096]{1,0:T(8,128)} %get-tuple-element.126), channel_id=1, source_target_pairs={{0,1},{1,0},{2,3},{3,2},{4,5},{5,4},{6,7},{7,6},{8,9},{9,8},{10,11... | collective-permute-start | bytes 25165832 | tf_op jit(solution)/shard_map/ppermute | solution.py:62
  19.4 12.1 %collective-permute-start.2 = (f32[4,72,128]{2,1,0:T(8,128)S(1)}, f32[4,72,128]{2,1,0:T(8,128)S(1)}, u32[]{:S(2)}, u32[]{:S(2)}) collective-permute-start(f32[4,72,128]{2,1,0:T(8,128)S(1)} %get-tuple-element.101), channel_id=1, source_target_pairs={{0,6},{1,7},{2,0},{3,1},{4,2},{5,3},{6,4},{7,5},{8,14},{9,15},{10,... | collective-permute-start | bytes 442376 | tf_op jit(solution)/shard_map/ppermute | solution.py:62
  23.5 8.3 %collective-permute-start.3 = (f32[4,72,128]{2,1,0:T(8,128)S(1)}, f32[4,72,128]{2,1,0:T(8,128)S(1)}, u32[]{:S(2)}, u32[]{:S(2)}) collective-permute-start(f32[4,72,128]{2,1,0:T(8,128)S(1)} %get-tuple-element.102), channel_id=1, source_target_pairs={{0,4},{1,5},{2,6},{3,7},{4,0},{5,1},{6,2},{7,3},{8,12},{9,13},{10,... | collective-permute-start | bytes 442376 | tf_op jit(solution)/shard_map/ppermute | solution.py:62
  23.5 10.2 %collective-permute-start.1 = (f32[4,72,128]{2,1,0:T(8,128)S(1)}, f32[4,72,128]{2,1,0:T(8,128)S(1)}, u32[]{:S(2)}, u32[]{:S(2)}) collective-permute-start(f32[4,72,128]{2,1,0:T(8,128)S(1)} %get-tuple-element.96.rest_0_), channel_id=1, source_target_pairs={{0,2},{1,3},{2,4},{3,5},{4,6},{5,7},{6,0},{7,1},{8,10},{9,11},{10,... | collective-permute-start | bytes 442376 | tf_op jit(solution)/shard_map/ppermute | solution.py:62
  34.3 9.8 %collective-permute-start.6 = (f32[4,72,128]{2,1,0:T(8,128)S(1)}, f32[4,72,128]{2,1,0:T(8,128)S(1)}, u32[]{:S(2)}, u32[]{:S(2)}) collective-permute-start(f32[4,72,128]{2,1,0:T(8,128)S(1)} %get-tuple-element.104.rest_3_.refs_2_), channel_id=1, source_target_pairs={{0,16},{1,17},{2,18},{3,19},{4,20},{5,21},{6,22},{7,23},{8,24},{9,... | collective-permute-start | bytes 442376 | tf_op jit(solution)/shard_map/ppermute | solution.py:62
  37.6 7.3 %collective-permute-start.5 = (f32[4,72,128]{2,1,0:T(8,128)S(1)}, f32[4,72,128]{2,1,0:T(8,128)S(1)}, u32[]{:S(2)}, u32[]{:S(2)}) collective-permute-start(f32[4,72,128]{2,1,0:T(8,128)S(1)} %get-tuple-element.104.rest_3_.refs_2_), channel_id=1, source_target_pairs={{0,24},{1,25},{2,26},{3,27},{4,28},{5,29},{6,30},{7,31},{8,0},{9,1... | collective-permute-start | bytes 442376 | tf_op jit(solution)/shard_map/ppermute | solution.py:62
  38.7 6.6 %collective-permute-start.4 = (f32[4,72,128]{2,1,0:T(8,128)S(1)}, f32[4,72,128]{2,1,0:T(8,128)S(1)}, u32[]{:S(2)}, u32[]{:S(2)}) collective-permute-start(f32[4,72,128]{2,1,0:T(8,128)S(1)} %get-tuple-element.104.rest_3_.refs_2_), channel_id=1, source_target_pairs={{0,8},{1,9},{2,10},{3,11},{4,12},{5,13},{6,14},{7,15},{8,16},{9,17... | collective-permute-start | bytes 442376 | tf_op jit(solution)/shard_map/ppermute | solution.py:62
  45.9 6.8 %collective-permute-start.8 = (f32[4,64,128]{2,1,0:T(8,128)S(1)}, f32[4,64,128]{2,1,0:T(8,128)S(1)}, u32[]{:S(2)}, u32[]{:S(2)}) collective-permute-start(f32[4,64,128]{2,1,0:T(8,128)S(1)} %get-tuple-element.115), channel_id=1, source_target_pairs={{0,6},{1,7},{2,0},{3,1},{4,2},{5,3},{6,4},{7,5},{8,14},{9,15},{10,... | collective-permute-start | bytes 393224 | tf_op jit(solution)/shard_map/ppermute | solution.py:62
  46.7 7.1 %collective-permute-start.9 = (f32[4,64,128]{2,1,0:T(8,128)S(1)}, f32[4,64,128]{2,1,0:T(8,128)S(1)}, u32[]{:S(2)}, u32[]{:S(2)}) collective-permute-start(f32[4,64,128]{2,1,0:T(8,128)S(1)} %get-tuple-element.116), channel_id=1, source_target_pairs={{0,4},{1,5},{2,6},{3,7},{4,0},{5,1},{6,2},{7,3},{8,12},{9,13},{10,... | collective-permute-start | bytes 393224 | tf_op jit(solution)/shard_map/ppermute | solution.py:62
  47.9 7.1 %collective-permute-start.7 = (f32[4,64,128]{2,1,0:T(8,128)S(1)}, f32[4,64,128]{2,1,0:T(8,128)S(1)}, u32[]{:S(2)}, u32[]{:S(2)}) collective-permute-start(f32[4,64,128]{2,1,0:T(8,128)S(1)} %get-tuple-element.110.rest_3_), channel_id=1, source_target_pairs={{0,2},{1,3},{2,4},{3,5},{4,6},{5,7},{6,0},{7,1},{8,10},{9,11},{10,... | collective-permute-start | bytes 393224 | tf_op jit(solution)/shard_map/ppermute | solution.py:62
  55.7 2.6 %collective-permute-start.10 = (f32[16,64,128]{2,1,0:T(8,128)S(1)}, f32[16,64,128]{2,1,0:T(8,128)S(1)}, u32[]{:S(2)}, u32[]{:S(2)}) collective-permute-start(f32[16,64,128]{2,1,0:T(8,128)S(1)} %get-tuple-element.118.rest_3_), channel_id=1, source_target_pairs={{0,1},{1,0},{2,3},{3,2},{4,5},{5,4},{6,7},{7,6},{8,9},{9,8},{10,11... | collective-permute-start | bytes 1572872 | tf_op jit(solution)/shard_map/ppermute | solution.py:62
  55.8 2.5 %copy-start.7 = (bf16[1,512,2048]{2,1,0:T(8,128)(2,1)S(1)}, bf16[1,512,2048]{2,1,0:T(8,128)(2,1)}, u32[]{:S(2)}) copy-start(bf16[1,512,2048]{2,1,0:T(8,128)(2,1)} %param.10) | copy-start | bytes 6291460
  58.3 12.2 %copy-start.1 = (bf16[1,512,4096]{2,1,0:T(8,128)(2,1)S(1)}, bf16[1,512,4096]{2,1,0:T(8,128)(2,1)}, u32[]{:S(2)}) copy-start(bf16[1,512,4096]{2,1,0:T(8,128)(2,1)} %param.11) | copy-start | bytes 12582916
  66.3 4.3 %collective-permute-start.11 = (f32[1024,512]{1,0:T(8,128)S(1)}, f32[1024,512]{1,0:T(8,128)S(1)}, u32[]{:S(2)}, u32[]{:S(2)}) collective-permute-start(f32[1024,512]{1,0:T(8,128)S(1)} %get-tuple-element.125), channel_id=1, source_target_pairs={{0,1},{1,0},{2,3},{3,2},{4,5},{5,4},{6,7},{7,6},{8,9},{9,8},{10,11... | collective-permute-start | bytes 6291464 | tf_op jit(solution)/shard_map/ppermute | solution.py:62
  77.2 16.1 %collective-permute-start.13 = (f32[256,1024]{1,0:T(8,128)S(1)}, f32[256,1024]{1,0:T(8,128)S(1)}, u32[]{:S(2)}, u32[]{:S(2)}) collective-permute-start(f32[256,1024]{1,0:T(8,128)S(1)} %get-tuple-element.133), channel_id=1, source_target_pairs={{0,32},{1,97},{2,34},{3,99},{4,36},{5,101},{6,38},{7,103},{8,40},{... | collective-permute-start | bytes 3145736 | tf_op jit(solution)/shard_map/ppermute | solution.py:62
  78.8 21.6 %collective-permute-start.16 = (f32[256,1536]{1,0:T(8,128)S(1)}, f32[256,1536]{1,0:T(8,128)S(1)}, u32[]{:S(2)}, u32[]{:S(2)}) collective-permute-start(f32[256,1536]{1,0:T(8,128)S(1)} %get-tuple-element.141), channel_id=1, source_target_pairs={{0,8},{1,25},{2,10},{3,27},{4,12},{5,29},{6,14},{7,31},{8,16},{9,1... | collective-permute-start | bytes 4718600 | tf_op jit(solution)/shard_map/ppermute | solution.py:62
  80.5 23.4 %collective-permute-start.15 = (f32[256,1536]{1,0:T(8,128)S(1)}, f32[256,1536]{1,0:T(8,128)S(1)}, u32[]{:S(2)}, u32[]{:S(2)}) collective-permute-start(f32[256,1536]{1,0:T(8,128)S(1)} %get-tuple-element.139), channel_id=1, source_target_pairs={{0,2},{1,7},{2,4},{3,1},{4,6},{5,3},{6,0},{7,5},{8,10},{9,15},{10,... | collective-permute-start | bytes 4718600 | tf_op jit(solution)/shard_map/ppermute | solution.py:62
  93.6 16.1 %collective-permute-start.14 = (f32[256,1024]{1,0:T(8,128)S(1)}, f32[256,1024]{1,0:T(8,128)S(1)}, u32[]{:S(2)}, u32[]{:S(2)}) collective-permute-start(f32[256,1024]{1,0:T(8,128)S(1)} %get-tuple-element.137), channel_id=1, source_target_pairs={{0,32},{1,97},{2,34},{3,99},{4,36},{5,101},{6,38},{7,103},{8,40},{... | collective-permute-start | bytes 3145736 | tf_op jit(solution)/shard_map/ppermute | solution.py:62
  94.2 33.9 %collective-permute-start.21 = (f32[256,1536]{1,0:T(8,128)S(1)}, f32[256,1536]{1,0:T(8,128)S(1)}, u32[]{:S(2)}, u32[]{:S(2)}) collective-permute-start(f32[256,1536]{1,0:T(8,128)S(1)} %get-tuple-element.151), channel_id=1, source_target_pairs={{0,6},{1,3},{2,0},{3,5},{4,2},{5,7},{6,4},{7,1},{8,14},{9,11},{10,... | collective-permute-start | bytes 4718600 | tf_op jit(solution)/shard_map/ppermute | solution.py:62
  97.4 30.7 %collective-permute-start.19 = (f32[256,1536]{1,0:T(8,128)S(1)}, f32[256,1536]{1,0:T(8,128)S(1)}, u32[]{:S(2)}, u32[]{:S(2)}) collective-permute-start(f32[256,1536]{1,0:T(8,128)S(1)} %get-tuple-element.148), channel_id=1, source_target_pairs={{0,24},{1,9},{2,26},{3,11},{4,28},{5,13},{6,30},{7,15},{8,0},{9,17... | collective-permute-start | bytes 4718600 | tf_op jit(solution)/shard_map/ppermute | solution.py:62
  104.4 31.4 %collective-permute-start.20 = (f32[256,1536]{1,0:T(8,128)S(1)}, f32[256,1536]{1,0:T(8,128)S(1)}, u32[]{:S(2)}, u32[]{:S(2)}) collective-permute-start(f32[256,1536]{1,0:T(8,128)S(1)} %get-tuple-element.150), channel_id=1, source_target_pairs={{0,2},{1,7},{2,4},{3,1},{4,6},{5,3},{6,0},{7,5},{8,10},{9,15},{10,... | collective-permute-start | bytes 4718600 | tf_op jit(solution)/shard_map/ppermute | solution.py:62
  104.5 31.3 %collective-permute-start.18 = (f32[256,1536]{1,0:T(8,128)S(1)}, f32[256,1536]{1,0:T(8,128)S(1)}, u32[]{:S(2)}, u32[]{:S(2)}) collective-permute-start(f32[256,1536]{1,0:T(8,128)S(1)} %get-tuple-element.147), channel_id=1, source_target_pairs={{0,8},{1,25},{2,10},{3,27},{4,12},{5,29},{6,14},{7,31},{8,16},{9,1... | collective-permute-start | bytes 4718600 | tf_op jit(solution)/shard_map/ppermute | solution.py:62
  110.7 17.5 %collective-permute-start.17 = (f32[256,1024]{1,0:T(8,128)S(1)}, f32[256,1024]{1,0:T(8,128)S(1)}, u32[]{:S(2)}, u32[]{:S(2)}) collective-permute-start(f32[256,1024]{1,0:T(8,128)S(1)} %get-tuple-element.145), channel_id=1, source_target_pairs={{0,32},{1,97},{2,34},{3,99},{4,36},{5,101},{6,38},{7,103},{8,40},{... | collective-permute-start | bytes 3145736 | tf_op jit(solution)/shard_map/ppermute | solution.py:62
  137.5 9.2 %collective-permute-start.23 = (f32[64,1536]{1,0:T(8,128)S(1)}, f32[64,1536]{1,0:T(8,128)S(1)}, u32[]{:S(2)}, u32[]{:S(2)}) collective-permute-start(f32[64,1536]{1,0:T(8,128)S(1)} %get-tuple-element.157), channel_id=1, source_target_pairs={{0,2},{1,7},{2,4},{3,1},{4,6},{5,3},{6,0},{7,5},{8,10},{9,15},{10,... | collective-permute-start | bytes 1179656 | tf_op jit(solution)/shard_map/ppermute | solution.py:62
  137.6 9.1 %collective-permute-start.24 = (f32[64,1536]{1,0:T(8,128)S(1)}, f32[64,1536]{1,0:T(8,128)S(1)}, u32[]{:S(2)}, u32[]{:S(2)}) collective-permute-start(f32[64,1536]{1,0:T(8,128)S(1)} %get-tuple-element.159), channel_id=1, source_target_pairs={{0,32},{1,97},{2,34},{3,99},{4,36},{5,101},{6,38},{7,103},{8,40},{... | collective-permute-start | bytes 1179656 | tf_op jit(solution)/shard_map/ppermute | solution.py:62
  139.2 7.6 %collective-permute-start.22 = (f32[64,1024]{1,0:T(8,128)S(1)}, f32[64,1024]{1,0:T(8,128)S(1)}, u32[]{:S(2)}, u32[]{:S(2)}) collective-permute-start(f32[64,1024]{1,0:T(8,128)S(1)} %get-tuple-element.155), channel_id=1, source_target_pairs={{0,8},{1,25},{2,10},{3,27},{4,12},{5,29},{6,14},{7,31},{8,16},{9,1... | collective-permute-start | bytes 786440 | tf_op jit(solution)/shard_map/ppermute | solution.py:62
  147.4 9.1 %collective-permute-start.26 = (f32[64,1536]{1,0:T(8,128)S(1)}, f32[64,1536]{1,0:T(8,128)S(1)}, u32[]{:S(2)}, u32[]{:S(2)}) collective-permute-start(f32[64,1536]{1,0:T(8,128)S(1)} %get-tuple-element.162), channel_id=1, source_target_pairs={{0,2},{1,7},{2,4},{3,1},{4,6},{5,3},{6,0},{7,5},{8,10},{9,15},{10,... | collective-permute-start | bytes 1179656 | tf_op jit(solution)/shard_map/ppermute | solution.py:62
  147.5 9.1 %collective-permute-start.27 = (f32[64,1536]{1,0:T(8,128)S(1)}, f32[64,1536]{1,0:T(8,128)S(1)}, u32[]{:S(2)}, u32[]{:S(2)}) collective-permute-start(f32[64,1536]{1,0:T(8,128)S(1)} %get-tuple-element.164), channel_id=1, source_target_pairs={{0,32},{1,97},{2,34},{3,99},{4,36},{5,101},{6,38},{7,103},{8,40},{... | collective-permute-start | bytes 1179656 | tf_op jit(solution)/shard_map/ppermute | solution.py:62
  148.9 7.6 %collective-permute-start.25 = (f32[64,1024]{1,0:T(8,128)S(1)}, f32[64,1024]{1,0:T(8,128)S(1)}, u32[]{:S(2)}, u32[]{:S(2)}) collective-permute-start(f32[64,1024]{1,0:T(8,128)S(1)} %get-tuple-element.160), channel_id=1, source_target_pairs={{0,8},{1,25},{2,10},{3,27},{4,12},{5,29},{6,14},{7,31},{8,16},{9,1... | collective-permute-start | bytes 786440 | tf_op jit(solution)/shard_map/ppermute | solution.py:62
  157.2 10.2 %collective-permute-start.29 = (f32[64,1536]{1,0:T(8,128)S(1)}, f32[64,1536]{1,0:T(8,128)S(1)}, u32[]{:S(2)}, u32[]{:S(2)}) collective-permute-start(f32[64,1536]{1,0:T(8,128)S(1)} %get-tuple-element.167), channel_id=1, source_target_pairs={{0,2},{1,7},{2,4},{3,1},{4,6},{5,3},{6,0},{7,5},{8,10},{9,15},{10,... | collective-permute-start | bytes 1179656 | tf_op jit(solution)/shard_map/ppermute | solution.py:62
  159.8 9.0 %collective-permute-start.30 = (f32[64,1536]{1,0:T(8,128)S(1)}, f32[64,1536]{1,0:T(8,128)S(1)}, u32[]{:S(2)}, u32[]{:S(2)}) collective-permute-start(f32[64,1536]{1,0:T(8,128)S(1)} %get-tuple-element.169), channel_id=1, source_target_pairs={{0,32},{1,97},{2,34},{3,99},{4,36},{5,101},{6,38},{7,103},{8,40},{... | collective-permute-start | bytes 1179656 | tf_op jit(solution)/shard_map/ppermute | solution.py:62
  159.8 7.6 %collective-permute-start.28 = (f32[64,1024]{1,0:T(8,128)S(1)}, f32[64,1024]{1,0:T(8,128)S(1)}, u32[]{:S(2)}, u32[]{:S(2)}) collective-permute-start(f32[64,1024]{1,0:T(8,128)S(1)} %get-tuple-element.165), channel_id=1, source_target_pairs={{0,8},{1,25},{2,10},{3,27},{4,12},{5,29},{6,14},{7,31},{8,16},{9,1... | collective-permute-start | bytes 786440 | tf_op jit(solution)/shard_map/ppermute | solution.py:62
  169.5 10.4 %collective-permute-start.32 = (f32[32,1536]{1,0:T(8,128)S(1)}, f32[32,1536]{1,0:T(8,128)S(1)}, u32[]{:S(2)}, u32[]{:S(2)}) collective-permute-start(f32[32,1536]{1,0:T(8,128)S(1)} %get-tuple-element.173), channel_id=1, source_target_pairs={{0,64},{1,65},{2,66},{3,67},{4,68},{5,69},{6,70},{7,71},{8,72},{9,... | collective-permute-start | bytes 589832 | tf_op jit(solution)/shard_map/ppermute | solution.py:58
  171.5 8.4 %collective-permute-start.33 = (f32[32,1536]{1,0:T(8,128)S(1)}, f32[32,1536]{1,0:T(8,128)S(1)}, u32[]{:S(2)}, u32[]{:S(2)}) collective-permute-start(f32[32,1536]{1,0:T(8,128)S(1)} %get-tuple-element.175), channel_id=1, source_target_pairs={{0,16},{1,17},{2,18},{3,19},{4,20},{5,21},{6,22},{7,23},{8,24},{9,... | collective-permute-start | bytes 589832 | tf_op jit(solution)/shard_map/ppermute | solution.py:58
  172.6 7.2 %collective-permute-start.31 = (f32[32,1024]{1,0:T(8,128)S(1)}, f32[32,1024]{1,0:T(8,128)S(1)}, u32[]{:S(2)}, u32[]{:S(2)}) collective-permute-start(f32[32,1024]{1,0:T(8,128)S(1)} %get-tuple-element.171), channel_id=1, source_target_pairs={{0,4},{1,5},{2,6},{3,7},{4,0},{5,1},{6,2},{7,3},{8,12},{9,13},{10,... | collective-permute-start | bytes 393224 | tf_op jit(solution)/shard_map/ppermute | solution.py:58
  180.5 6.3 %collective-permute-start.34 = (f32[16,1536]{1,0:T(8,128)S(1)}, f32[16,1536]{1,0:T(8,128)S(1)}, u32[]{:S(2)}, u32[]{:S(2)}) collective-permute-start(f32[16,1536]{1,0:T(8,128)S(1)} %get-tuple-element.177), channel_id=1, source_target_pairs={{0,32},{1,33},{2,34},{3,35},{4,36},{5,37},{6,38},{7,39},{8,40},{9,... | collective-permute-start | bytes 294920 | tf_op jit(solution)/shard_map/ppermute | solution.py:58
  180.9 5.9 %collective-permute-start.35 = (f32[16,1536]{1,0:T(8,128)S(1)}, f32[16,1536]{1,0:T(8,128)S(1)}, u32[]{:S(2)}, u32[]{:S(2)}) collective-permute-start(f32[16,1536]{1,0:T(8,128)S(1)} %get-tuple-element.179), channel_id=1, source_target_pairs={{0,8},{1,9},{2,10},{3,11},{4,12},{5,13},{6,14},{7,15},{8,0},{9,1},... | collective-permute-start | bytes 294920 | tf_op jit(solution)/shard_map/ppermute | solution.py:58
  180.9 5.8 %collective-permute-start.36 = (f32[16,1024]{1,0:T(8,128)S(1)}, f32[16,1024]{1,0:T(8,128)S(1)}, u32[]{:S(2)}, u32[]{:S(2)}) collective-permute-start(f32[16,1024]{1,0:T(8,128)S(1)} %get-tuple-element.181), channel_id=1, source_target_pairs={{0,2},{1,3},{2,0},{3,1},{4,6},{5,7},{6,4},{7,5},{8,10},{9,11},{10,... | collective-permute-start | bytes 196616 | tf_op jit(solution)/shard_map/ppermute | solution.py:58
  187.4 8.0 %collective-permute-start.39 = (f32[16,4096]{1,0:T(8,128)S(1)}, f32[16,4096]{1,0:T(8,128)S(1)}, u32[]{:S(2)}, u32[]{:S(2)}) collective-permute-start(f32[16,4096]{1,0:T(8,128)S(1)} %last.1.refs_0_), channel_id=1, source_target_pairs={{0,64},{1,65},{2,66},{3,67},{4,68},{5,69},{6,70},{7,71},{8,72},{9,... | collective-permute-start | bytes 786440 | tf_op jit(solution)/shard_map/ppermute | solution.py:62
  191.1 7.8 %collective-permute-start.38 = (f32[16,4096]{1,0:T(8,128)S(1)}, f32[16,4096]{1,0:T(8,128)S(1)}, u32[]{:S(2)}, u32[]{:S(2)}) collective-permute-start(f32[16,4096]{1,0:T(8,128)S(1)} %last.1.refs_0_), channel_id=1, source_target_pairs={{0,96},{1,97},{2,98},{3,99},{4,100},{5,101},{6,102},{7,103},{8,104... | collective-permute-start | bytes 786440 | tf_op jit(solution)/shard_map/ppermute | solution.py:62
  191.8 7.6 %collective-permute-start.37 = (f32[16,4096]{1,0:T(8,128)S(1)}, f32[16,4096]{1,0:T(8,128)S(1)}, u32[]{:S(2)}, u32[]{:S(2)}) collective-permute-start(f32[16,4096]{1,0:T(8,128)S(1)} %last.1.refs_0_), channel_id=1, source_target_pairs={{0,32},{1,33},{2,34},{3,35},{4,36},{5,37},{6,38},{7,39},{8,40},{9,... | collective-permute-start | bytes 786440 | tf_op jit(solution)/shard_map/ppermute | solution.py:62

commit v3 on v2

--- a/solution.py
+++ b/solution.py
@@ -490,7 +490,8 @@
     core = where_ref[3]
     total[...] = sum((ref[...] for ref in came), mine[...])
     for t in range(4):
-        j = lax.rem(where_ref[me] + jnp.where(core == 0, 7 - t, 1 + t), 4)
+        step = (OPPOSITE, BEFORE, AFTER, MINE)[t]
+        j = lax.rem(where_ref[me] + step(core), 4)
         if axis == "z":
             for y in range(4):
                 row = pl.multiple_of(64 * y + 16 * j, 16)
@@ -499,12 +500,14 @@
             outs[t][...] = total[pl.ds(pl.multiple_of(64 * j, 64), 64), :]
 
 
-def add_kernel(where_ref, a, b, out):
-    out[...] = a[...] + b[...]
-
-
-def halves_kernel(me, place, where_ref, a, b, keep, away, total):
-    total[...] = a[...] + b[...]
+def pass_kernel(where_ref, forth, came, *rest):
+    rest[-2][...] = forth[...] + came[...]
+    rest[-1][...] = sum((ref[...] for ref in rest[1:-2]), rest[0][...])
+
+
+def halves_kernel(me, place, where_ref, a, *rest):
+    came, (keep, away, total) = rest[:-3], rest[-3:]
+    total[...] = sum((ref[...] for ref in came), a[...])
     rows = keep.shape[0]
     row = rows * place(where_ref[me])
     keep[...] = total[pl.ds(pl.multiple_of(row, rows), rows), :]
@@ -592,20 +595,26 @@
         [[(256, width[a])] for a in order],
         "second",
     )
-    held = [part[0] for part in parts]
-    for step in (1, 2):
-        came = [send(h, following[a][0], forward) for h, a in zip(held, order)]
-        held = together(
-            [add_kernel] * 3,
-            where,
-            [[part[step], c] for part, c in zip(parts, came)],
-            [[(64, width[a])] for a in order],
-            [[]] * 3,
-            "add",
-        )
-        held = [h[0] for h in held]
-    came = [send(h, following[a][0], forward) for h, a in zip(held, order)]
-    pairs = [[part[3], c] for part, c in zip(parts, came)]
+    parts = dict(zip(order, parts))
+    came = {a: send(parts[a][0], following[a][0], forward) for a in ("y", "z", "x")}
+    straight = {a: [send(parts[a][1], following[a][0], backward)] for a in ("y", "z")}
+    passed = together(
+        [pass_kernel] * 3,
+        where,
+        [
+            [parts[a][2], came[a]] + ([parts[a][3]] + straight[a] if a != "x" else [parts[a][1]])
+            for a in order
+        ],
+        [[(64, width[a])] * 2 for a in order],
+        [[]] * 3,
+        "pass_on",
+    )
+    pairs = []
+    for (forth, mine), a in zip(passed, order):
+        arrived = [send(forth, following[a][0], forward)]
+        if a == "x":
+            mine, arrived = parts[a][3], arrived + [send(mine, following[a][0], backward)]
+        pairs.append([mine] + arrived)
     upper, odd = (lambda p: lax.div(p, 2)), (lambda p: lax.rem(p, 2))
     for rows, distance, place_of in ((32, 2, upper), (16, 1, odd)):
         pairs = together(

time: 201 us -> 197 us (0.980)
    ppermute x34, waiting for transfers between devices: 72.2 us -> 66.6 us  [send(): return lax.ppermute(array, AXES, shift_pairs(axis, by))]
    ppermute x6, waiting for transfers between devices: 5.26 us -> 9.37 us  [swap(): return lax.ppermute(array, AXES, pairs)]
    ppermute x6, starting transfers between devices: 11.4 us -> 7.74 us  [swap(): return lax.ppermute(array, AXES, pairs)]
    pallas_call x9 -> x8, Pallas kernels: 6.92 us -> 6.39 us  [small_call(): pl.pallas_call(body, in_specs=[pl.BlockSpec(memory_space=pltpu.SMEM)] + w...]
  transfers between devices with their start and end apart: 40 -> 40, of which waited for: 24 -> 23; matrix products, arithmetic and copies ran while one was open for 0% -> 0% of each run, Pallas kernels for 21% -> 21%
where the time goes in v3:
time: 197 us
  waiting for transfers between devices  76 us (39%)
  Pallas kernels  63.6 us (32%)
  starting transfers between devices  48.9 us (25%)
  local copies, waits for them, and re-layouts  7.58 us (4%)
    ppermute x34, waiting for transfers between devices, send(): return lax.ppermute(array, AXES, shift_pairs(axis, by))  66.6 us
    ppermute x34, starting transfers between devices, send(): return lax.ppermute(array, AXES, shift_pairs(axis, by))  41.2 us
    pallas_call x6, Pallas kernels, products(): pl.pallas_call(functools.partial(product_kernel, axis, steps), grid_spec=...  18.3 us
    pallas_call x4, Pallas kernels, local_core(): pl.pallas_call(core_kernel, grid=(steps,), in_specs=[spec] * 4 + [pl.Bloc...  18.1 us
    ppermute x6, waiting for transfers between devices, swap(): return lax.ppermute(array, AXES, pairs)  9.37 us
    pallas_call x1, Pallas kernels, local_state(): pl.pallas_call(state_kernel, grid_spec=pltpu.PrefetchScalarGridSpec(num_s...  8.18 us
    pallas_call x1, Pallas kernels, gated(): pl.pallas_call(hidden_kernel, grid_spec=pltpu.PrefetchScalarGridSpec(num_...  7.96 us
    ppermute x6, starting transfers between devices, swap(): return lax.ppermute(array, AXES, pairs)  7.74 us
  transfers between devices with their start and end apart: 40, of which 23 were waited for; matrix products, arithmetic and copies ran while one was open for 0% of the time, Pallas kernels for 21%

profile of v3, /device:TPU:0, one launch (start us, length us, event | category | flops | bytes accessed | tf_op | source)
XLA Modules:
  0.0 197.0 jit_solution(1820340376038423489)
XLA Ops:
  0.7 2.2 %copy-done = bf16[1,512,4096]{2,1,0:T(8,128)(2,1)S(1)} copy-done((bf16[1,512,4096]{2,1,0:T(8,128)(2,1)S(1)}, bf16[1,512,4096]{2,1,0:T(8,128)(2,1)}, u32[]{:S(2)}) %copy-start) | copy-done | bytes 4194328
  2.9 1.6 copy-done.2
  4.5 1.6 copy-done.4
  6.1 2.2 %copy-done.6 = f32[1,512,2048]{2,1,0:T(8,128)S(1)} copy-done((f32[1,512,2048]{2,1,0:T(8,128)S(1)}, f32[1,512,2048]{2,1,0:T(8,128)}, u32[]{:S(2)}) %copy-start.6) | copy-done | bytes 4194328
  8.3 8.2 %local_state.1 = (f32[16,72,128]{2,1,0:T(8,128)S(1)}, f32[16,72,128]{2,1,0:T(8,128)S(1)}, f32[512,2048]{1,0:T(8,128)S(1)}, f32[512,4096]{1,0:T(8,128)}) custom-call(s32[4]{0:T(128)S(1)} %pad_add_fusion.where_ref.refs_0_, bf16[512,2048]{1,0:T(8,128)(2,1)S(1)} %bitcast.26, bf16[512,2048]{1,0:T(8,128)(2,1)S(1)} %bitcast.31, f32[512,2048]{1,0:T(8,128)S(1)} %bitcast.46, ...), custom_call_target="tpu_custom_call" | custom-call | flops 268435456 | bytes 26000000 | tf_op jit(solution)/shard_map/local_state/pallas_call | solution.py:147
  16.5 2.0 %collective-permute-done.got_ref.refs_2_ = f32[16,72,128]{2,1,0:T(8,128)S(1)} collective-permute-done((f32[16,72,128]{2,1,0:T(8,128)S(1)}, f32[16,72,128]{2,1,0:T(8,128)S(1)}, u32[]{:S(2)}, u32[]{:S(2)}) %collective-permute-start) | collective-permute-done | bytes 589856 | tf_op jit(solution)/shard_map/ppermute | solution.py:62
  19.3 4.1 %collective-permute-start.2 = (f32[4,72,128]{2,1,0:T(8,128)S(1)}, f32[4,72,128]{2,1,0:T(8,128)S(1)}, u32[]{:S(2)}, u32[]{:S(2)}) collective-permute-start(f32[4,72,128]{2,1,0:T(8,128)S(1)} %get-tuple-element.101), channel_id=1, source_target_pairs={{0,6},{1,7},{2,0},{3,1},{4,2},{5,3},{6,4},{7,5},{8,14},{9,15},{10,... | collective-permute-start | bytes 442376 | tf_op jit(solution)/shard_map/ppermute | solution.py:62
  24.7 6.7 %local_core.4 = (f32[512,2048]{1,0:T(8,128)S(1)}, bf16[512,2048]{1,0:T(8,128)(2,1)S(1)}, bf16[512,2048]{1,0:T(8,128)(2,1)S(1)}, f32[8,128]{1,0:T(8,128)S(1)}) custom-call(bf16[512,2048]{1,0:T(8,128)(2,1)S(1)} %bitcast.42, bf16[512,2048]{1,0:T(8,128)(2,1)S(1)} %bitcast.27, bf16[512,2048]{1,0:T(8,128)(2,1)S(1)} %bitcast.32, ...), custom_call_target="tpu_custom_call" | custom-call | flops 536870912 | bytes 20000000 | tf_op jit(solution)/shard_map/local_core/pallas_call | solution.py:214
  31.7 2.0 collective-permute-done.1.refs_2_
  34.3 3.3 %collective-permute-start.6 = (f32[4,72,128]{2,1,0:T(8,128)S(1)}, f32[4,72,128]{2,1,0:T(8,128)S(1)}, u32[]{:S(2)}, u32[]{:S(2)}) collective-permute-start(f32[4,72,128]{2,1,0:T(8,128)S(1)} %get-tuple-element.104.rest_3_.refs_2_), channel_id=1, source_target_pairs={{0,16},{1,17},{2,18},{3,19},{4,20},{5,21},{6,22},{7,23},{8,24},{9,... | collective-permute-start | bytes 442376 | tf_op jit(solution)/shard_map/ppermute | solution.py:62
  39.6 4.5 %local_core.5 = (f32[512,2048]{1,0:T(8,128)S(1)}, bf16[512,2048]{1,0:T(8,128)(2,1)S(1)}, bf16[512,2048]{1,0:T(8,128)(2,1)S(1)}, f32[8,128]{1,0:T(8,128)S(1)}) custom-call(bf16[512,2048]{1,0:T(8,128)(2,1)S(1)} %bitcast.43, bf16[512,2048]{1,0:T(8,128)(2,1)S(1)} %bitcast.28, ...), custom_call_target="tpu_custom_call", output_to_operand_aliasing={{0}: (4, {}), {1}: (5, {}), {2}: (6, {})} | custom-call | flops 536870912 | bytes 20000000 | tf_op jit(solution)/shard_map/local_core/pallas_call | solution.py:214
  48.2 4.5 %local_core.6 = (f32[512,2048]{1,0:T(8,128)S(1)}, bf16[512,2048]{1,0:T(8,128)(2,1)S(1)}, bf16[512,2048]{1,0:T(8,128)(2,1)S(1)}, f32[8,128]{1,0:T(8,128)S(1)}) custom-call(bf16[512,2048]{1,0:T(8,128)(2,1)S(1)} %bitcast.44, bf16[512,2048]{1,0:T(8,128)(2,1)S(1)} %bitcast.29, ...), custom_call_target="tpu_custom_call", output_to_operand_aliasing={{0}: (4, {}), {1}: (5, {}), {2}: (6, {})} | custom-call | flops 536870912 | bytes 20000000 | tf_op jit(solution)/shard_map/local_core/pallas_call | solution.py:214
  55.8 2.5 %local_core.7 = (f32[512,2048]{1,0:T(8,128)S(1)}, bf16[512,2048]{1,0:T(8,128)(2,1)S(1)}, bf16[512,2048]{1,0:T(8,128)(2,1)S(1)}, f32[8,128]{1,0:T(8,128)}) custom-call(bf16[512,2048]{1,0:T(8,128)(2,1)S(1)} %bitcast.45, bf16[512,2048]{1,0:T(8,128)(2,1)S(1)} %bitcast.30, ...), custom_call_target="tpu_custom_call", output_to_operand_aliasing={{0}: (4, {}), {1}: (5, {}), {2}: (6, {})} | custom-call | flops 536870912 | bytes 20000000 | tf_op jit(solution)/shard_map/local_core/pallas_call | solution.py:214
  58.3 8.0 %gated_hidden.1 = (bf16[512,2048]{1,0:T(8,128)(2,1)}, bf16[1024,512]{1,0:T(8,128)(2,1)S(1)}, f32[1024,512]{1,0:T(8,128)S(1)}) custom-call(s32[4]{0:T(128)S(1)} %pad_add_fusion.where_ref.refs_0_, f32[512,2048]{1,0:T(8,128)S(1)} %get-tuple-element.119.out_ref, bf16[512,2048]{1,0:T(8,128)(2,1)S(1)} %get-tuple-element.120.high_ref, ...), custom_call_target="tpu_custom_call" | custom-call | flops 805306368 | bytes 17000000 | tf_op jit(solution)/shard_map/gated_hidden/pallas_call | solution.py:380
  66.7 3.8 %collective-permute-done.11 = f32[1024,512]{1,0:T(8,128)S(1)} collective-permute-done((f32[1024,512]{1,0:T(8,128)S(1)}, f32[1024,512]{1,0:T(8,128)S(1)}, u32[]{:S(2)}, u32[]{:S(2)}) %collective-permute-start.11) | collective-permute-done | bytes 2097184 | tf_op jit(solution)/shard_map/ppermute | solution.py:62
  70.5 2.4 %products_y.2 = (f32[256,1536]{1,0:T(8,128)S(1)}, f32[8,128]{1,0:T(8,128)S(1)}) custom-call(s32[4]{0:T(128)S(1)} %pad_add_fusion.where_ref.refs_0_, bf16[4,4,4,16,512]{4,3,2,1,0:T(8,128)(2,1)S(1)} %bitcast.36, f32[4,4,4,16,512]{4,3,2,1,0:T(8,128)S(1)} %bitcast.20, bf16[512,4096]{1,0:T(8,128)(2,1)S(1)} %bitcast.14, ...), custom_call_target="tpu_custom_call" | custom-call | flops 1000000 | bytes 1000000 | tf_op jit(solution)/shard_map/products_y/pallas_call | solution.py:441
  72.9 2.4 %products_z.2 = (f32[256,1536]{1,0:T(8,128)S(1)}, f32[8,128]{1,0:T(8,128)S(1)}) custom-call(s32[4]{0:T(128)S(1)} %pad_add_fusion.where_ref.refs_0_, bf16[4,4,4,16,512]{4,3,2,1,0:T(8,128)(2,1)S(1)} %bitcast.37, f32[4,4,4,16,512]{4,3,2,1,0:T(8,128)S(1)} %bitcast.21, bf16[512,4096]{1,0:T(8,128)(2,1)S(1)} %bitcast.15, ...), custom_call_target="tpu_custom_call" | custom-call | flops 1000000 | bytes 1000000 | tf_op jit(solution)/shard_map/products_z/pallas_call | solution.py:441
  75.3 1.8 products_x.2
  77.2 1.6 collective-permute-start.13
  78.7 1.8 collective-permute-start.16
  80.5 3.1 %products_x.3 = (f32[256,1024]{1,0:T(8,128)S(1)}, f32[256,1024]{1,0:T(8,128)S(1)}, f32[256,1024]{1,0:T(8,128)S(1)}, f32[8,128]{1,0:T(8,128)S(1)}) custom-call(s32[4]{0:T(128)S(1)} %pad_add_fusion.where_ref.refs_0_, bf16[4,4,4,16,512]{4,3,2,1,0:T(8,128)(2,1)S(1)} %bitcast.39, f32[4,4,4,16,512]{4,3,2,1,0:T(8,128)S(1)} %bitcast.23, ...), custom_call_target="tpu_custom_call" | custom-call | flops 1000000 | bytes 1000000 | tf_op jit(solution)/shard_map/products_x/pallas_call | solution.py:441
  83.6 4.3 %products_y.3 = (f32[256,1536]{1,0:T(8,128)S(1)}, f32[256,1536]{1,0:T(8,128)S(1)}, f32[256,1536]{1,0:T(8,128)S(1)}, f32[8,128]{1,0:T(8,128)S(1)}) custom-call(s32[4]{0:T(128)S(1)} %pad_add_fusion.where_ref.refs_0_, bf16[4,4,4,16,512]{4,3,2,1,0:T(8,128)(2,1)S(1)} %bitcast.40, f32[4,4,4,16,512]{4,3,2,1,0:T(8,128)S(1)} %bitcast.24, ...), custom_call_target="tpu_custom_call" | custom-call | flops 1000000 | bytes 1000000 | tf_op jit(solution)/shard_map/products_y/pallas_call | solution.py:441
  87.9 4.3 %products_z.3 = (f32[256,1536]{1,0:T(8,128)S(1)}, f32[256,1536]{1,0:T(8,128)S(1)}, f32[256,1536]{1,0:T(8,128)S(1)}, f32[8,128]{1,0:T(8,128)S(1)}) custom-call(s32[4]{0:T(128)S(1)} %pad_add_fusion.where_ref.refs_0_, bf16[4,4,4,16,512]{4,3,2,1,0:T(8,128)(2,1)S(1)} %bitcast.41, f32[4,4,4,16,512]{4,3,2,1,0:T(8,128)S(1)} %bitcast.25, ...), custom_call_target="tpu_custom_call" | custom-call | flops 1000000 | bytes 1000000 | tf_op jit(solution)/shard_map/products_z/pallas_call | solution.py:441
  94.2 3.2 %collective-permute-start.21 = (f32[256,1536]{1,0:T(8,128)S(1)}, f32[256,1536]{1,0:T(8,128)S(1)}, u32[]{:S(2)}, u32[]{:S(2)}) collective-permute-start(f32[256,1536]{1,0:T(8,128)S(1)} %get-tuple-element.151), channel_id=1, source_target_pairs={{0,6},{1,3},{2,0},{3,5},{4,2},{5,7},{6,4},{7,1},{8,14},{9,11},{10,... | collective-permute-start | bytes 4718600 | tf_op jit(solution)/shard_map/ppermute | solution.py:62
  97.4 1.5 collective-permute-start.19
  98.9 1.5 collective-permute-done.16.b
  100.9 3.0 %collective-permute-done.15.b = f32[256,1536]{1,0:T(8,128)S(1)} collective-permute-done((f32[256,1536]{1,0:T(8,128)S(1)}, f32[256,1536]{1,0:T(8,128)S(1)}, u32[]{:S(2)}, u32[]{:S(2)}) %collective-permute-start.15) | collective-permute-done | bytes 1572896 | tf_op jit(solution)/shard_map/ppermute | solution.py:62
  104.5 1.9 collective-permute-start.18
  106.4 3.3 %collective-permute-done.14.b = f32[256,1024]{1,0:T(8,128)S(1)} collective-permute-done((f32[256,1024]{1,0:T(8,128)S(1)}, f32[256,1024]{1,0:T(8,128)S(1)}, u32[]{:S(2)}, u32[]{:S(2)}) %collective-permute-start.14) | collective-permute-done | bytes 1048608 | tf_op jit(solution)/shard_map/ppermute | solution.py:62
  111.2 16.9 %collective-permute-done.21.refs_8_ = f32[256,1536]{1,0:T(8,128)S(1)} collective-permute-done((f32[256,1536]{1,0:T(8,128)S(1)}, f32[256,1536]{1,0:T(8,128)S(1)}, u32[]{:S(2)}, u32[]{:S(2)}) %collective-permute-start.21) | collective-permute-done | bytes 1572896 | tf_op jit(solution)/shard_map/ppermute | solution.py:62
  128.1 7.7 %collective-permute-done.20.refs_7_ = f32[256,1536]{1,0:T(8,128)S(1)} collective-permute-done((f32[256,1536]{1,0:T(8,128)S(1)}, f32[256,1536]{1,0:T(8,128)S(1)}, u32[]{:S(2)}, u32[]{:S(2)}) %collective-permute-start.20) | collective-permute-done | bytes 1572896 | tf_op jit(solution)/shard_map/ppermute | solution.py:62
  135.8 1.7 second.1
  137.6 3.2 %collective-permute-start.24 = (f32[64,1536]{1,0:T(8,128)S(1)}, f32[64,1536]{1,0:T(8,128)S(1)}, u32[]{:S(2)}, u32[]{:S(2)}) collective-permute-start(f32[64,1536]{1,0:T(8,128)S(1)} %get-tuple-element.159), channel_id=1, source_target_pairs={{0,6},{1,3},{2,0},{3,5},{4,2},{5,7},{6,4},{7,1},{8,14},{9,11},{10,... | collective-permute-start | bytes 1179656 | tf_op jit(solution)/shard_map/ppermute | solution.py:62
  140.8 1.5 collective-permute-start.25
  142.3 1.8 collective-permute-start.26
  145.4 6.2 %collective-permute-done.22.refs_2_ = f32[64,1024]{1,0:T(8,128)S(1)} collective-permute-done((f32[64,1024]{1,0:T(8,128)S(1)}, f32[64,1024]{1,0:T(8,128)S(1)}, u32[]{:S(2)}, u32[]{:S(2)}) %collective-permute-start.22) | collective-permute-done | bytes 262176 | tf_op jit(solution)/shard_map/ppermute | solution.py:62
  154.3 2.6 %collective-permute-start.28 = (f32[64,1024]{1,0:T(8,128)S(1)}, f32[64,1024]{1,0:T(8,128)S(1)}, u32[]{:S(2)}, u32[]{:S(2)}) collective-permute-start(f32[64,1024]{1,0:T(8,128)S(1)} %get-tuple-element.165), channel_id=1, source_target_pairs={{0,24},{1,9},{2,26},{3,11},{4,28},{5,13},{6,30},{7,15},{8,0},{9,17... | collective-permute-start | bytes 786440 | tf_op jit(solution)/shard_map/ppermute | solution.py:62
  156.9 6.2 %collective-permute-done.27.refs_2_ = f32[64,1024]{1,0:T(8,128)S(1)} collective-permute-done((f32[64,1024]{1,0:T(8,128)S(1)}, f32[64,1024]{1,0:T(8,128)S(1)}, u32[]{:S(2)}, u32[]{:S(2)}) %collective-permute-start.27) | collective-permute-done | bytes 262176 | tf_op jit(solution)/shard_map/ppermute | solution.py:62
  163.9 1.8 collective-permute-start.32
  165.7 1.8 collective-permute-start.33
  167.5 1.8 collective-permute-start.31
  169.3 4.7 %collective-permute-done.31.refs_2_ = f32[32,1024]{1,0:T(8,128)S(1)} collective-permute-done((f32[32,1024]{1,0:T(8,128)S(1)}, f32[32,1024]{1,0:T(8,128)S(1)}, u32[]{:S(2)}, u32[]{:S(2)}) %collective-permute-start.31) | collective-permute-done | bytes 131104 | tf_op jit(solution)/shard_map/ppermute | solution.py:58
  175.7 1.7 collective-permute-start.35
  177.7 4.0 %collective-permute-done.36.refs_6_ = f32[16,1024]{1,0:T(8,128)S(1)} collective-permute-done((f32[16,1024]{1,0:T(8,128)S(1)}, f32[16,1024]{1,0:T(8,128)S(1)}, u32[]{:S(2)}, u32[]{:S(2)}) %collective-permute-start.36) | collective-permute-done | bytes 65568 | tf_op jit(solution)/shard_map/ppermute | solution.py:58
  182.3 2.7 %collective-permute-start.39 = (f32[16,4096]{1,0:T(8,128)S(1)}, f32[16,4096]{1,0:T(8,128)S(1)}, u32[]{:S(2)}, u32[]{:S(2)}) collective-permute-start(f32[16,4096]{1,0:T(8,128)S(1)} %last.1.refs_0_), channel_id=1, source_target_pairs={{0,64},{1,65},{2,66},{3,67},{4,68},{5,69},{6,70},{7,71},{8,72},{9,... | collective-permute-start | bytes 786440 | tf_op jit(solution)/shard_map/ppermute | solution.py:62
  187.0 5.1 %collective-permute-done.39.refs_3_ = f32[16,4096]{1,0:T(8,128)S(1)} collective-permute-done((f32[16,4096]{1,0:T(8,128)S(1)}, f32[16,4096]{1,0:T(8,128)S(1)}, u32[]{:S(2)}, u32[]{:S(2)}) %collective-permute-start.39) | collective-permute-done | bytes 262176 | tf_op jit(solution)/shard_map/ppermute | solution.py:62
  192.1 2.0 collective-permute-done.38.refs_2_
  195.4 1.6 assemble.1
  (75 shorter events, 28.2 us)
Async XLA Ops:
  0.7 2.2 %copy-start = (bf16[1,512,4096]{2,1,0:T(8,128)(2,1)S(1)}, bf16[1,512,4096]{2,1,0:T(8,128)(2,1)}, u32[]{:S(2)}) copy-start(bf16[1,512,4096]{2,1,0:T(8,128)(2,1)} %param.11) | copy-start | bytes 12582916
  2.9 1.6 copy-start.2
  4.5 1.6 copy-start.4
  6.1 2.2 %copy-start.6 = (f32[1,512,2048]{2,1,0:T(8,128)S(1)}, f32[1,512,2048]{2,1,0:T(8,128)}, u32[]{:S(2)}) copy-start(f32[1,512,2048]{2,1,0:T(8,128)} %param.9) | copy-start | bytes 12582916
  16.5 2.0 %collective-permute-start = (f32[16,72,128]{2,1,0:T(8,128)S(1)}, f32[16,72,128]{2,1,0:T(8,128)S(1)}, u32[]{:S(2)}, u32[]{:S(2)}) collective-permute-start(f32[16,72,128]{2,1,0:T(8,128)S(1)} %get-tuple-element.94), channel_id=1, source_target_pairs={{0,1},{1,0},{2,3},{3,2},{4,5},{5,4},{6,7},{7,6},{8,9},{9,8},{10,11... | collective-permute-start | bytes 1769480 | tf_op jit(solution)/shard_map/ppermute | solution.py:62
  18.5 6.3 %copy-start.3 = (bf16[1,512,2048]{2,1,0:T(8,128)(2,1)S(1)}, bf16[1,512,2048]{2,1,0:T(8,128)(2,1)}, u32[]{:S(2)}) copy-start(bf16[1,512,2048]{2,1,0:T(8,128)(2,1)} %param.7) | copy-start | bytes 6291460
  18.5 6.3 %copy-start.5 = (bf16[1,512,2048]{2,1,0:T(8,128)(2,1)S(1)}, bf16[1,512,2048]{2,1,0:T(8,128)(2,1)}, u32[]{:S(2)}) copy-start(bf16[1,512,2048]{2,1,0:T(8,128)(2,1)} %param.6) | copy-start | bytes 6291460
  19.1 51.4 %collective-permute-start.12 = (f32[512,4096]{1,0:T(8,128)}, f32[512,4096]{1,0:T(8,128)S(1)}, u32[]{:S(2)}, u32[]{:S(2)}) collective-permute-start(f32[512,4096]{1,0:T(8,128)} %get-tuple-element.126), channel_id=1, source_target_pairs={{0,1},{1,0},{2,3},{3,2},{4,5},{5,4},{6,7},{7,6},{8,9},{9,8},{10,11... | collective-permute-start | bytes 25165832 | tf_op jit(solution)/shard_map/ppermute | solution.py:62
  19.3 12.1 %collective-permute-start.2 = (f32[4,72,128]{2,1,0:T(8,128)S(1)}, f32[4,72,128]{2,1,0:T(8,128)S(1)}, u32[]{:S(2)}, u32[]{:S(2)}) collective-permute-start(f32[4,72,128]{2,1,0:T(8,128)S(1)} %get-tuple-element.101), channel_id=1, source_target_pairs={{0,6},{1,7},{2,0},{3,1},{4,2},{5,3},{6,4},{7,5},{8,14},{9,15},{10,... | collective-permute-start | bytes 442376 | tf_op jit(solution)/shard_map/ppermute | solution.py:62
  23.5 8.3 %collective-permute-start.3 = (f32[4,72,128]{2,1,0:T(8,128)S(1)}, f32[4,72,128]{2,1,0:T(8,128)S(1)}, u32[]{:S(2)}, u32[]{:S(2)}) collective-permute-start(f32[4,72,128]{2,1,0:T(8,128)S(1)} %get-tuple-element.102), channel_id=1, source_target_pairs={{0,4},{1,5},{2,6},{3,7},{4,0},{5,1},{6,2},{7,3},{8,12},{9,13},{10,... | collective-permute-start | bytes 442376 | tf_op jit(solution)/shard_map/ppermute | solution.py:62
  23.5 10.2 %collective-permute-start.1 = (f32[4,72,128]{2,1,0:T(8,128)S(1)}, f32[4,72,128]{2,1,0:T(8,128)S(1)}, u32[]{:S(2)}, u32[]{:S(2)}) collective-permute-start(f32[4,72,128]{2,1,0:T(8,128)S(1)} %get-tuple-element.96.rest_0_), channel_id=1, source_target_pairs={{0,2},{1,3},{2,4},{3,5},{4,6},{5,7},{6,0},{7,1},{8,10},{9,11},{10,... | collective-permute-start | bytes 442376 | tf_op jit(solution)/shard_map/ppermute | solution.py:62
  34.3 9.8 %collective-permute-start.6 = (f32[4,72,128]{2,1,0:T(8,128)S(1)}, f32[4,72,128]{2,1,0:T(8,128)S(1)}, u32[]{:S(2)}, u32[]{:S(2)}) collective-permute-start(f32[4,72,128]{2,1,0:T(8,128)S(1)} %get-tuple-element.104.rest_3_.refs_2_), channel_id=1, source_target_pairs={{0,16},{1,17},{2,18},{3,19},{4,20},{5,21},{6,22},{7,23},{8,24},{9,... | collective-permute-start | bytes 442376 | tf_op jit(solution)/shard_map/ppermute | solution.py:62
  37.6 7.3 %collective-permute-start.5 = (f32[4,72,128]{2,1,0:T(8,128)S(1)}, f32[4,72,128]{2,1,0:T(8,128)S(1)}, u32[]{:S(2)}, u32[]{:S(2)}) collective-permute-start(f32[4,72,128]{2,1,0:T(8,128)S(1)} %get-tuple-element.104.rest_3_.refs_2_), channel_id=1, source_target_pairs={{0,24},{1,25},{2,26},{3,27},{4,28},{5,29},{6,30},{7,31},{8,0},{9,1... | collective-permute-start | bytes 442376 | tf_op jit(solution)/shard_map/ppermute | solution.py:62
  38.6 6.6 %collective-permute-start.4 = (f32[4,72,128]{2,1,0:T(8,128)S(1)}, f32[4,72,128]{2,1,0:T(8,128)S(1)}, u32[]{:S(2)}, u32[]{:S(2)}) collective-permute-start(f32[4,72,128]{2,1,0:T(8,128)S(1)} %get-tuple-element.104.rest_3_.refs_2_), channel_id=1, source_target_pairs={{0,8},{1,9},{2,10},{3,11},{4,12},{5,13},{6,14},{7,15},{8,16},{9,17... | collective-permute-start | bytes 442376 | tf_op jit(solution)/shard_map/ppermute | solution.py:62
  45.9 6.8 %collective-permute-start.8 = (f32[4,64,128]{2,1,0:T(8,128)S(1)}, f32[4,64,128]{2,1,0:T(8,128)S(1)}, u32[]{:S(2)}, u32[]{:S(2)}) collective-permute-start(f32[4,64,128]{2,1,0:T(8,128)S(1)} %get-tuple-element.115), channel_id=1, source_target_pairs={{0,6},{1,7},{2,0},{3,1},{4,2},{5,3},{6,4},{7,5},{8,14},{9,15},{10,... | collective-permute-start | bytes 393224 | tf_op jit(solution)/shard_map/ppermute | solution.py:62
  46.7 7.1 %collective-permute-start.9 = (f32[4,64,128]{2,1,0:T(8,128)S(1)}, f32[4,64,128]{2,1,0:T(8,128)S(1)}, u32[]{:S(2)}, u32[]{:S(2)}) collective-permute-start(f32[4,64,128]{2,1,0:T(8,128)S(1)} %get-tuple-element.116), channel_id=1, source_target_pairs={{0,4},{1,5},{2,6},{3,7},{4,0},{5,1},{6,2},{7,3},{8,12},{9,13},{10,... | collective-permute-start | bytes 393224 | tf_op jit(solution)/shard_map/ppermute | solution.py:62
  47.9 7.1 %collective-permute-start.7 = (f32[4,64,128]{2,1,0:T(8,128)S(1)}, f32[4,64,128]{2,1,0:T(8,128)S(1)}, u32[]{:S(2)}, u32[]{:S(2)}) collective-permute-start(f32[4,64,128]{2,1,0:T(8,128)S(1)} %get-tuple-element.110.rest_3_), channel_id=1, source_target_pairs={{0,2},{1,3},{2,4},{3,5},{4,6},{5,7},{6,0},{7,1},{8,10},{9,11},{10,... | collective-permute-start | bytes 393224 | tf_op jit(solution)/shard_map/ppermute | solution.py:62
  55.7 2.6 %collective-permute-start.10 = (f32[16,64,128]{2,1,0:T(8,128)S(1)}, f32[16,64,128]{2,1,0:T(8,128)S(1)}, u32[]{:S(2)}, u32[]{:S(2)}) collective-permute-start(f32[16,64,128]{2,1,0:T(8,128)S(1)} %get-tuple-element.118.rest_3_), channel_id=1, source_target_pairs={{0,1},{1,0},{2,3},{3,2},{4,5},{5,4},{6,7},{7,6},{8,9},{9,8},{10,11... | collective-permute-start | bytes 1572872 | tf_op jit(solution)/shard_map/ppermute | solution.py:62
  55.8 2.5 %copy-start.7 = (bf16[1,512,2048]{2,1,0:T(8,128)(2,1)S(1)}, bf16[1,512,2048]{2,1,0:T(8,128)(2,1)}, u32[]{:S(2)}) copy-start(bf16[1,512,2048]{2,1,0:T(8,128)(2,1)} %param.10) | copy-start | bytes 6291460
  58.3 12.2 %copy-start.1 = (bf16[1,512,4096]{2,1,0:T(8,128)(2,1)S(1)}, bf16[1,512,4096]{2,1,0:T(8,128)(2,1)}, u32[]{:S(2)}) copy-start(bf16[1,512,4096]{2,1,0:T(8,128)(2,1)} %param.11) | copy-start | bytes 12582916
  66.3 4.3 %collective-permute-start.11 = (f32[1024,512]{1,0:T(8,128)S(1)}, f32[1024,512]{1,0:T(8,128)S(1)}, u32[]{:S(2)}, u32[]{:S(2)}) collective-permute-start(f32[1024,512]{1,0:T(8,128)S(1)} %get-tuple-element.125), channel_id=1, source_target_pairs={{0,1},{1,0},{2,3},{3,2},{4,5},{5,4},{6,7},{7,6},{8,9},{9,8},{10,11... | collective-permute-start | bytes 6291464 | tf_op jit(solution)/shard_map/ppermute | solution.py:62
  77.2 16.1 %collective-permute-start.13 = (f32[256,1024]{1,0:T(8,128)S(1)}, f32[256,1024]{1,0:T(8,128)S(1)}, u32[]{:S(2)}, u32[]{:S(2)}) collective-permute-start(f32[256,1024]{1,0:T(8,128)S(1)} %get-tuple-element.133), channel_id=1, source_target_pairs={{0,32},{1,97},{2,34},{3,99},{4,36},{5,101},{6,38},{7,103},{8,40},{... | collective-permute-start | bytes 3145736 | tf_op jit(solution)/shard_map/ppermute | solution.py:62
  78.7 21.6 %collective-permute-start.16 = (f32[256,1536]{1,0:T(8,128)S(1)}, f32[256,1536]{1,0:T(8,128)S(1)}, u32[]{:S(2)}, u32[]{:S(2)}) collective-permute-start(f32[256,1536]{1,0:T(8,128)S(1)} %get-tuple-element.141), channel_id=1, source_target_pairs={{0,8},{1,25},{2,10},{3,27},{4,12},{5,29},{6,14},{7,31},{8,16},{9,1... | collective-permute-start | bytes 4718600 | tf_op jit(solution)/shard_map/ppermute | solution.py:62
  80.5 23.4 %collective-permute-start.15 = (f32[256,1536]{1,0:T(8,128)S(1)}, f32[256,1536]{1,0:T(8,128)S(1)}, u32[]{:S(2)}, u32[]{:S(2)}) collective-permute-start(f32[256,1536]{1,0:T(8,128)S(1)} %get-tuple-element.139), channel_id=1, source_target_pairs={{0,2},{1,7},{2,4},{3,1},{4,6},{5,3},{6,0},{7,5},{8,10},{9,15},{10,... | collective-permute-start | bytes 4718600 | tf_op jit(solution)/shard_map/ppermute | solution.py:62
  93.6 16.1 %collective-permute-start.14 = (f32[256,1024]{1,0:T(8,128)S(1)}, f32[256,1024]{1,0:T(8,128)S(1)}, u32[]{:S(2)}, u32[]{:S(2)}) collective-permute-start(f32[256,1024]{1,0:T(8,128)S(1)} %get-tuple-element.137), channel_id=1, source_target_pairs={{0,32},{1,97},{2,34},{3,99},{4,36},{5,101},{6,38},{7,103},{8,40},{... | collective-permute-start | bytes 3145736 | tf_op jit(solution)/shard_map/ppermute | solution.py:62
  94.2 33.9 %collective-permute-start.21 = (f32[256,1536]{1,0:T(8,128)S(1)}, f32[256,1536]{1,0:T(8,128)S(1)}, u32[]{:S(2)}, u32[]{:S(2)}) collective-permute-start(f32[256,1536]{1,0:T(8,128)S(1)} %get-tuple-element.151), channel_id=1, source_target_pairs={{0,6},{1,3},{2,0},{3,5},{4,2},{5,7},{6,4},{7,1},{8,14},{9,11},{10,... | collective-permute-start | bytes 4718600 | tf_op jit(solution)/shard_map/ppermute | solution.py:62
  97.4 30.7 %collective-permute-start.19 = (f32[256,1536]{1,0:T(8,128)S(1)}, f32[256,1536]{1,0:T(8,128)S(1)}, u32[]{:S(2)}, u32[]{:S(2)}) collective-permute-start(f32[256,1536]{1,0:T(8,128)S(1)} %get-tuple-element.148), channel_id=1, source_target_pairs={{0,24},{1,9},{2,26},{3,11},{4,28},{5,13},{6,30},{7,15},{8,0},{9,17... | collective-permute-start | bytes 4718600 | tf_op jit(solution)/shard_map/ppermute | solution.py:62
  104.4 31.4 %collective-permute-start.20 = (f32[256,1536]{1,0:T(8,128)S(1)}, f32[256,1536]{1,0:T(8,128)S(1)}, u32[]{:S(2)}, u32[]{:S(2)}) collective-permute-start(f32[256,1536]{1,0:T(8,128)S(1)} %get-tuple-element.150), channel_id=1, source_target_pairs={{0,2},{1,7},{2,4},{3,1},{4,6},{5,3},{6,0},{7,5},{8,10},{9,15},{10,... | collective-permute-start | bytes 4718600 | tf_op jit(solution)/shard_map/ppermute | solution.py:62
  104.5 31.3 %collective-permute-start.18 = (f32[256,1536]{1,0:T(8,128)S(1)}, f32[256,1536]{1,0:T(8,128)S(1)}, u32[]{:S(2)}, u32[]{:S(2)}) collective-permute-start(f32[256,1536]{1,0:T(8,128)S(1)} %get-tuple-element.147), channel_id=1, source_target_pairs={{0,8},{1,25},{2,10},{3,27},{4,12},{5,29},{6,14},{7,31},{8,16},{9,1... | collective-permute-start | bytes 4718600 | tf_op jit(solution)/shard_map/ppermute | solution.py:62
  110.7 17.5 %collective-permute-start.17 = (f32[256,1024]{1,0:T(8,128)S(1)}, f32[256,1024]{1,0:T(8,128)S(1)}, u32[]{:S(2)}, u32[]{:S(2)}) collective-permute-start(f32[256,1024]{1,0:T(8,128)S(1)} %get-tuple-element.145), channel_id=1, source_target_pairs={{0,32},{1,97},{2,34},{3,99},{4,36},{5,101},{6,38},{7,103},{8,40},{... | collective-permute-start | bytes 3145736 | tf_op jit(solution)/shard_map/ppermute | solution.py:62
  137.5 14.1 %collective-permute-start.23 = (f32[64,1536]{1,0:T(8,128)S(1)}, f32[64,1536]{1,0:T(8,128)S(1)}, u32[]{:S(2)}, u32[]{:S(2)}) collective-permute-start(f32[64,1536]{1,0:T(8,128)S(1)} %get-tuple-element.157), channel_id=1, source_target_pairs={{0,2},{1,7},{2,4},{3,1},{4,6},{5,3},{6,0},{7,5},{8,10},{9,15},{10,... | collective-permute-start | bytes 1179656 | tf_op jit(solution)/shard_map/ppermute | solution.py:62
  137.6 14.1 %collective-permute-start.24 = (f32[64,1536]{1,0:T(8,128)S(1)}, f32[64,1536]{1,0:T(8,128)S(1)}, u32[]{:S(2)}, u32[]{:S(2)}) collective-permute-start(f32[64,1536]{1,0:T(8,128)S(1)} %get-tuple-element.159), channel_id=1, source_target_pairs={{0,6},{1,3},{2,0},{3,5},{4,2},{5,7},{6,4},{7,1},{8,14},{9,11},{10,... | collective-permute-start | bytes 1179656 | tf_op jit(solution)/shard_map/ppermute | solution.py:62
  140.8 11.7 %collective-permute-start.25 = (f32[64,1536]{1,0:T(8,128)S(1)}, f32[64,1536]{1,0:T(8,128)S(1)}, u32[]{:S(2)}, u32[]{:S(2)}) collective-permute-start(f32[64,1536]{1,0:T(8,128)S(1)} %get-tuple-element.161), channel_id=1, source_target_pairs={{0,32},{1,97},{2,34},{3,99},{4,36},{5,101},{6,38},{7,103},{8,40},{... | collective-permute-start | bytes 1179656 | tf_op jit(solution)/shard_map/ppermute | solution.py:62
  142.3 10.2 %collective-permute-start.26 = (f32[64,1536]{1,0:T(8,128)S(1)}, f32[64,1536]{1,0:T(8,128)S(1)}, u32[]{:S(2)}, u32[]{:S(2)}) collective-permute-start(f32[64,1536]{1,0:T(8,128)S(1)} %get-tuple-element.163), channel_id=1, source_target_pairs={{0,96},{1,33},{2,98},{3,35},{4,100},{5,37},{6,102},{7,39},{8,104},... | collective-permute-start | bytes 1179656 | tf_op jit(solution)/shard_map/ppermute | solution.py:62
  144.1 7.6 %collective-permute-start.22 = (f32[64,1024]{1,0:T(8,128)S(1)}, f32[64,1024]{1,0:T(8,128)S(1)}, u32[]{:S(2)}, u32[]{:S(2)}) collective-permute-start(f32[64,1024]{1,0:T(8,128)S(1)} %get-tuple-element.154), channel_id=1, source_target_pairs={{0,8},{1,25},{2,10},{3,27},{4,12},{5,29},{6,14},{7,31},{8,16},{9,1... | collective-permute-start | bytes 786440 | tf_op jit(solution)/shard_map/ppermute | solution.py:62
  153.2 9.9 %collective-permute-start.29 = (f32[64,1536]{1,0:T(8,128)S(1)}, f32[64,1536]{1,0:T(8,128)S(1)}, u32[]{:S(2)}, u32[]{:S(2)}) collective-permute-start(f32[64,1536]{1,0:T(8,128)S(1)} %get-tuple-element.167), channel_id=1, source_target_pairs={{0,2},{1,7},{2,4},{3,1},{4,6},{5,3},{6,0},{7,5},{8,10},{9,15},{10,... | collective-permute-start | bytes 1179656 | tf_op jit(solution)/shard_map/ppermute | solution.py:62
  153.3 9.8 %collective-permute-start.30 = (f32[64,1536]{1,0:T(8,128)S(1)}, f32[64,1536]{1,0:T(8,128)S(1)}, u32[]{:S(2)}, u32[]{:S(2)}) collective-permute-start(f32[64,1536]{1,0:T(8,128)S(1)} %get-tuple-element.169), channel_id=1, source_target_pairs={{0,32},{1,97},{2,34},{3,99},{4,36},{5,101},{6,38},{7,103},{8,40},{... | collective-permute-start | bytes 1179656 | tf_op jit(solution)/shard_map/ppermute | solution.py:62
  153.6 9.6 %collective-permute-start.27 = (f32[64,1024]{1,0:T(8,128)S(1)}, f32[64,1024]{1,0:T(8,128)S(1)}, u32[]{:S(2)}, u32[]{:S(2)}) collective-permute-start(f32[64,1024]{1,0:T(8,128)S(1)} %get-tuple-element.164), channel_id=1, source_target_pairs={{0,8},{1,25},{2,10},{3,27},{4,12},{5,29},{6,14},{7,31},{8,16},{9,1... | collective-permute-start | bytes 786440 | tf_op jit(solution)/shard_map/ppermute | solution.py:62
  154.3 8.9 %collective-permute-start.28 = (f32[64,1024]{1,0:T(8,128)S(1)}, f32[64,1024]{1,0:T(8,128)S(1)}, u32[]{:S(2)}, u32[]{:S(2)}) collective-permute-start(f32[64,1024]{1,0:T(8,128)S(1)} %get-tuple-element.165), channel_id=1, source_target_pairs={{0,24},{1,9},{2,26},{3,11},{4,28},{5,13},{6,30},{7,15},{8,0},{9,17... | collective-permute-start | bytes 786440 | tf_op jit(solution)/shard_map/ppermute | solution.py:62
  163.9 10.1 %collective-permute-start.32 = (f32[32,1536]{1,0:T(8,128)S(1)}, f32[32,1536]{1,0:T(8,128)S(1)}, u32[]{:S(2)}, u32[]{:S(2)}) collective-permute-start(f32[32,1536]{1,0:T(8,128)S(1)} %get-tuple-element.173), channel_id=1, source_target_pairs={{0,64},{1,65},{2,66},{3,67},{4,68},{5,69},{6,70},{7,71},{8,72},{9,... | collective-permute-start | bytes 589832 | tf_op jit(solution)/shard_map/ppermute | solution.py:58
  165.7 9.0 %collective-permute-start.33 = (f32[32,1536]{1,0:T(8,128)S(1)}, f32[32,1536]{1,0:T(8,128)S(1)}, u32[]{:S(2)}, u32[]{:S(2)}) collective-permute-start(f32[32,1536]{1,0:T(8,128)S(1)} %get-tuple-element.175), channel_id=1, source_target_pairs={{0,16},{1,17},{2,18},{3,19},{4,20},{5,21},{6,22},{7,23},{8,24},{9,... | collective-permute-start | bytes 589832 | tf_op jit(solution)/shard_map/ppermute | solution.py:58
  167.5 6.5 %collective-permute-start.31 = (f32[32,1024]{1,0:T(8,128)S(1)}, f32[32,1024]{1,0:T(8,128)S(1)}, u32[]{:S(2)}, u32[]{:S(2)}) collective-permute-start(f32[32,1024]{1,0:T(8,128)S(1)} %get-tuple-element.171), channel_id=1, source_target_pairs={{0,4},{1,5},{2,6},{3,7},{4,0},{5,1},{6,2},{7,3},{8,12},{9,13},{10,... | collective-permute-start | bytes 393224 | tf_op jit(solution)/shard_map/ppermute | solution.py:58
  175.3 6.3 %collective-permute-start.34 = (f32[16,1536]{1,0:T(8,128)S(1)}, f32[16,1536]{1,0:T(8,128)S(1)}, u32[]{:S(2)}, u32[]{:S(2)}) collective-permute-start(f32[16,1536]{1,0:T(8,128)S(1)} %get-tuple-element.177), channel_id=1, source_target_pairs={{0,32},{1,33},{2,34},{3,35},{4,36},{5,37},{6,38},{7,39},{8,40},{9,... | collective-permute-start | bytes 294920 | tf_op jit(solution)/shard_map/ppermute | solution.py:58
  175.7 6.0 %collective-permute-start.35 = (f32[16,1536]{1,0:T(8,128)S(1)}, f32[16,1536]{1,0:T(8,128)S(1)}, u32[]{:S(2)}, u32[]{:S(2)}) collective-permute-start(f32[16,1536]{1,0:T(8,128)S(1)} %get-tuple-element.179), channel_id=1, source_target_pairs={{0,8},{1,9},{2,10},{3,11},{4,12},{5,13},{6,14},{7,15},{8,0},{9,1},... | collective-permute-start | bytes 294920 | tf_op jit(solution)/shard_map/ppermute | solution.py:58
  177.4 4.3 %collective-permute-start.36 = (f32[16,1024]{1,0:T(8,128)S(1)}, f32[16,1024]{1,0:T(8,128)S(1)}, u32[]{:S(2)}, u32[]{:S(2)}) collective-permute-start(f32[16,1024]{1,0:T(8,128)S(1)} %get-tuple-element.181), channel_id=1, source_target_pairs={{0,2},{1,3},{2,0},{3,1},{4,6},{5,7},{6,4},{7,5},{8,10},{9,11},{10,... | collective-permute-start | bytes 196616 | tf_op jit(solution)/shard_map/ppermute | solution.py:58
  182.3 9.8 %collective-permute-start.39 = (f32[16,4096]{1,0:T(8,128)S(1)}, f32[16,4096]{1,0:T(8,128)S(1)}, u32[]{:S(2)}, u32[]{:S(2)}) collective-permute-start(f32[16,4096]{1,0:T(8,128)S(1)} %last.1.refs_0_), channel_id=1, source_target_pairs={{0,64},{1,65},{2,66},{3,67},{4,68},{5,69},{6,70},{7,71},{8,72},{9,... | collective-permute-start | bytes 786440 | tf_op jit(solution)/shard_map/ppermute | solution.py:62
  185.0 9.0 %collective-permute-start.38 = (f32[16,4096]{1,0:T(8,128)S(1)}, f32[16,4096]{1,0:T(8,128)S(1)}, u32[]{:S(2)}, u32[]{:S(2)}) collective-permute-start(f32[16,4096]{1,0:T(8,128)S(1)} %last.1.refs_0_), channel_id=1, source_target_pairs={{0,96},{1,97},{2,98},{3,99},{4,100},{5,101},{6,102},{7,103},{8,104... | collective-permute-start | bytes 786440 | tf_op jit(solution)/shard_map/ppermute | solution.py:62
  185.9 9.5 %collective-permute-start.37 = (f32[16,4096]{1,0:T(8,128)S(1)}, f32[16,4096]{1,0:T(8,128)S(1)}, u32[]{:S(2)}, u32[]{:S(2)}) collective-permute-start(f32[16,4096]{1,0:T(8,128)S(1)} %last.1.refs_0_), channel_id=1, source_target_pairs={{0,32},{1,33},{2,34},{3,35},{4,36},{5,37},{6,38},{7,39},{8,40},{9,... | collective-permute-start | bytes 786440 | tf_op jit(solution)/shard_map/ppermute | solution.py:62

commit v4 on v3

--- a/solution.py
+++ b/solution.py
@@ -27,6 +27,7 @@
 
 KINDS = {"y": (0, 1, 2), "z": (3, 4, 5), "x": (6, 7)}
 GROUP = 2
+LARGE = 4
 
 
 def linear(p):
@@ -115,7 +116,7 @@
 ):
     first = where_ref[3] == 0
     wide_ref[...] = cotan_ref[...].astype(F32)
-    for head in range(GROUP):
+    for head in range(LARGE):
         lanes = slice(head * DK, (head + 1) * DK)
         cum, end = block_cumsum(g_ref[:, lanes])
         cum_ref[:, lanes] = cum.reshape(TOK, DK)
@@ -141,8 +142,8 @@
 
 def local_state(where, k, v, g, cotan):
     out = jax.ShapeDtypeStruct((H, MSG, DK), F32)
-    steps = H // GROUP
-    heads = pl.BlockSpec((TOK, GROUP * DK), lambda h, w: (0, h))
+    steps = H // LARGE
+    heads = pl.BlockSpec((TOK, LARGE * DK), lambda h, w: (0, h))
     wide = pl.BlockSpec((TOK, D // steps), lambda h, w: (0, h))
     return pl.pallas_call(
         state_kernel,
@@ -150,7 +151,7 @@
             num_scalar_prefetch=1,
             grid=(steps,),
             in_specs=[heads] * 3 + [wide],
-            out_specs=[pl.BlockSpec((GROUP, MSG, DK), lambda h, w: (h, 0, 0))] * 2
+            out_specs=[pl.BlockSpec((LARGE, MSG, DK), lambda h, w: (h, 0, 0))] * 2
             + [heads, wide],
         ),
         out_shape=[out, out]
@@ -356,7 +357,7 @@
     where_ref, out_ref, high_ref, low_ref, mine_ref, got_ref, gate_ref, hid_ref, keep_ref, send_ref
 ):
     first = where_ref[3] == 0
-    for head in range(GROUP):
+    for head in range(LARGE):
         lanes = slice(head * DK, (head + 1) * DK)
         a, b = mine_ref[head], got_ref[head]
         state = jnp.concatenate([jnp.where(first, a, b), jnp.where(first, b, a)], axis=0)
@@ -374,14 +375,14 @@
 
 
 def gated(where, local, mine, got, gate):
-    spec = pl.BlockSpec((TOK, GROUP * DK), lambda h, w: (0, h))
-    state = pl.BlockSpec((GROUP, HALF, DK), lambda h, w: (h, 0, 0))
-    turned = pl.BlockSpec((GROUP * HALF, TOK), lambda h, w: (h, 0))
+    spec = pl.BlockSpec((TOK, LARGE * DK), lambda h, w: (0, h))
+    state = pl.BlockSpec((LARGE, HALF, DK), lambda h, w: (h, 0, 0))
+    turned = pl.BlockSpec((LARGE * HALF, TOK), lambda h, w: (h, 0))
     return pl.pallas_call(
         hidden_kernel,
         grid_spec=pltpu.PrefetchScalarGridSpec(
             num_scalar_prefetch=1,
-            grid=(H // GROUP,),
+            grid=(H // LARGE,),
             in_specs=[spec, spec, spec, state, state, spec],
             out_specs=[spec, turned, turned],
         ),

time: 197 us -> 195 us (0.990)
  Pallas kernels: 63.6 us -> 60.8 us
  transfers between devices with their start and end apart: 40 -> 40, of which waited for: 23 -> 24; matrix products, arithmetic and copies ran while one was open for 0% -> 0% of each run, Pallas kernels for 21% -> 21%
where the time goes in v4:
time: 195 us; the launch traced here: 194 us
  waiting for transfers between devices  75.5 us (39%)
  Pallas kernels  60.8 us (31%)
  starting transfers between devices  49.4 us (25%)
  local copies, waits for them, and re-layouts  7.58 us (4%)
    ppermute x34, waiting for transfers between devices, send(): return lax.ppermute(array, AXES, shift_pairs(axis, by))  66.6 us
    ppermute x34, starting transfers between devices, send(): return lax.ppermute(array, AXES, shift_pairs(axis, by))  41.3 us
    pallas_call x6, Pallas kernels, products(): pl.pallas_call(functools.partial(product_kernel, axis, steps), grid_spec=...  18.3 us
    pallas_call x4, Pallas kernels, local_core(): pl.pallas_call(core_kernel, grid=(steps,), in_specs=[spec] * 4 + [pl.Bloc...  18.1 us
    ppermute x6, waiting for transfers between devices, swap(): return lax.ppermute(array, AXES, pairs)  8.91 us
    ppermute x6, starting transfers between devices, swap(): return lax.ppermute(array, AXES, pairs)  8.03 us
    unnamed x16, local copies, waits for them, and re-layouts  7.58 us
    pallas_call x1, Pallas kernels, local_state(): pl.pallas_call(state_kernel, grid_spec=pltpu.PrefetchScalarGridSpec(num_s...  7.09 us
  transfers between devices with their start and end apart: 40, of which 24 were waited for; matrix products, arithmetic and copies ran while one was open for 0% of the time, Pallas kernels for 21%

profile of v4, /device:TPU:0, one launch (start us, length us, event | category | flops | bytes accessed | tf_op | source)
XLA Modules:
  0.0 194.3 jit_solution(8685113960752683739)
XLA Ops:
  0.7 2.2 %copy-done = bf16[1,512,4096]{2,1,0:T(8,128)(2,1)S(1)} copy-done((bf16[1,512,4096]{2,1,0:T(8,128)(2,1)S(1)}, bf16[1,512,4096]{2,1,0:T(8,128)(2,1)}, u32[]{:S(2)}) %copy-start) | copy-done | bytes 4194328
  2.9 1.6 copy-done.2
  4.5 1.6 copy-done.4
  6.1 2.2 %copy-done.6 = f32[1,512,2048]{2,1,0:T(8,128)S(1)} copy-done((f32[1,512,2048]{2,1,0:T(8,128)S(1)}, f32[1,512,2048]{2,1,0:T(8,128)}, u32[]{:S(2)}) %copy-start.6) | copy-done | bytes 4194328
  8.3 7.1 %local_state.1 = (f32[16,72,128]{2,1,0:T(8,128)S(1)}, f32[16,72,128]{2,1,0:T(8,128)S(1)}, f32[512,2048]{1,0:T(8,128)S(1)}, f32[512,4096]{1,0:T(8,128)}) custom-call(s32[4]{0:T(128)S(1)} %pad_add_fusion.where_ref.refs_0_, bf16[512,2048]{1,0:T(8,128)(2,1)S(1)} %bitcast.26, bf16[512,2048]{1,0:T(8,128)(2,1)S(1)} %bitcast.31, f32[512,2048]{1,0:T(8,128)S(1)} %bitcast.46, ...), custom_call_target="tpu_custom_call" | custom-call | flops 268435456 | bytes 26000000 | tf_op jit(solution)/shard_map/local_state/pallas_call | solution.py:148
  15.4 2.0 %collective-permute-done.got_ref.refs_2_ = f32[16,72,128]{2,1,0:T(8,128)S(1)} collective-permute-done((f32[16,72,128]{2,1,0:T(8,128)S(1)}, f32[16,72,128]{2,1,0:T(8,128)S(1)}, u32[]{:S(2)}, u32[]{:S(2)}) %collective-permute-start) | collective-permute-done | bytes 589856 | tf_op jit(solution)/shard_map/ppermute | solution.py:63
  18.2 4.1 %collective-permute-start.2 = (f32[4,72,128]{2,1,0:T(8,128)S(1)}, f32[4,72,128]{2,1,0:T(8,128)S(1)}, u32[]{:S(2)}, u32[]{:S(2)}) collective-permute-start(f32[4,72,128]{2,1,0:T(8,128)S(1)} %get-tuple-element.101), channel_id=1, source_target_pairs={{0,6},{1,7},{2,0},{3,1},{4,2},{5,3},{6,4},{7,5},{8,14},{9,15},{10,... | collective-permute-start | bytes 442376 | tf_op jit(solution)/shard_map/ppermute | solution.py:63
  23.6 6.7 %local_core.4 = (f32[512,2048]{1,0:T(8,128)S(1)}, bf16[512,2048]{1,0:T(8,128)(2,1)S(1)}, bf16[512,2048]{1,0:T(8,128)(2,1)S(1)}, f32[8,128]{1,0:T(8,128)S(1)}) custom-call(bf16[512,2048]{1,0:T(8,128)(2,1)S(1)} %bitcast.42, bf16[512,2048]{1,0:T(8,128)(2,1)S(1)} %bitcast.27, bf16[512,2048]{1,0:T(8,128)(2,1)S(1)} %bitcast.32, ...), custom_call_target="tpu_custom_call" | custom-call | flops 536870912 | bytes 20000000 | tf_op jit(solution)/shard_map/local_core/pallas_call | solution.py:215
  30.6 2.0 %collective-permute-done.1.refs_2_ = f32[4,72,128]{2,1,0:T(8,128)S(1)} collective-permute-done((f32[4,72,128]{2,1,0:T(8,128)S(1)}, f32[4,72,128]{2,1,0:T(8,128)S(1)}, u32[]{:S(2)}, u32[]{:S(2)}) %collective-permute-start.1) | collective-permute-done | bytes 147488 | tf_op jit(solution)/shard_map/ppermute | solution.py:63
  33.2 3.3 %collective-permute-start.6 = (f32[4,72,128]{2,1,0:T(8,128)S(1)}, f32[4,72,128]{2,1,0:T(8,128)S(1)}, u32[]{:S(2)}, u32[]{:S(2)}) collective-permute-start(f32[4,72,128]{2,1,0:T(8,128)S(1)} %get-tuple-element.104.rest_3_.refs_2_), channel_id=1, source_target_pairs={{0,16},{1,17},{2,18},{3,19},{4,20},{5,21},{6,22},{7,23},{8,24},{9,... | collective-permute-start | bytes 442376 | tf_op jit(solution)/shard_map/ppermute | solution.py:63
  38.5 4.5 %local_core.5 = (f32[512,2048]{1,0:T(8,128)S(1)}, bf16[512,2048]{1,0:T(8,128)(2,1)S(1)}, bf16[512,2048]{1,0:T(8,128)(2,1)S(1)}, f32[8,128]{1,0:T(8,128)S(1)}) custom-call(bf16[512,2048]{1,0:T(8,128)(2,1)S(1)} %bitcast.43, bf16[512,2048]{1,0:T(8,128)(2,1)S(1)} %bitcast.28, ...), custom_call_target="tpu_custom_call", output_to_operand_aliasing={{0}: (4, {}), {1}: (5, {}), {2}: (6, {})} | custom-call | flops 536870912 | bytes 20000000 | tf_op jit(solution)/shard_map/local_core/pallas_call | solution.py:215
  47.1 4.5 %local_core.6 = (f32[512,2048]{1,0:T(8,128)S(1)}, bf16[512,2048]{1,0:T(8,128)(2,1)S(1)}, bf16[512,2048]{1,0:T(8,128)(2,1)S(1)}, f32[8,128]{1,0:T(8,128)S(1)}) custom-call(bf16[512,2048]{1,0:T(8,128)(2,1)S(1)} %bitcast.44, bf16[512,2048]{1,0:T(8,128)(2,1)S(1)} %bitcast.29, ...), custom_call_target="tpu_custom_call", output_to_operand_aliasing={{0}: (4, {}), {1}: (5, {}), {2}: (6, {})} | custom-call | flops 536870912 | bytes 20000000 | tf_op jit(solution)/shard_map/local_core/pallas_call | solution.py:215
  54.9 2.5 %local_core.7 = (f32[512,2048]{1,0:T(8,128)S(1)}, bf16[512,2048]{1,0:T(8,128)(2,1)S(1)}, bf16[512,2048]{1,0:T(8,128)(2,1)S(1)}, f32[8,128]{1,0:T(8,128)}) custom-call(bf16[512,2048]{1,0:T(8,128)(2,1)S(1)} %bitcast.45, bf16[512,2048]{1,0:T(8,128)(2,1)S(1)} %bitcast.30, ...), custom_call_target="tpu_custom_call", output_to_operand_aliasing={{0}: (4, {}), {1}: (5, {}), {2}: (6, {})} | custom-call | flops 536870912 | bytes 20000000 | tf_op jit(solution)/shard_map/local_core/pallas_call | solution.py:215
  57.4 6.3 %gated_hidden.1 = (bf16[512,2048]{1,0:T(8,128)(2,1)}, bf16[1024,512]{1,0:T(8,128)(2,1)S(1)}, f32[1024,512]{1,0:T(8,128)S(1)}) custom-call(s32[4]{0:T(128)S(1)} %pad_add_fusion.where_ref.refs_0_, f32[512,2048]{1,0:T(8,128)S(1)} %get-tuple-element.119.out_ref, bf16[512,2048]{1,0:T(8,128)(2,1)S(1)} %get-tuple-element.120.high_ref, ...), custom_call_target="tpu_custom_call" | custom-call | flops 805306368 | bytes 17000000 | tf_op jit(solution)/shard_map/gated_hidden/pallas_call | solution.py:381
  64.2 3.8 %collective-permute-done.11 = f32[1024,512]{1,0:T(8,128)S(1)} collective-permute-done((f32[1024,512]{1,0:T(8,128)S(1)}, f32[1024,512]{1,0:T(8,128)S(1)}, u32[]{:S(2)}, u32[]{:S(2)}) %collective-permute-start.11) | collective-permute-done | bytes 2097184 | tf_op jit(solution)/shard_map/ppermute | solution.py:63
  68.0 2.4 %products_y.2 = (f32[256,1536]{1,0:T(8,128)S(1)}, f32[8,128]{1,0:T(8,128)S(1)}) custom-call(s32[4]{0:T(128)S(1)} %pad_add_fusion.where_ref.refs_0_, bf16[4,4,4,16,512]{4,3,2,1,0:T(8,128)(2,1)S(1)} %bitcast.36, f32[4,4,4,16,512]{4,3,2,1,0:T(8,128)S(1)} %bitcast.20, bf16[512,4096]{1,0:T(8,128)(2,1)S(1)} %bitcast.14, ...), custom_call_target="tpu_custom_call" | custom-call | flops 1000000 | bytes 1000000 | tf_op jit(solution)/shard_map/products_y/pallas_call | solution.py:442
  70.4 2.4 %products_z.2 = (f32[256,1536]{1,0:T(8,128)S(1)}, f32[8,128]{1,0:T(8,128)S(1)}) custom-call(s32[4]{0:T(128)S(1)} %pad_add_fusion.where_ref.refs_0_, bf16[4,4,4,16,512]{4,3,2,1,0:T(8,128)(2,1)S(1)} %bitcast.37, f32[4,4,4,16,512]{4,3,2,1,0:T(8,128)S(1)} %bitcast.21, bf16[512,4096]{1,0:T(8,128)(2,1)S(1)} %bitcast.15, ...), custom_call_target="tpu_custom_call" | custom-call | flops 1000000 | bytes 1000000 | tf_op jit(solution)/shard_map/products_z/pallas_call | solution.py:442
  72.8 1.8 products_x.2
  74.6 1.6 collective-permute-start.13
  76.2 1.8 collective-permute-start.16
  77.9 3.1 %products_x.3 = (f32[256,1024]{1,0:T(8,128)S(1)}, f32[256,1024]{1,0:T(8,128)S(1)}, f32[256,1024]{1,0:T(8,128)S(1)}, f32[8,128]{1,0:T(8,128)S(1)}) custom-call(s32[4]{0:T(128)S(1)} %pad_add_fusion.where_ref.refs_0_, bf16[4,4,4,16,512]{4,3,2,1,0:T(8,128)(2,1)S(1)} %bitcast.39, f32[4,4,4,16,512]{4,3,2,1,0:T(8,128)S(1)} %bitcast.23, ...), custom_call_target="tpu_custom_call" | custom-call | flops 1000000 | bytes 1000000 | tf_op jit(solution)/shard_map/products_x/pallas_call | solution.py:442
  81.0 4.3 %products_y.3 = (f32[256,1536]{1,0:T(8,128)S(1)}, f32[256,1536]{1,0:T(8,128)S(1)}, f32[256,1536]{1,0:T(8,128)S(1)}, f32[8,128]{1,0:T(8,128)S(1)}) custom-call(s32[4]{0:T(128)S(1)} %pad_add_fusion.where_ref.refs_0_, bf16[4,4,4,16,512]{4,3,2,1,0:T(8,128)(2,1)S(1)} %bitcast.40, f32[4,4,4,16,512]{4,3,2,1,0:T(8,128)S(1)} %bitcast.24, ...), custom_call_target="tpu_custom_call" | custom-call | flops 1000000 | bytes 1000000 | tf_op jit(solution)/shard_map/products_y/pallas_call | solution.py:442
  85.3 4.3 %products_z.3 = (f32[256,1536]{1,0:T(8,128)S(1)}, f32[256,1536]{1,0:T(8,128)S(1)}, f32[256,1536]{1,0:T(8,128)S(1)}, f32[8,128]{1,0:T(8,128)S(1)}) custom-call(s32[4]{0:T(128)S(1)} %pad_add_fusion.where_ref.refs_0_, bf16[4,4,4,16,512]{4,3,2,1,0:T(8,128)(2,1)S(1)} %bitcast.41, f32[4,4,4,16,512]{4,3,2,1,0:T(8,128)S(1)} %bitcast.25, ...), custom_call_target="tpu_custom_call" | custom-call | flops 1000000 | bytes 1000000 | tf_op jit(solution)/shard_map/products_z/pallas_call | solution.py:442
  91.6 3.2 %collective-permute-start.21 = (f32[256,1536]{1,0:T(8,128)S(1)}, f32[256,1536]{1,0:T(8,128)S(1)}, u32[]{:S(2)}, u32[]{:S(2)}) collective-permute-start(f32[256,1536]{1,0:T(8,128)S(1)} %get-tuple-element.151), channel_id=1, source_target_pairs={{0,6},{1,3},{2,0},{3,5},{4,2},{5,7},{6,4},{7,1},{8,14},{9,11},{10,... | collective-permute-start | bytes 4718600 | tf_op jit(solution)/shard_map/ppermute | solution.py:63
  94.8 1.5 collective-permute-start.19
  96.3 1.5 collective-permute-done.16.b
  98.4 2.9 %collective-permute-done.15.b = f32[256,1536]{1,0:T(8,128)S(1)} collective-permute-done((f32[256,1536]{1,0:T(8,128)S(1)}, f32[256,1536]{1,0:T(8,128)S(1)}, u32[]{:S(2)}, u32[]{:S(2)}) %collective-permute-start.15) | collective-permute-done | bytes 1572896 | tf_op jit(solution)/shard_map/ppermute | solution.py:63
  101.9 1.9 collective-permute-start.18
  103.8 3.3 %collective-permute-done.14.b = f32[256,1024]{1,0:T(8,128)S(1)} collective-permute-done((f32[256,1024]{1,0:T(8,128)S(1)}, f32[256,1024]{1,0:T(8,128)S(1)}, u32[]{:S(2)}, u32[]{:S(2)}) %collective-permute-start.14) | collective-permute-done | bytes 1048608 | tf_op jit(solution)/shard_map/ppermute | solution.py:63
  108.6 16.9 %collective-permute-done.21.refs_8_ = f32[256,1536]{1,0:T(8,128)S(1)} collective-permute-done((f32[256,1536]{1,0:T(8,128)S(1)}, f32[256,1536]{1,0:T(8,128)S(1)}, u32[]{:S(2)}, u32[]{:S(2)}) %collective-permute-start.21) | collective-permute-done | bytes 1572896 | tf_op jit(solution)/shard_map/ppermute | solution.py:63
  125.6 7.7 %collective-permute-done.20.refs_7_ = f32[256,1536]{1,0:T(8,128)S(1)} collective-permute-done((f32[256,1536]{1,0:T(8,128)S(1)}, f32[256,1536]{1,0:T(8,128)S(1)}, u32[]{:S(2)}, u32[]{:S(2)}) %collective-permute-start.20) | collective-permute-done | bytes 1572896 | tf_op jit(solution)/shard_map/ppermute | solution.py:63
  133.3 1.7 second.1
  135.0 3.2 %collective-permute-start.24 = (f32[64,1536]{1,0:T(8,128)S(1)}, f32[64,1536]{1,0:T(8,128)S(1)}, u32[]{:S(2)}, u32[]{:S(2)}) collective-permute-start(f32[64,1536]{1,0:T(8,128)S(1)} %get-tuple-element.159), channel_id=1, source_target_pairs={{0,6},{1,3},{2,0},{3,5},{4,2},{5,7},{6,4},{7,1},{8,14},{9,11},{10,... | collective-permute-start | bytes 1179656 | tf_op jit(solution)/shard_map/ppermute | solution.py:63
  138.3 1.5 collective-permute-start.25
  139.7 1.7 collective-permute-start.26
  142.9 6.2 %collective-permute-done.22.refs_2_ = f32[64,1024]{1,0:T(8,128)S(1)} collective-permute-done((f32[64,1024]{1,0:T(8,128)S(1)}, f32[64,1024]{1,0:T(8,128)S(1)}, u32[]{:S(2)}, u32[]{:S(2)}) %collective-permute-start.22) | collective-permute-done | bytes 262176 | tf_op jit(solution)/shard_map/ppermute | solution.py:63
  151.6 2.5 %collective-permute-start.28 = (f32[64,1024]{1,0:T(8,128)S(1)}, f32[64,1024]{1,0:T(8,128)S(1)}, u32[]{:S(2)}, u32[]{:S(2)}) collective-permute-start(f32[64,1024]{1,0:T(8,128)S(1)} %get-tuple-element.165), channel_id=1, source_target_pairs={{0,24},{1,9},{2,26},{3,11},{4,28},{5,13},{6,30},{7,15},{8,0},{9,17... | collective-permute-start | bytes 786440 | tf_op jit(solution)/shard_map/ppermute | solution.py:63
  154.2 6.0 %collective-permute-done.27.refs_2_ = f32[64,1024]{1,0:T(8,128)S(1)} collective-permute-done((f32[64,1024]{1,0:T(8,128)S(1)}, f32[64,1024]{1,0:T(8,128)S(1)}, u32[]{:S(2)}, u32[]{:S(2)}) %collective-permute-start.27) | collective-permute-done | bytes 262176 | tf_op jit(solution)/shard_map/ppermute | solution.py:63
  161.3 1.6 collective-permute-start.32
  162.9 2.1 %collective-permute-start.33 = (f32[32,1536]{1,0:T(8,128)S(1)}, f32[32,1536]{1,0:T(8,128)S(1)}, u32[]{:S(2)}, u32[]{:S(2)}) collective-permute-start(f32[32,1536]{1,0:T(8,128)S(1)} %get-tuple-element.175), channel_id=1, source_target_pairs={{0,16},{1,17},{2,18},{3,19},{4,20},{5,21},{6,22},{7,23},{8,24},{9,... | collective-permute-start | bytes 589832 | tf_op jit(solution)/shard_map/ppermute | solution.py:59
  165.0 1.8 collective-permute-start.31
  166.8 4.7 %collective-permute-done.31.refs_2_ = f32[32,1024]{1,0:T(8,128)S(1)} collective-permute-done((f32[32,1024]{1,0:T(8,128)S(1)}, f32[32,1024]{1,0:T(8,128)S(1)}, u32[]{:S(2)}, u32[]{:S(2)}) %collective-permute-start.31) | collective-permute-done | bytes 131104 | tf_op jit(solution)/shard_map/ppermute | solution.py:59
  172.9 1.7 collective-permute-start.35
  175.1 3.8 %collective-permute-done.36.refs_6_ = f32[16,1024]{1,0:T(8,128)S(1)} collective-permute-done((f32[16,1024]{1,0:T(8,128)S(1)}, f32[16,1024]{1,0:T(8,128)S(1)}, u32[]{:S(2)}, u32[]{:S(2)}) %collective-permute-start.36) | collective-permute-done | bytes 65568 | tf_op jit(solution)/shard_map/ppermute | solution.py:59
  179.5 2.9 %collective-permute-start.39 = (f32[16,4096]{1,0:T(8,128)S(1)}, f32[16,4096]{1,0:T(8,128)S(1)}, u32[]{:S(2)}, u32[]{:S(2)}) collective-permute-start(f32[16,4096]{1,0:T(8,128)S(1)} %last.1.refs_0_), channel_id=1, source_target_pairs={{0,64},{1,65},{2,66},{3,67},{4,68},{5,69},{6,70},{7,71},{8,72},{9,... | collective-permute-start | bytes 786440 | tf_op jit(solution)/shard_map/ppermute | solution.py:63
  184.4 5.2 %collective-permute-done.39.refs_3_ = f32[16,4096]{1,0:T(8,128)S(1)} collective-permute-done((f32[16,4096]{1,0:T(8,128)S(1)}, f32[16,4096]{1,0:T(8,128)S(1)}, u32[]{:S(2)}, u32[]{:S(2)}) %collective-permute-start.39) | collective-permute-done | bytes 262176 | tf_op jit(solution)/shard_map/ppermute | solution.py:63
  190.8 1.9 collective-permute-done.37.refs_1_
  192.7 1.6 assemble.1
  (75 shorter events, 28.5 us)
Async XLA Ops:
  0.7 2.2 %copy-start = (bf16[1,512,4096]{2,1,0:T(8,128)(2,1)S(1)}, bf16[1,512,4096]{2,1,0:T(8,128)(2,1)}, u32[]{:S(2)}) copy-start(bf16[1,512,4096]{2,1,0:T(8,128)(2,1)} %param.11) | copy-start | bytes 12582916
  2.9 1.6 copy-start.2
  4.5 1.6 copy-start.4
  6.1 2.2 %copy-start.6 = (f32[1,512,2048]{2,1,0:T(8,128)S(1)}, f32[1,512,2048]{2,1,0:T(8,128)}, u32[]{:S(2)}) copy-start(f32[1,512,2048]{2,1,0:T(8,128)} %param.9) | copy-start | bytes 12582916
  15.4 2.0 %collective-permute-start = (f32[16,72,128]{2,1,0:T(8,128)S(1)}, f32[16,72,128]{2,1,0:T(8,128)S(1)}, u32[]{:S(2)}, u32[]{:S(2)}) collective-permute-start(f32[16,72,128]{2,1,0:T(8,128)S(1)} %get-tuple-element.94), channel_id=1, source_target_pairs={{0,1},{1,0},{2,3},{3,2},{4,5},{5,4},{6,7},{7,6},{8,9},{9,8},{10,11... | collective-permute-start | bytes 1769480 | tf_op jit(solution)/shard_map/ppermute | solution.py:63
  17.4 6.3 %copy-start.3 = (bf16[1,512,2048]{2,1,0:T(8,128)(2,1)S(1)}, bf16[1,512,2048]{2,1,0:T(8,128)(2,1)}, u32[]{:S(2)}) copy-start(bf16[1,512,2048]{2,1,0:T(8,128)(2,1)} %param.7) | copy-start | bytes 6291460
  17.4 6.3 %copy-start.5 = (bf16[1,512,2048]{2,1,0:T(8,128)(2,1)S(1)}, bf16[1,512,2048]{2,1,0:T(8,128)(2,1)}, u32[]{:S(2)}) copy-start(bf16[1,512,2048]{2,1,0:T(8,128)(2,1)} %param.6) | copy-start | bytes 6291460
  18.0 50.0 %collective-permute-start.12 = (f32[512,4096]{1,0:T(8,128)}, f32[512,4096]{1,0:T(8,128)S(1)}, u32[]{:S(2)}, u32[]{:S(2)}) collective-permute-start(f32[512,4096]{1,0:T(8,128)} %get-tuple-element.126), channel_id=1, source_target_pairs={{0,1},{1,0},{2,3},{3,2},{4,5},{5,4},{6,7},{7,6},{8,9},{9,8},{10,11... | collective-permute-start | bytes 25165832 | tf_op jit(solution)/shard_map/ppermute | solution.py:63
  18.2 12.1 %collective-permute-start.2 = (f32[4,72,128]{2,1,0:T(8,128)S(1)}, f32[4,72,128]{2,1,0:T(8,128)S(1)}, u32[]{:S(2)}, u32[]{:S(2)}) collective-permute-start(f32[4,72,128]{2,1,0:T(8,128)S(1)} %get-tuple-element.101), channel_id=1, source_target_pairs={{0,6},{1,7},{2,0},{3,1},{4,2},{5,3},{6,4},{7,5},{8,14},{9,15},{10,... | collective-permute-start | bytes 442376 | tf_op jit(solution)/shard_map/ppermute | solution.py:63
  22.4 8.3 %collective-permute-start.3 = (f32[4,72,128]{2,1,0:T(8,128)S(1)}, f32[4,72,128]{2,1,0:T(8,128)S(1)}, u32[]{:S(2)}, u32[]{:S(2)}) collective-permute-start(f32[4,72,128]{2,1,0:T(8,128)S(1)} %get-tuple-element.102), channel_id=1, source_target_pairs={{0,4},{1,5},{2,6},{3,7},{4,0},{5,1},{6,2},{7,3},{8,12},{9,13},{10,... | collective-permute-start | bytes 442376 | tf_op jit(solution)/shard_map/ppermute | solution.py:63
  22.4 10.2 %collective-permute-start.1 = (f32[4,72,128]{2,1,0:T(8,128)S(1)}, f32[4,72,128]{2,1,0:T(8,128)S(1)}, u32[]{:S(2)}, u32[]{:S(2)}) collective-permute-start(f32[4,72,128]{2,1,0:T(8,128)S(1)} %get-tuple-element.96.rest_0_), channel_id=1, source_target_pairs={{0,2},{1,3},{2,4},{3,5},{4,6},{5,7},{6,0},{7,1},{8,10},{9,11},{10,... | collective-permute-start | bytes 442376 | tf_op jit(solution)/shard_map/ppermute | solution.py:63
  33.2 9.8 %collective-permute-start.6 = (f32[4,72,128]{2,1,0:T(8,128)S(1)}, f32[4,72,128]{2,1,0:T(8,128)S(1)}, u32[]{:S(2)}, u32[]{:S(2)}) collective-permute-start(f32[4,72,128]{2,1,0:T(8,128)S(1)} %get-tuple-element.104.rest_3_.refs_2_), channel_id=1, source_target_pairs={{0,16},{1,17},{2,18},{3,19},{4,20},{5,21},{6,22},{7,23},{8,24},{9,... | collective-permute-start | bytes 442376 | tf_op jit(solution)/shard_map/ppermute | solution.py:63
  36.5 7.3 %collective-permute-start.5 = (f32[4,72,128]{2,1,0:T(8,128)S(1)}, f32[4,72,128]{2,1,0:T(8,128)S(1)}, u32[]{:S(2)}, u32[]{:S(2)}) collective-permute-start(f32[4,72,128]{2,1,0:T(8,128)S(1)} %get-tuple-element.104.rest_3_.refs_2_), channel_id=1, source_target_pairs={{0,24},{1,25},{2,26},{3,27},{4,28},{5,29},{6,30},{7,31},{8,0},{9,1... | collective-permute-start | bytes 442376 | tf_op jit(solution)/shard_map/ppermute | solution.py:63
  37.6 6.6 %collective-permute-start.4 = (f32[4,72,128]{2,1,0:T(8,128)S(1)}, f32[4,72,128]{2,1,0:T(8,128)S(1)}, u32[]{:S(2)}, u32[]{:S(2)}) collective-permute-start(f32[4,72,128]{2,1,0:T(8,128)S(1)} %get-tuple-element.104.rest_3_.refs_2_), channel_id=1, source_target_pairs={{0,8},{1,9},{2,10},{3,11},{4,12},{5,13},{6,14},{7,15},{8,16},{9,17... | collective-permute-start | bytes 442376 | tf_op jit(solution)/shard_map/ppermute | solution.py:63
  44.8 6.8 %collective-permute-start.8 = (f32[4,64,128]{2,1,0:T(8,128)S(1)}, f32[4,64,128]{2,1,0:T(8,128)S(1)}, u32[]{:S(2)}, u32[]{:S(2)}) collective-permute-start(f32[4,64,128]{2,1,0:T(8,128)S(1)} %get-tuple-element.115), channel_id=1, source_target_pairs={{0,6},{1,7},{2,0},{3,1},{4,2},{5,3},{6,4},{7,5},{8,14},{9,15},{10,... | collective-permute-start | bytes 393224 | tf_op jit(solution)/shard_map/ppermute | solution.py:63
  45.6 7.1 %collective-permute-start.9 = (f32[4,64,128]{2,1,0:T(8,128)S(1)}, f32[4,64,128]{2,1,0:T(8,128)S(1)}, u32[]{:S(2)}, u32[]{:S(2)}) collective-permute-start(f32[4,64,128]{2,1,0:T(8,128)S(1)} %get-tuple-element.116), channel_id=1, source_target_pairs={{0,4},{1,5},{2,6},{3,7},{4,0},{5,1},{6,2},{7,3},{8,12},{9,13},{10,... | collective-permute-start | bytes 393224 | tf_op jit(solution)/shard_map/ppermute | solution.py:63
  46.8 7.1 %collective-permute-start.7 = (f32[4,64,128]{2,1,0:T(8,128)S(1)}, f32[4,64,128]{2,1,0:T(8,128)S(1)}, u32[]{:S(2)}, u32[]{:S(2)}) collective-permute-start(f32[4,64,128]{2,1,0:T(8,128)S(1)} %get-tuple-element.110.rest_3_), channel_id=1, source_target_pairs={{0,2},{1,3},{2,4},{3,5},{4,6},{5,7},{6,0},{7,1},{8,10},{9,11},{10,... | collective-permute-start | bytes 393224 | tf_op jit(solution)/shard_map/ppermute | solution.py:63
  54.6 2.8 %collective-permute-start.10 = (f32[16,64,128]{2,1,0:T(8,128)S(1)}, f32[16,64,128]{2,1,0:T(8,128)S(1)}, u32[]{:S(2)}, u32[]{:S(2)}) collective-permute-start(f32[16,64,128]{2,1,0:T(8,128)S(1)} %get-tuple-element.118.rest_3_), channel_id=1, source_target_pairs={{0,1},{1,0},{2,3},{3,2},{4,5},{5,4},{6,7},{7,6},{8,9},{9,8},{10,11... | collective-permute-start | bytes 1572872 | tf_op jit(solution)/shard_map/ppermute | solution.py:63
  54.9 2.5 %copy-start.7 = (bf16[1,512,2048]{2,1,0:T(8,128)(2,1)S(1)}, bf16[1,512,2048]{2,1,0:T(8,128)(2,1)}, u32[]{:S(2)}) copy-start(bf16[1,512,2048]{2,1,0:T(8,128)(2,1)} %param.10) | copy-start | bytes 6291460
  57.4 10.6 %copy-start.1 = (bf16[1,512,4096]{2,1,0:T(8,128)(2,1)S(1)}, bf16[1,512,4096]{2,1,0:T(8,128)(2,1)}, u32[]{:S(2)}) copy-start(bf16[1,512,4096]{2,1,0:T(8,128)(2,1)} %param.11) | copy-start | bytes 12582916
  63.7 4.3 %collective-permute-start.11 = (f32[1024,512]{1,0:T(8,128)S(1)}, f32[1024,512]{1,0:T(8,128)S(1)}, u32[]{:S(2)}, u32[]{:S(2)}) collective-permute-start(f32[1024,512]{1,0:T(8,128)S(1)} %get-tuple-element.125), channel_id=1, source_target_pairs={{0,1},{1,0},{2,3},{3,2},{4,5},{5,4},{6,7},{7,6},{8,9},{9,8},{10,11... | collective-permute-start | bytes 6291464 | tf_op jit(solution)/shard_map/ppermute | solution.py:63
  74.6 16.1 %collective-permute-start.13 = (f32[256,1024]{1,0:T(8,128)S(1)}, f32[256,1024]{1,0:T(8,128)S(1)}, u32[]{:S(2)}, u32[]{:S(2)}) collective-permute-start(f32[256,1024]{1,0:T(8,128)S(1)} %get-tuple-element.133), channel_id=1, source_target_pairs={{0,32},{1,97},{2,34},{3,99},{4,36},{5,101},{6,38},{7,103},{8,40},{... | collective-permute-start | bytes 3145736 | tf_op jit(solution)/shard_map/ppermute | solution.py:63
  76.2 21.6 %collective-permute-start.16 = (f32[256,1536]{1,0:T(8,128)S(1)}, f32[256,1536]{1,0:T(8,128)S(1)}, u32[]{:S(2)}, u32[]{:S(2)}) collective-permute-start(f32[256,1536]{1,0:T(8,128)S(1)} %get-tuple-element.141), channel_id=1, source_target_pairs={{0,8},{1,25},{2,10},{3,27},{4,12},{5,29},{6,14},{7,31},{8,16},{9,1... | collective-permute-start | bytes 4718600 | tf_op jit(solution)/shard_map/ppermute | solution.py:63
  77.9 23.4 %collective-permute-start.15 = (f32[256,1536]{1,0:T(8,128)S(1)}, f32[256,1536]{1,0:T(8,128)S(1)}, u32[]{:S(2)}, u32[]{:S(2)}) collective-permute-start(f32[256,1536]{1,0:T(8,128)S(1)} %get-tuple-element.139), channel_id=1, source_target_pairs={{0,2},{1,7},{2,4},{3,1},{4,6},{5,3},{6,0},{7,5},{8,10},{9,15},{10,... | collective-permute-start | bytes 4718600 | tf_op jit(solution)/shard_map/ppermute | solution.py:63
  91.1 16.1 %collective-permute-start.14 = (f32[256,1024]{1,0:T(8,128)S(1)}, f32[256,1024]{1,0:T(8,128)S(1)}, u32[]{:S(2)}, u32[]{:S(2)}) collective-permute-start(f32[256,1024]{1,0:T(8,128)S(1)} %get-tuple-element.137), channel_id=1, source_target_pairs={{0,32},{1,97},{2,34},{3,99},{4,36},{5,101},{6,38},{7,103},{8,40},{... | collective-permute-start | bytes 3145736 | tf_op jit(solution)/shard_map/ppermute | solution.py:63
  91.6 33.9 %collective-permute-start.21 = (f32[256,1536]{1,0:T(8,128)S(1)}, f32[256,1536]{1,0:T(8,128)S(1)}, u32[]{:S(2)}, u32[]{:S(2)}) collective-permute-start(f32[256,1536]{1,0:T(8,128)S(1)} %get-tuple-element.151), channel_id=1, source_target_pairs={{0,6},{1,3},{2,0},{3,5},{4,2},{5,7},{6,4},{7,1},{8,14},{9,11},{10,... | collective-permute-start | bytes 4718600 | tf_op jit(solution)/shard_map/ppermute | solution.py:63
  94.8 30.7 %collective-permute-start.19 = (f32[256,1536]{1,0:T(8,128)S(1)}, f32[256,1536]{1,0:T(8,128)S(1)}, u32[]{:S(2)}, u32[]{:S(2)}) collective-permute-start(f32[256,1536]{1,0:T(8,128)S(1)} %get-tuple-element.148), channel_id=1, source_target_pairs={{0,24},{1,9},{2,26},{3,11},{4,28},{5,13},{6,30},{7,15},{8,0},{9,17... | collective-permute-start | bytes 4718600 | tf_op jit(solution)/shard_map/ppermute | solution.py:63
  101.8 31.4 %collective-permute-start.20 = (f32[256,1536]{1,0:T(8,128)S(1)}, f32[256,1536]{1,0:T(8,128)S(1)}, u32[]{:S(2)}, u32[]{:S(2)}) collective-permute-start(f32[256,1536]{1,0:T(8,128)S(1)} %get-tuple-element.150), channel_id=1, source_target_pairs={{0,2},{1,7},{2,4},{3,1},{4,6},{5,3},{6,0},{7,5},{8,10},{9,15},{10,... | collective-permute-start | bytes 4718600 | tf_op jit(solution)/shard_map/ppermute | solution.py:63
  101.9 31.3 %collective-permute-start.18 = (f32[256,1536]{1,0:T(8,128)S(1)}, f32[256,1536]{1,0:T(8,128)S(1)}, u32[]{:S(2)}, u32[]{:S(2)}) collective-permute-start(f32[256,1536]{1,0:T(8,128)S(1)} %get-tuple-element.147), channel_id=1, source_target_pairs={{0,8},{1,25},{2,10},{3,27},{4,12},{5,29},{6,14},{7,31},{8,16},{9,1... | collective-permute-start | bytes 4718600 | tf_op jit(solution)/shard_map/ppermute | solution.py:63
  108.1 17.5 %collective-permute-start.17 = (f32[256,1024]{1,0:T(8,128)S(1)}, f32[256,1024]{1,0:T(8,128)S(1)}, u32[]{:S(2)}, u32[]{:S(2)}) collective-permute-start(f32[256,1024]{1,0:T(8,128)S(1)} %get-tuple-element.145), channel_id=1, source_target_pairs={{0,32},{1,97},{2,34},{3,99},{4,36},{5,101},{6,38},{7,103},{8,40},{... | collective-permute-start | bytes 3145736 | tf_op jit(solution)/shard_map/ppermute | solution.py:63
  134.9 14.1 %collective-permute-start.23 = (f32[64,1536]{1,0:T(8,128)S(1)}, f32[64,1536]{1,0:T(8,128)S(1)}, u32[]{:S(2)}, u32[]{:S(2)}) collective-permute-start(f32[64,1536]{1,0:T(8,128)S(1)} %get-tuple-element.157), channel_id=1, source_target_pairs={{0,2},{1,7},{2,4},{3,1},{4,6},{5,3},{6,0},{7,5},{8,10},{9,15},{10,... | collective-permute-start | bytes 1179656 | tf_op jit(solution)/shard_map/ppermute | solution.py:63
  135.0 14.1 %collective-permute-start.24 = (f32[64,1536]{1,0:T(8,128)S(1)}, f32[64,1536]{1,0:T(8,128)S(1)}, u32[]{:S(2)}, u32[]{:S(2)}) collective-permute-start(f32[64,1536]{1,0:T(8,128)S(1)} %get-tuple-element.159), channel_id=1, source_target_pairs={{0,6},{1,3},{2,0},{3,5},{4,2},{5,7},{6,4},{7,1},{8,14},{9,11},{10,... | collective-permute-start | bytes 1179656 | tf_op jit(solution)/shard_map/ppermute | solution.py:63
  138.3 11.7 %collective-permute-start.25 = (f32[64,1536]{1,0:T(8,128)S(1)}, f32[64,1536]{1,0:T(8,128)S(1)}, u32[]{:S(2)}, u32[]{:S(2)}) collective-permute-start(f32[64,1536]{1,0:T(8,128)S(1)} %get-tuple-element.161), channel_id=1, source_target_pairs={{0,32},{1,97},{2,34},{3,99},{4,36},{5,101},{6,38},{7,103},{8,40},{... | collective-permute-start | bytes 1179656 | tf_op jit(solution)/shard_map/ppermute | solution.py:63
  139.7 10.2 %collective-permute-start.26 = (f32[64,1536]{1,0:T(8,128)S(1)}, f32[64,1536]{1,0:T(8,128)S(1)}, u32[]{:S(2)}, u32[]{:S(2)}) collective-permute-start(f32[64,1536]{1,0:T(8,128)S(1)} %get-tuple-element.163), channel_id=1, source_target_pairs={{0,96},{1,33},{2,98},{3,35},{4,100},{5,37},{6,102},{7,39},{8,104},... | collective-permute-start | bytes 1179656 | tf_op jit(solution)/shard_map/ppermute | solution.py:63
  141.5 7.6 %collective-permute-start.22 = (f32[64,1024]{1,0:T(8,128)S(1)}, f32[64,1024]{1,0:T(8,128)S(1)}, u32[]{:S(2)}, u32[]{:S(2)}) collective-permute-start(f32[64,1024]{1,0:T(8,128)S(1)} %get-tuple-element.154), channel_id=1, source_target_pairs={{0,8},{1,25},{2,10},{3,27},{4,12},{5,29},{6,14},{7,31},{8,16},{9,1... | collective-permute-start | bytes 786440 | tf_op jit(solution)/shard_map/ppermute | solution.py:63
  150.7 9.9 %collective-permute-start.29 = (f32[64,1536]{1,0:T(8,128)S(1)}, f32[64,1536]{1,0:T(8,128)S(1)}, u32[]{:S(2)}, u32[]{:S(2)}) collective-permute-start(f32[64,1536]{1,0:T(8,128)S(1)} %get-tuple-element.167), channel_id=1, source_target_pairs={{0,2},{1,7},{2,4},{3,1},{4,6},{5,3},{6,0},{7,5},{8,10},{9,15},{10,... | collective-permute-start | bytes 1179656 | tf_op jit(solution)/shard_map/ppermute | solution.py:63
  150.8 9.8 %collective-permute-start.30 = (f32[64,1536]{1,0:T(8,128)S(1)}, f32[64,1536]{1,0:T(8,128)S(1)}, u32[]{:S(2)}, u32[]{:S(2)}) collective-permute-start(f32[64,1536]{1,0:T(8,128)S(1)} %get-tuple-element.169), channel_id=1, source_target_pairs={{0,32},{1,97},{2,34},{3,99},{4,36},{5,101},{6,38},{7,103},{8,40},{... | collective-permute-start | bytes 1179656 | tf_op jit(solution)/shard_map/ppermute | solution.py:63
  150.9 9.3 %collective-permute-start.27 = (f32[64,1024]{1,0:T(8,128)S(1)}, f32[64,1024]{1,0:T(8,128)S(1)}, u32[]{:S(2)}, u32[]{:S(2)}) collective-permute-start(f32[64,1024]{1,0:T(8,128)S(1)} %get-tuple-element.164), channel_id=1, source_target_pairs={{0,8},{1,25},{2,10},{3,27},{4,12},{5,29},{6,14},{7,31},{8,16},{9,1... | collective-permute-start | bytes 786440 | tf_op jit(solution)/shard_map/ppermute | solution.py:63
  151.6 8.9 %collective-permute-start.28 = (f32[64,1024]{1,0:T(8,128)S(1)}, f32[64,1024]{1,0:T(8,128)S(1)}, u32[]{:S(2)}, u32[]{:S(2)}) collective-permute-start(f32[64,1024]{1,0:T(8,128)S(1)} %get-tuple-element.165), channel_id=1, source_target_pairs={{0,24},{1,9},{2,26},{3,11},{4,28},{5,13},{6,30},{7,15},{8,0},{9,17... | collective-permute-start | bytes 786440 | tf_op jit(solution)/shard_map/ppermute | solution.py:63
  161.3 10.2 %collective-permute-start.32 = (f32[32,1536]{1,0:T(8,128)S(1)}, f32[32,1536]{1,0:T(8,128)S(1)}, u32[]{:S(2)}, u32[]{:S(2)}) collective-permute-start(f32[32,1536]{1,0:T(8,128)S(1)} %get-tuple-element.173), channel_id=1, source_target_pairs={{0,64},{1,65},{2,66},{3,67},{4,68},{5,69},{6,70},{7,71},{8,72},{9,... | collective-permute-start | bytes 589832 | tf_op jit(solution)/shard_map/ppermute | solution.py:59
  162.9 9.0 %collective-permute-start.33 = (f32[32,1536]{1,0:T(8,128)S(1)}, f32[32,1536]{1,0:T(8,128)S(1)}, u32[]{:S(2)}, u32[]{:S(2)}) collective-permute-start(f32[32,1536]{1,0:T(8,128)S(1)} %get-tuple-element.175), channel_id=1, source_target_pairs={{0,16},{1,17},{2,18},{3,19},{4,20},{5,21},{6,22},{7,23},{8,24},{9,... | collective-permute-start | bytes 589832 | tf_op jit(solution)/shard_map/ppermute | solution.py:59
  165.0 6.5 %collective-permute-start.31 = (f32[32,1024]{1,0:T(8,128)S(1)}, f32[32,1024]{1,0:T(8,128)S(1)}, u32[]{:S(2)}, u32[]{:S(2)}) collective-permute-start(f32[32,1024]{1,0:T(8,128)S(1)} %get-tuple-element.171), channel_id=1, source_target_pairs={{0,4},{1,5},{2,6},{3,7},{4,0},{5,1},{6,2},{7,3},{8,12},{9,13},{10,... | collective-permute-start | bytes 393224 | tf_op jit(solution)/shard_map/ppermute | solution.py:59
  172.6 6.4 %collective-permute-start.34 = (f32[16,1536]{1,0:T(8,128)S(1)}, f32[16,1536]{1,0:T(8,128)S(1)}, u32[]{:S(2)}, u32[]{:S(2)}) collective-permute-start(f32[16,1536]{1,0:T(8,128)S(1)} %get-tuple-element.177), channel_id=1, source_target_pairs={{0,32},{1,33},{2,34},{3,35},{4,36},{5,37},{6,38},{7,39},{8,40},{9,... | collective-permute-start | bytes 294920 | tf_op jit(solution)/shard_map/ppermute | solution.py:59
  172.9 6.0 %collective-permute-start.35 = (f32[16,1536]{1,0:T(8,128)S(1)}, f32[16,1536]{1,0:T(8,128)S(1)}, u32[]{:S(2)}, u32[]{:S(2)}) collective-permute-start(f32[16,1536]{1,0:T(8,128)S(1)} %get-tuple-element.179), channel_id=1, source_target_pairs={{0,8},{1,9},{2,10},{3,11},{4,12},{5,13},{6,14},{7,15},{8,0},{9,1},... | collective-permute-start | bytes 294920 | tf_op jit(solution)/shard_map/ppermute | solution.py:59
  174.6 4.3 %collective-permute-start.36 = (f32[16,1024]{1,0:T(8,128)S(1)}, f32[16,1024]{1,0:T(8,128)S(1)}, u32[]{:S(2)}, u32[]{:S(2)}) collective-permute-start(f32[16,1024]{1,0:T(8,128)S(1)} %get-tuple-element.181), channel_id=1, source_target_pairs={{0,2},{1,3},{2,0},{3,1},{4,6},{5,7},{6,4},{7,5},{8,10},{9,11},{10,... | collective-permute-start | bytes 196616 | tf_op jit(solution)/shard_map/ppermute | solution.py:59
  179.5 10.1 %collective-permute-start.39 = (f32[16,4096]{1,0:T(8,128)S(1)}, f32[16,4096]{1,0:T(8,128)S(1)}, u32[]{:S(2)}, u32[]{:S(2)}) collective-permute-start(f32[16,4096]{1,0:T(8,128)S(1)} %last.1.refs_0_), channel_id=1, source_target_pairs={{0,64},{1,65},{2,66},{3,67},{4,68},{5,69},{6,70},{7,71},{8,72},{9,... | collective-permute-start | bytes 786440 | tf_op jit(solution)/shard_map/ppermute | solution.py:63
  182.4 8.4 %collective-permute-start.38 = (f32[16,4096]{1,0:T(8,128)S(1)}, f32[16,4096]{1,0:T(8,128)S(1)}, u32[]{:S(2)}, u32[]{:S(2)}) collective-permute-start(f32[16,4096]{1,0:T(8,128)S(1)} %last.1.refs_0_), channel_id=1, source_target_pairs={{0,96},{1,97},{2,98},{3,99},{4,100},{5,101},{6,102},{7,103},{8,104... | collective-permute-start | bytes 786440 | tf_op jit(solution)/shard_map/ppermute | solution.py:63
  183.4 9.3 %collective-permute-start.37 = (f32[16,4096]{1,0:T(8,128)S(1)}, f32[16,4096]{1,0:T(8,128)S(1)}, u32[]{:S(2)}, u32[]{:S(2)}) collective-permute-start(f32[16,4096]{1,0:T(8,128)S(1)} %last.1.refs_0_), channel_id=1, source_target_pairs={{0,32},{1,33},{2,34},{3,35},{4,36},{5,37},{6,38},{7,39},{8,40},{9,... | collective-permute-start | bytes 786440 | tf_op jit(solution)/shard_map/ppermute | solution.py:63

commit v5 on v3

--- a/solution.py
+++ b/solution.py
@@ -26,7 +26,7 @@
 SMALL_LIMIT = 16 * 1024 * 1024
 
 KINDS = {"y": (0, 1, 2), "z": (3, 4, 5), "x": (6, 7)}
-GROUP = 2
+GROUP = 4
 
 
 def linear(p):
@@ -328,18 +328,18 @@
     *parts, wide = chip_total(where, keep, got, wide)
     other = send(wide, "c", 1)
     arrived = around(parts, "z")
-    *local, token = local_core(0, 3, q, k, v, cum, parts[1], ())
+    *local, token = local_core(0, 2, q, k, v, cum, parts[1], ())
     prefix, total = small_call(
         row_kernel, where, arrived, [(4,) + msg, msg], [(4,) + msg], [token], "row_total"
     )
     rows = around([total] * 4, "y")
-    *local, token = local_core(3, 2, q, k, v, cum, total, local)
+    *local, token = local_core(2, 1, q, k, v, cum, total, local)
     out = (4, HALF, DK)
     back = small_call(
         back_kernel, where, [prefix] + rows, [out] * 4, [(4,) + msg], [token], "row_start"
     )
     arrived = around(back, "z")
-    *local, token = local_core(5, 2, q, k, v, cum, back[1], local)
+    *local, token = local_core(3, 1, q, k, v, cum, back[1], local)
     mine, theirs = small_call(
         core_start_kernel,
         where,
@@ -348,7 +348,6 @@
         after=[token],
         name="core_start",
     )
-    *local, token = local_core(7, 1, q, k, v, cum, theirs, local)
     return mine, send(theirs, "c", 1), local, other
 
 

time: 197 us -> 195 us (0.990)
  Pallas kernels: 63.6 us -> 58.5 us
  starting transfers between devices: 48.9 us -> 53.8 us
  waiting for transfers between devices: 76 us -> 73.7 us
    ppermute x34, starting transfers between devices: 41.2 us -> 44.7 us  [send(): return lax.ppermute(array, AXES, shift_pairs(axis, by))]
    pallas_call x4 -> x3, Pallas kernels: 18.1 us -> 15.6 us  [local_core(): pl.pallas_call(core_kernel, grid=(steps,), in_specs=[spec] * 4 + [pl.Bloc...]
  transfers between devices with their start and end apart: 40 -> 40, of which waited for: 23 -> 24; matrix products, arithmetic and copies ran while one was open for 0% -> 0% of each run, Pallas kernels for 21% -> 20%
where the time goes in v5:
time: 195 us
  waiting for transfers between devices  73.7 us (38%)
  Pallas kernels  58.5 us (30%)
  starting transfers between devices  53.8 us (28%)
  local copies, waits for them, and re-layouts  7.57 us (4%)
    ppermute x34, waiting for transfers between devices, send(): return lax.ppermute(array, AXES, shift_pairs(axis, by))  65.6 us
    ppermute x34, starting transfers between devices, send(): return lax.ppermute(array, AXES, shift_pairs(axis, by))  44.7 us
    pallas_call x6, Pallas kernels, products(): pl.pallas_call(functools.partial(product_kernel, axis, steps), grid_spec=...  18.3 us
    pallas_call x3, Pallas kernels, local_core(): pl.pallas_call(core_kernel, grid=(steps,), in_specs=[spec] * 4 + [pl.Bloc...  15.6 us
    ppermute x6, starting transfers between devices, swap(): return lax.ppermute(array, AXES, pairs)  9.11 us
    ppermute x6, waiting for transfers between devices, swap(): return lax.ppermute(array, AXES, pairs)  8.15 us
    unnamed x16, local copies, waits for them, and re-layouts  7.57 us
    pallas_call x1, Pallas kernels, local_state(): pl.pallas_call(state_kernel, grid_spec=pltpu.PrefetchScalarGridSpec(num_s...  7.25 us
  transfers between devices with their start and end apart: 40, of which 24 were waited for; matrix products, arithmetic and copies ran while one was open for 0% of the time, Pallas kernels for 20%

profile of v5, /device:TPU:0, one launch (start us, length us, event | category | flops | bytes accessed | tf_op | source)
XLA Modules:
  0.0 194.6 jit_solution(3326143899505137069)
XLA Ops:
  0.7 2.2 %copy-done = bf16[1,512,4096]{2,1,0:T(8,128)(2,1)S(1)} copy-done((bf16[1,512,4096]{2,1,0:T(8,128)(2,1)S(1)}, bf16[1,512,4096]{2,1,0:T(8,128)(2,1)}, u32[]{:S(2)}) %copy-start) | copy-done | bytes 4194328
  2.9 1.6 copy-done.2
  4.5 1.6 copy-done.4
  6.1 2.2 %copy-done.6 = f32[1,512,2048]{2,1,0:T(8,128)S(1)} copy-done((f32[1,512,2048]{2,1,0:T(8,128)S(1)}, f32[1,512,2048]{2,1,0:T(8,128)}, u32[]{:S(2)}) %copy-start.6) | copy-done | bytes 4194328
  8.3 7.2 %local_state.1 = (f32[16,72,128]{2,1,0:T(8,128)S(1)}, f32[16,72,128]{2,1,0:T(8,128)S(1)}, f32[512,2048]{1,0:T(8,128)S(1)}, f32[512,4096]{1,0:T(8,128)}) custom-call(s32[4]{0:T(128)S(1)} %pad_add_fusion.where_ref.refs_0_, bf16[512,2048]{1,0:T(8,128)(2,1)S(1)} %bitcast.32, bf16[512,2048]{1,0:T(8,128)(2,1)S(1)} %bitcast.36, f32[512,2048]{1,0:T(8,128)S(1)} %bitcast.43, ...), custom_call_target="tpu_custom_call" | custom-call | flops 268435456 | bytes 26000000 | tf_op jit(solution)/shard_map/local_state/pallas_call | solution.py:147
  15.5 2.0 %collective-permute-done.got_ref.refs_2_ = f32[16,72,128]{2,1,0:T(8,128)S(1)} collective-permute-done((f32[16,72,128]{2,1,0:T(8,128)S(1)}, f32[16,72,128]{2,1,0:T(8,128)S(1)}, u32[]{:S(2)}, u32[]{:S(2)}) %collective-permute-start) | collective-permute-done | bytes 589856 | tf_op jit(solution)/shard_map/ppermute | solution.py:62
  18.4 4.1 %collective-permute-start.2 = (f32[4,72,128]{2,1,0:T(8,128)S(1)}, f32[4,72,128]{2,1,0:T(8,128)S(1)}, u32[]{:S(2)}, u32[]{:S(2)}) collective-permute-start(f32[4,72,128]{2,1,0:T(8,128)S(1)} %get-tuple-element.98), channel_id=1, source_target_pairs={{0,6},{1,7},{2,0},{3,1},{4,2},{5,3},{6,4},{7,5},{8,14},{9,15},{10,... | collective-permute-start | bytes 442376 | tf_op jit(solution)/shard_map/ppermute | solution.py:62
  23.8 8.0 %local_core.3 = (f32[512,2048]{1,0:T(8,128)S(1)}, bf16[512,2048]{1,0:T(8,128)(2,1)S(1)}, bf16[512,2048]{1,0:T(8,128)(2,1)S(1)}, f32[8,128]{1,0:T(8,128)S(1)}) custom-call(bf16[512,2048]{1,0:T(8,128)(2,1)S(1)} %bitcast.40, bf16[512,2048]{1,0:T(8,128)(2,1)S(1)} %bitcast.33, bf16[512,2048]{1,0:T(8,128)(2,1)S(1)} %bitcast.37, ...), custom_call_target="tpu_custom_call" | custom-call | flops 536870912 | bytes 20000000 | tf_op jit(solution)/shard_map/local_core/pallas_call | solution.py:214
  33.4 3.3 %collective-permute-start.6 = (f32[4,72,128]{2,1,0:T(8,128)S(1)}, f32[4,72,128]{2,1,0:T(8,128)S(1)}, u32[]{:S(2)}, u32[]{:S(2)}) collective-permute-start(f32[4,72,128]{2,1,0:T(8,128)S(1)} %get-tuple-element.101.rest_3_.refs_2_), channel_id=1, source_target_pairs={{0,16},{1,17},{2,18},{3,19},{4,20},{5,21},{6,22},{7,23},{8,24},{9,... | collective-permute-start | bytes 442376 | tf_op jit(solution)/shard_map/ppermute | solution.py:62
  38.7 3.8 %local_core.4 = (f32[512,2048]{1,0:T(8,128)S(1)}, bf16[512,2048]{1,0:T(8,128)(2,1)S(1)}, bf16[512,2048]{1,0:T(8,128)(2,1)S(1)}, f32[8,128]{1,0:T(8,128)S(1)}) custom-call(bf16[512,2048]{1,0:T(8,128)(2,1)S(1)} %bitcast.41, bf16[512,2048]{1,0:T(8,128)(2,1)S(1)} %bitcast.34, ...), custom_call_target="tpu_custom_call", output_to_operand_aliasing={{0}: (4, {}), {1}: (5, {}), {2}: (6, {})} | custom-call | flops 536870912 | bytes 20000000 | tf_op jit(solution)/shard_map/local_core/pallas_call | solution.py:214
  42.5 1.5 collective-permute-done.5.refs_4_
  46.2 2.1 %collective-permute-start.9 = (f32[4,64,128]{2,1,0:T(8,128)S(1)}, f32[4,64,128]{2,1,0:T(8,128)S(1)}, u32[]{:S(2)}, u32[]{:S(2)}) collective-permute-start(f32[4,64,128]{2,1,0:T(8,128)S(1)} %get-tuple-element.113), channel_id=1, source_target_pairs={{0,4},{1,5},{2,6},{3,7},{4,0},{5,1},{6,2},{7,3},{8,12},{9,13},{10,... | collective-permute-start | bytes 393224 | tf_op jit(solution)/shard_map/ppermute | solution.py:62
  48.3 3.8 %local_core.5 = (f32[512,2048]{1,0:T(8,128)S(1)}, bf16[512,2048]{1,0:T(8,128)(2,1)S(1)}, bf16[512,2048]{1,0:T(8,128)(2,1)S(1)}, f32[8,128]{1,0:T(8,128)S(1)}) custom-call(bf16[512,2048]{1,0:T(8,128)(2,1)S(1)} %bitcast.42, bf16[512,2048]{1,0:T(8,128)(2,1)S(1)} %bitcast.35, ...), custom_call_target="tpu_custom_call", output_to_operand_aliasing={{0}: (4, {}), {1}: (5, {}), {2}: (6, {})} | custom-call | flops 536870912 | bytes 20000000 | tf_op jit(solution)/shard_map/local_core/pallas_call | solution.py:214
  53.0 1.5 collective-permute-done.7.refs_4_
  55.2 1.9 collective-permute-done.10.got_ref
  57.1 6.3 %gated_hidden.1 = (bf16[512,2048]{1,0:T(8,128)(2,1)}, bf16[1024,512]{1,0:T(8,128)(2,1)S(1)}, f32[1024,512]{1,0:T(8,128)S(1)}) custom-call(s32[4]{0:T(128)S(1)} %pad_add_fusion.where_ref.refs_0_, f32[512,2048]{1,0:T(8,128)S(1)} %get-tuple-element.108.out_ref, bf16[512,2048]{1,0:T(8,128)(2,1)S(1)} %get-tuple-element.109.high_ref, ...), custom_call_target="tpu_custom_call" | custom-call | flops 805306368 | bytes 17000000 | tf_op jit(solution)/shard_map/gated_hidden/pallas_call | solution.py:379
  63.6 4.0 %collective-permute-done.11 = f32[1024,512]{1,0:T(8,128)S(1)} collective-permute-done((f32[1024,512]{1,0:T(8,128)S(1)}, f32[1024,512]{1,0:T(8,128)S(1)}, u32[]{:S(2)}, u32[]{:S(2)}) %collective-permute-start.11) | collective-permute-done | bytes 2097184 | tf_op jit(solution)/shard_map/ppermute | solution.py:62
  67.6 2.4 %products_y.2 = (f32[256,1536]{1,0:T(8,128)S(1)}, f32[8,128]{1,0:T(8,128)S(1)}) custom-call(s32[4]{0:T(128)S(1)} %pad_add_fusion.where_ref.refs_0_, bf16[4,4,4,16,512]{4,3,2,1,0:T(8,128)(2,1)S(1)} %bitcast.26, f32[4,4,4,16,512]{4,3,2,1,0:T(8,128)S(1)} %bitcast.20, bf16[512,4096]{1,0:T(8,128)(2,1)S(1)} %bitcast.14, ...), custom_call_target="tpu_custom_call" | custom-call | flops 1000000 | bytes 1000000 | tf_op jit(solution)/shard_map/products_y/pallas_call | solution.py:440
  70.0 2.4 %products_z.2 = (f32[256,1536]{1,0:T(8,128)S(1)}, f32[8,128]{1,0:T(8,128)S(1)}) custom-call(s32[4]{0:T(128)S(1)} %pad_add_fusion.where_ref.refs_0_, bf16[4,4,4,16,512]{4,3,2,1,0:T(8,128)(2,1)S(1)} %bitcast.27, f32[4,4,4,16,512]{4,3,2,1,0:T(8,128)S(1)} %bitcast.21, bf16[512,4096]{1,0:T(8,128)(2,1)S(1)} %bitcast.15, ...), custom_call_target="tpu_custom_call" | custom-call | flops 1000000 | bytes 1000000 | tf_op jit(solution)/shard_map/products_z/pallas_call | solution.py:440
  72.4 1.8 products_x.2
  74.3 1.6 collective-permute-start.13
  75.8 2.1 %collective-permute-start.16 = (f32[256,1536]{1,0:T(8,128)S(1)}, f32[256,1536]{1,0:T(8,128)S(1)}, u32[]{:S(2)}, u32[]{:S(2)}) collective-permute-start(f32[256,1536]{1,0:T(8,128)S(1)} %get-tuple-element.135), channel_id=1, source_target_pairs={{0,8},{1,25},{2,10},{3,27},{4,12},{5,29},{6,14},{7,31},{8,16},{9,1... | collective-permute-start | bytes 4718600 | tf_op jit(solution)/shard_map/ppermute | solution.py:62
  78.4 3.1 %products_x.3 = (f32[256,1024]{1,0:T(8,128)S(1)}, f32[256,1024]{1,0:T(8,128)S(1)}, f32[256,1024]{1,0:T(8,128)S(1)}, f32[8,128]{1,0:T(8,128)S(1)}) custom-call(s32[4]{0:T(128)S(1)} %pad_add_fusion.where_ref.refs_0_, bf16[4,4,4,16,512]{4,3,2,1,0:T(8,128)(2,1)S(1)} %bitcast.29, f32[4,4,4,16,512]{4,3,2,1,0:T(8,128)S(1)} %bitcast.23, ...), custom_call_target="tpu_custom_call" | custom-call | flops 1000000 | bytes 1000000 | tf_op jit(solution)/shard_map/products_x/pallas_call | solution.py:440
  81.5 4.3 %products_y.3 = (f32[256,1536]{1,0:T(8,128)S(1)}, f32[256,1536]{1,0:T(8,128)S(1)}, f32[256,1536]{1,0:T(8,128)S(1)}, f32[8,128]{1,0:T(8,128)S(1)}) custom-call(s32[4]{0:T(128)S(1)} %pad_add_fusion.where_ref.refs_0_, bf16[4,4,4,16,512]{4,3,2,1,0:T(8,128)(2,1)S(1)} %bitcast.30, f32[4,4,4,16,512]{4,3,2,1,0:T(8,128)S(1)} %bitcast.24, ...), custom_call_target="tpu_custom_call" | custom-call | flops 1000000 | bytes 1000000 | tf_op jit(solution)/shard_map/products_y/pallas_call | solution.py:440
  85.8 4.3 %products_z.3 = (f32[256,1536]{1,0:T(8,128)S(1)}, f32[256,1536]{1,0:T(8,128)S(1)}, f32[256,1536]{1,0:T(8,128)S(1)}, f32[8,128]{1,0:T(8,128)S(1)}) custom-call(s32[4]{0:T(128)S(1)} %pad_add_fusion.where_ref.refs_0_, bf16[4,4,4,16,512]{4,3,2,1,0:T(8,128)(2,1)S(1)} %bitcast.31, f32[4,4,4,16,512]{4,3,2,1,0:T(8,128)S(1)} %bitcast.25, ...), custom_call_target="tpu_custom_call" | custom-call | flops 1000000 | bytes 1000000 | tf_op jit(solution)/shard_map/products_z/pallas_call | solution.py:440
  92.0 2.9 %collective-permute-start.21 = (f32[256,1536]{1,0:T(8,128)S(1)}, f32[256,1536]{1,0:T(8,128)S(1)}, u32[]{:S(2)}, u32[]{:S(2)}) collective-permute-start(f32[256,1536]{1,0:T(8,128)S(1)} %get-tuple-element.145), channel_id=1, source_target_pairs={{0,6},{1,3},{2,0},{3,5},{4,2},{5,7},{6,4},{7,1},{8,14},{9,11},{10,... | collective-permute-start | bytes 4718600 | tf_op jit(solution)/shard_map/ppermute | solution.py:62
  98.4 3.7 %collective-permute-done.15.b = f32[256,1536]{1,0:T(8,128)S(1)} collective-permute-done((f32[256,1536]{1,0:T(8,128)S(1)}, f32[256,1536]{1,0:T(8,128)S(1)}, u32[]{:S(2)}, u32[]{:S(2)}) %collective-permute-start.15) | collective-permute-done | bytes 1572896 | tf_op jit(solution)/shard_map/ppermute | solution.py:62
  102.7 1.7 collective-permute-start.18
  104.5 2.4 %collective-permute-done.14.b = f32[256,1024]{1,0:T(8,128)S(1)} collective-permute-done((f32[256,1024]{1,0:T(8,128)S(1)}, f32[256,1024]{1,0:T(8,128)S(1)}, u32[]{:S(2)}, u32[]{:S(2)}) %collective-permute-start.14) | collective-permute-done | bytes 1048608 | tf_op jit(solution)/shard_map/ppermute | solution.py:62
  107.7 2.0 %collective-permute-start.17 = (f32[256,1024]{1,0:T(8,128)S(1)}, f32[256,1024]{1,0:T(8,128)S(1)}, u32[]{:S(2)}, u32[]{:S(2)}) collective-permute-start(f32[256,1024]{1,0:T(8,128)S(1)} %get-tuple-element.139), channel_id=1, source_target_pairs={{0,32},{1,97},{2,34},{3,99},{4,36},{5,101},{6,38},{7,103},{8,40},{... | collective-permute-start | bytes 3145736 | tf_op jit(solution)/shard_map/ppermute | solution.py:62
  109.8 16.2 %collective-permute-done.21.refs_8_ = f32[256,1536]{1,0:T(8,128)S(1)} collective-permute-done((f32[256,1536]{1,0:T(8,128)S(1)}, f32[256,1536]{1,0:T(8,128)S(1)}, u32[]{:S(2)}, u32[]{:S(2)}) %collective-permute-start.21) | collective-permute-done | bytes 1572896 | tf_op jit(solution)/shard_map/ppermute | solution.py:62
  126.0 7.3 %collective-permute-done.20.refs_7_ = f32[256,1536]{1,0:T(8,128)S(1)} collective-permute-done((f32[256,1536]{1,0:T(8,128)S(1)}, f32[256,1536]{1,0:T(8,128)S(1)}, u32[]{:S(2)}, u32[]{:S(2)}) %collective-permute-start.20) | collective-permute-done | bytes 1572896 | tf_op jit(solution)/shard_map/ppermute | solution.py:62
  133.3 1.7 second.1
  135.1 3.2 %collective-permute-start.24 = (f32[64,1536]{1,0:T(8,128)S(1)}, f32[64,1536]{1,0:T(8,128)S(1)}, u32[]{:S(2)}, u32[]{:S(2)}) collective-permute-start(f32[64,1536]{1,0:T(8,128)S(1)} %get-tuple-element.153), channel_id=1, source_target_pairs={{0,6},{1,3},{2,0},{3,5},{4,2},{5,7},{6,4},{7,1},{8,14},{9,11},{10,... | collective-permute-start | bytes 1179656 | tf_op jit(solution)/shard_map/ppermute | solution.py:62
  138.3 1.5 collective-permute-start.25
  139.8 1.7 collective-permute-start.26
  143.0 6.1 %collective-permute-done.22.refs_2_ = f32[64,1024]{1,0:T(8,128)S(1)} collective-permute-done((f32[64,1024]{1,0:T(8,128)S(1)}, f32[64,1024]{1,0:T(8,128)S(1)}, u32[]{:S(2)}, u32[]{:S(2)}) %collective-permute-start.22) | collective-permute-done | bytes 262176 | tf_op jit(solution)/shard_map/ppermute | solution.py:62
  151.7 2.2 %collective-permute-start.28 = (f32[64,1024]{1,0:T(8,128)S(1)}, f32[64,1024]{1,0:T(8,128)S(1)}, u32[]{:S(2)}, u32[]{:S(2)}) collective-permute-start(f32[64,1024]{1,0:T(8,128)S(1)} %get-tuple-element.159), channel_id=1, source_target_pairs={{0,24},{1,9},{2,26},{3,11},{4,28},{5,13},{6,30},{7,15},{8,0},{9,17... | collective-permute-start | bytes 786440 | tf_op jit(solution)/shard_map/ppermute | solution.py:62
  153.9 5.1 %collective-permute-done.27.refs_2_ = f32[64,1024]{1,0:T(8,128)S(1)} collective-permute-done((f32[64,1024]{1,0:T(8,128)S(1)}, f32[64,1024]{1,0:T(8,128)S(1)}, u32[]{:S(2)}, u32[]{:S(2)}) %collective-permute-start.27) | collective-permute-done | bytes 262176 | tf_op jit(solution)/shard_map/ppermute | solution.py:62
  160.8 2.1 %collective-permute-start.32 = (f32[32,1536]{1,0:T(8,128)S(1)}, f32[32,1536]{1,0:T(8,128)S(1)}, u32[]{:S(2)}, u32[]{:S(2)}) collective-permute-start(f32[32,1536]{1,0:T(8,128)S(1)} %get-tuple-element.167), channel_id=1, source_target_pairs={{0,64},{1,65},{2,66},{3,67},{4,68},{5,69},{6,70},{7,71},{8,72},{9,... | collective-permute-start | bytes 589832 | tf_op jit(solution)/shard_map/ppermute | solution.py:58
  163.0 2.1 %collective-permute-start.33 = (f32[32,1536]{1,0:T(8,128)S(1)}, f32[32,1536]{1,0:T(8,128)S(1)}, u32[]{:S(2)}, u32[]{:S(2)}) collective-permute-start(f32[32,1536]{1,0:T(8,128)S(1)} %get-tuple-element.169), channel_id=1, source_target_pairs={{0,16},{1,17},{2,18},{3,19},{4,20},{5,21},{6,22},{7,23},{8,24},{9,... | collective-permute-start | bytes 589832 | tf_op jit(solution)/shard_map/ppermute | solution.py:58
  165.1 2.2 %collective-permute-start.31 = (f32[32,1024]{1,0:T(8,128)S(1)}, f32[32,1024]{1,0:T(8,128)S(1)}, u32[]{:S(2)}, u32[]{:S(2)}) collective-permute-start(f32[32,1024]{1,0:T(8,128)S(1)} %get-tuple-element.165), channel_id=1, source_target_pairs={{0,4},{1,5},{2,6},{3,7},{4,0},{5,1},{6,2},{7,3},{8,12},{9,13},{10,... | collective-permute-start | bytes 393224 | tf_op jit(solution)/shard_map/ppermute | solution.py:58
  167.2 4.3 %collective-permute-done.31.refs_2_ = f32[32,1024]{1,0:T(8,128)S(1)} collective-permute-done((f32[32,1024]{1,0:T(8,128)S(1)}, f32[32,1024]{1,0:T(8,128)S(1)}, u32[]{:S(2)}, u32[]{:S(2)}) %collective-permute-start.31) | collective-permute-done | bytes 131104 | tf_op jit(solution)/shard_map/ppermute | solution.py:58
  175.3 3.4 %collective-permute-done.36.refs_6_ = f32[16,1024]{1,0:T(8,128)S(1)} collective-permute-done((f32[16,1024]{1,0:T(8,128)S(1)}, f32[16,1024]{1,0:T(8,128)S(1)}, u32[]{:S(2)}, u32[]{:S(2)}) %collective-permute-start.36) | collective-permute-done | bytes 65568 | tf_op jit(solution)/shard_map/ppermute | solution.py:58
  179.3 3.1 %collective-permute-start.39 = (f32[16,4096]{1,0:T(8,128)S(1)}, f32[16,4096]{1,0:T(8,128)S(1)}, u32[]{:S(2)}, u32[]{:S(2)}) collective-permute-start(f32[16,4096]{1,0:T(8,128)S(1)} %last.1.refs_0_), channel_id=1, source_target_pairs={{0,64},{1,65},{2,66},{3,67},{4,68},{5,69},{6,70},{7,71},{8,72},{9,... | collective-permute-start | bytes 786440 | tf_op jit(solution)/shard_map/ppermute | solution.py:62
  184.4 4.9 %collective-permute-done.39.refs_3_ = f32[16,4096]{1,0:T(8,128)S(1)} collective-permute-done((f32[16,4096]{1,0:T(8,128)S(1)}, f32[16,4096]{1,0:T(8,128)S(1)}, u32[]{:S(2)}, u32[]{:S(2)}) %collective-permute-start.39) | collective-permute-done | bytes 262176 | tf_op jit(solution)/shard_map/ppermute | solution.py:62
  190.8 2.2 %collective-permute-done.37.refs_1_ = f32[16,4096]{1,0:T(8,128)S(1)} collective-permute-done((f32[16,4096]{1,0:T(8,128)S(1)}, f32[16,4096]{1,0:T(8,128)S(1)}, u32[]{:S(2)}, u32[]{:S(2)}) %collective-permute-start.37) | collective-permute-done | bytes 262176 | tf_op jit(solution)/shard_map/ppermute | solution.py:62
  193.0 1.6 assemble.1
  (74 shorter events, 30.9 us)
Async XLA Ops:
  0.7 2.2 %copy-start = (bf16[1,512,4096]{2,1,0:T(8,128)(2,1)S(1)}, bf16[1,512,4096]{2,1,0:T(8,128)(2,1)}, u32[]{:S(2)}) copy-start(bf16[1,512,4096]{2,1,0:T(8,128)(2,1)} %param.11) | copy-start | bytes 12582916
  2.9 1.6 copy-start.2
  4.5 1.6 copy-start.4
  6.1 2.2 %copy-start.6 = (f32[1,512,2048]{2,1,0:T(8,128)S(1)}, f32[1,512,2048]{2,1,0:T(8,128)}, u32[]{:S(2)}) copy-start(f32[1,512,2048]{2,1,0:T(8,128)} %param.9) | copy-start | bytes 12582916
  15.5 2.0 %collective-permute-start = (f32[16,72,128]{2,1,0:T(8,128)S(1)}, f32[16,72,128]{2,1,0:T(8,128)S(1)}, u32[]{:S(2)}, u32[]{:S(2)}) collective-permute-start(f32[16,72,128]{2,1,0:T(8,128)S(1)} %get-tuple-element.91), channel_id=1, source_target_pairs={{0,1},{1,0},{2,3},{3,2},{4,5},{5,4},{6,7},{7,6},{8,9},{9,8},{10,11... | collective-permute-start | bytes 1769480 | tf_op jit(solution)/shard_map/ppermute | solution.py:62
  17.5 6.3 %copy-start.3 = (bf16[1,512,2048]{2,1,0:T(8,128)(2,1)S(1)}, bf16[1,512,2048]{2,1,0:T(8,128)(2,1)}, u32[]{:S(2)}) copy-start(bf16[1,512,2048]{2,1,0:T(8,128)(2,1)} %param.7) | copy-start | bytes 6291460
  17.5 6.3 %copy-start.5 = (bf16[1,512,2048]{2,1,0:T(8,128)(2,1)S(1)}, bf16[1,512,2048]{2,1,0:T(8,128)(2,1)}, u32[]{:S(2)}) copy-start(bf16[1,512,2048]{2,1,0:T(8,128)(2,1)} %param.6) | copy-start | bytes 6291460
  18.2 49.4 %collective-permute-start.12 = (f32[512,4096]{1,0:T(8,128)}, f32[512,4096]{1,0:T(8,128)S(1)}, u32[]{:S(2)}, u32[]{:S(2)}) collective-permute-start(f32[512,4096]{1,0:T(8,128)} %get-tuple-element.120), channel_id=1, source_target_pairs={{0,1},{1,0},{2,3},{3,2},{4,5},{5,4},{6,7},{7,6},{8,9},{9,8},{10,11... | collective-permute-start | bytes 25165832 | tf_op jit(solution)/shard_map/ppermute | solution.py:62
  18.4 13.4 %collective-permute-start.2 = (f32[4,72,128]{2,1,0:T(8,128)S(1)}, f32[4,72,128]{2,1,0:T(8,128)S(1)}, u32[]{:S(2)}, u32[]{:S(2)}) collective-permute-start(f32[4,72,128]{2,1,0:T(8,128)S(1)} %get-tuple-element.98), channel_id=1, source_target_pairs={{0,6},{1,7},{2,0},{3,1},{4,2},{5,3},{6,4},{7,5},{8,14},{9,15},{10,... | collective-permute-start | bytes 442376 | tf_op jit(solution)/shard_map/ppermute | solution.py:62
  22.5 9.3 %collective-permute-start.3 = (f32[4,72,128]{2,1,0:T(8,128)S(1)}, f32[4,72,128]{2,1,0:T(8,128)S(1)}, u32[]{:S(2)}, u32[]{:S(2)}) collective-permute-start(f32[4,72,128]{2,1,0:T(8,128)S(1)} %get-tuple-element.99), channel_id=1, source_target_pairs={{0,4},{1,5},{2,6},{3,7},{4,0},{5,1},{6,2},{7,3},{8,12},{9,13},{10,... | collective-permute-start | bytes 442376 | tf_op jit(solution)/shard_map/ppermute | solution.py:62
  22.5 10.2 %collective-permute-start.1 = (f32[4,72,128]{2,1,0:T(8,128)S(1)}, f32[4,72,128]{2,1,0:T(8,128)S(1)}, u32[]{:S(2)}, u32[]{:S(2)}) collective-permute-start(f32[4,72,128]{2,1,0:T(8,128)S(1)} %get-tuple-element.93.rest_0_), channel_id=1, source_target_pairs={{0,2},{1,3},{2,4},{3,5},{4,6},{5,7},{6,0},{7,1},{8,10},{9,11},{10,... | collective-permute-start | bytes 442376 | tf_op jit(solution)/shard_map/ppermute | solution.py:62
  33.4 9.1 %collective-permute-start.6 = (f32[4,72,128]{2,1,0:T(8,128)S(1)}, f32[4,72,128]{2,1,0:T(8,128)S(1)}, u32[]{:S(2)}, u32[]{:S(2)}) collective-permute-start(f32[4,72,128]{2,1,0:T(8,128)S(1)} %get-tuple-element.101.rest_3_.refs_2_), channel_id=1, source_target_pairs={{0,16},{1,17},{2,18},{3,19},{4,20},{5,21},{6,22},{7,23},{8,24},{9,... | collective-permute-start | bytes 442376 | tf_op jit(solution)/shard_map/ppermute | solution.py:62
  36.7 7.3 %collective-permute-start.5 = (f32[4,72,128]{2,1,0:T(8,128)S(1)}, f32[4,72,128]{2,1,0:T(8,128)S(1)}, u32[]{:S(2)}, u32[]{:S(2)}) collective-permute-start(f32[4,72,128]{2,1,0:T(8,128)S(1)} %get-tuple-element.101.rest_3_.refs_2_), channel_id=1, source_target_pairs={{0,24},{1,25},{2,26},{3,27},{4,28},{5,29},{6,30},{7,31},{8,0},{9,1... | collective-permute-start | bytes 442376 | tf_op jit(solution)/shard_map/ppermute | solution.py:62
  37.7 6.6 %collective-permute-start.4 = (f32[4,72,128]{2,1,0:T(8,128)S(1)}, f32[4,72,128]{2,1,0:T(8,128)S(1)}, u32[]{:S(2)}, u32[]{:S(2)}) collective-permute-start(f32[4,72,128]{2,1,0:T(8,128)S(1)} %get-tuple-element.101.rest_3_.refs_2_), channel_id=1, source_target_pairs={{0,8},{1,9},{2,10},{3,11},{4,12},{5,13},{6,14},{7,15},{8,16},{9,17... | collective-permute-start | bytes 442376 | tf_op jit(solution)/shard_map/ppermute | solution.py:62
  45.0 7.1 %collective-permute-start.8 = (f32[4,64,128]{2,1,0:T(8,128)S(1)}, f32[4,64,128]{2,1,0:T(8,128)S(1)}, u32[]{:S(2)}, u32[]{:S(2)}) collective-permute-start(f32[4,64,128]{2,1,0:T(8,128)S(1)} %get-tuple-element.112), channel_id=1, source_target_pairs={{0,6},{1,7},{2,0},{3,1},{4,2},{5,3},{6,4},{7,5},{8,14},{9,15},{10,... | collective-permute-start | bytes 393224 | tf_op jit(solution)/shard_map/ppermute | solution.py:62
  46.2 6.7 %collective-permute-start.9 = (f32[4,64,128]{2,1,0:T(8,128)S(1)}, f32[4,64,128]{2,1,0:T(8,128)S(1)}, u32[]{:S(2)}, u32[]{:S(2)}) collective-permute-start(f32[4,64,128]{2,1,0:T(8,128)S(1)} %get-tuple-element.113), channel_id=1, source_target_pairs={{0,4},{1,5},{2,6},{3,7},{4,0},{5,1},{6,2},{7,3},{8,12},{9,13},{10,... | collective-permute-start | bytes 393224 | tf_op jit(solution)/shard_map/ppermute | solution.py:62
  48.3 6.2 %collective-permute-start.7 = (f32[4,64,128]{2,1,0:T(8,128)S(1)}, f32[4,64,128]{2,1,0:T(8,128)S(1)}, u32[]{:S(2)}, u32[]{:S(2)}) collective-permute-start(f32[4,64,128]{2,1,0:T(8,128)S(1)} %get-tuple-element.107.rest_3_), channel_id=1, source_target_pairs={{0,2},{1,3},{2,4},{3,5},{4,6},{5,7},{6,0},{7,1},{8,10},{9,11},{10,... | collective-permute-start | bytes 393224 | tf_op jit(solution)/shard_map/ppermute | solution.py:62
  48.3 8.9 %copy-start.7 = (bf16[1,512,2048]{2,1,0:T(8,128)(2,1)S(1)}, bf16[1,512,2048]{2,1,0:T(8,128)(2,1)}, u32[]{:S(2)}) copy-start(bf16[1,512,2048]{2,1,0:T(8,128)(2,1)} %param.10) | copy-start | bytes 6291460
  55.1 2.0 %collective-permute-start.10 = (f32[16,64,128]{2,1,0:T(8,128)S(1)}, f32[16,64,128]{2,1,0:T(8,128)S(1)}, u32[]{:S(2)}, u32[]{:S(2)}) collective-permute-start(f32[16,64,128]{2,1,0:T(8,128)S(1)} %get-tuple-element.116), channel_id=1, source_target_pairs={{0,1},{1,0},{2,3},{3,2},{4,5},{5,4},{6,7},{7,6},{8,9},{9,8},{10,11... | collective-permute-start | bytes 1572872 | tf_op jit(solution)/shard_map/ppermute | solution.py:62
  57.1 10.5 %copy-start.1 = (bf16[1,512,4096]{2,1,0:T(8,128)(2,1)S(1)}, bf16[1,512,4096]{2,1,0:T(8,128)(2,1)}, u32[]{:S(2)}) copy-start(bf16[1,512,4096]{2,1,0:T(8,128)(2,1)} %param.11) | copy-start | bytes 12582916
  63.5 4.2 %collective-permute-start.11 = (f32[1024,512]{1,0:T(8,128)S(1)}, f32[1024,512]{1,0:T(8,128)S(1)}, u32[]{:S(2)}, u32[]{:S(2)}) collective-permute-start(f32[1024,512]{1,0:T(8,128)S(1)} %get-tuple-element.119), channel_id=1, source_target_pairs={{0,1},{1,0},{2,3},{3,2},{4,5},{5,4},{6,7},{7,6},{8,9},{9,8},{10,11... | collective-permute-start | bytes 6291464 | tf_op jit(solution)/shard_map/ppermute | solution.py:62
  74.3 16.1 %collective-permute-start.13 = (f32[256,1024]{1,0:T(8,128)S(1)}, f32[256,1024]{1,0:T(8,128)S(1)}, u32[]{:S(2)}, u32[]{:S(2)}) collective-permute-start(f32[256,1024]{1,0:T(8,128)S(1)} %get-tuple-element.127), channel_id=1, source_target_pairs={{0,32},{1,97},{2,34},{3,99},{4,36},{5,101},{6,38},{7,103},{8,40},{... | collective-permute-start | bytes 3145736 | tf_op jit(solution)/shard_map/ppermute | solution.py:62
  75.8 22.0 %collective-permute-start.16 = (f32[256,1536]{1,0:T(8,128)S(1)}, f32[256,1536]{1,0:T(8,128)S(1)}, u32[]{:S(2)}, u32[]{:S(2)}) collective-permute-start(f32[256,1536]{1,0:T(8,128)S(1)} %get-tuple-element.135), channel_id=1, source_target_pairs={{0,8},{1,25},{2,10},{3,27},{4,12},{5,29},{6,14},{7,31},{8,16},{9,1... | collective-permute-start | bytes 4718600 | tf_op jit(solution)/shard_map/ppermute | solution.py:62
  78.0 24.1 %collective-permute-start.15 = (f32[256,1536]{1,0:T(8,128)S(1)}, f32[256,1536]{1,0:T(8,128)S(1)}, u32[]{:S(2)}, u32[]{:S(2)}) collective-permute-start(f32[256,1536]{1,0:T(8,128)S(1)} %get-tuple-element.133), channel_id=1, source_target_pairs={{0,2},{1,7},{2,4},{3,1},{4,6},{5,3},{6,0},{7,5},{8,10},{9,15},{10,... | collective-permute-start | bytes 4718600 | tf_op jit(solution)/shard_map/ppermute | solution.py:62
  90.7 16.1 %collective-permute-start.14 = (f32[256,1024]{1,0:T(8,128)S(1)}, f32[256,1024]{1,0:T(8,128)S(1)}, u32[]{:S(2)}, u32[]{:S(2)}) collective-permute-start(f32[256,1024]{1,0:T(8,128)S(1)} %get-tuple-element.131), channel_id=1, source_target_pairs={{0,32},{1,97},{2,34},{3,99},{4,36},{5,101},{6,38},{7,103},{8,40},{... | collective-permute-start | bytes 3145736 | tf_op jit(solution)/shard_map/ppermute | solution.py:62
  92.0 33.9 %collective-permute-start.21 = (f32[256,1536]{1,0:T(8,128)S(1)}, f32[256,1536]{1,0:T(8,128)S(1)}, u32[]{:S(2)}, u32[]{:S(2)}) collective-permute-start(f32[256,1536]{1,0:T(8,128)S(1)} %get-tuple-element.145), channel_id=1, source_target_pairs={{0,6},{1,3},{2,0},{3,5},{4,2},{5,7},{6,4},{7,1},{8,14},{9,11},{10,... | collective-permute-start | bytes 4718600 | tf_op jit(solution)/shard_map/ppermute | solution.py:62
  94.9 31.1 %collective-permute-start.19 = (f32[256,1536]{1,0:T(8,128)S(1)}, f32[256,1536]{1,0:T(8,128)S(1)}, u32[]{:S(2)}, u32[]{:S(2)}) collective-permute-start(f32[256,1536]{1,0:T(8,128)S(1)} %get-tuple-element.142), channel_id=1, source_target_pairs={{0,24},{1,9},{2,26},{3,11},{4,28},{5,13},{6,30},{7,15},{8,0},{9,17... | collective-permute-start | bytes 4718600 | tf_op jit(solution)/shard_map/ppermute | solution.py:62
  102.6 30.7 %collective-permute-start.20 = (f32[256,1536]{1,0:T(8,128)S(1)}, f32[256,1536]{1,0:T(8,128)S(1)}, u32[]{:S(2)}, u32[]{:S(2)}) collective-permute-start(f32[256,1536]{1,0:T(8,128)S(1)} %get-tuple-element.144), channel_id=1, source_target_pairs={{0,2},{1,7},{2,4},{3,1},{4,6},{5,3},{6,0},{7,5},{8,10},{9,15},{10,... | collective-permute-start | bytes 4718600 | tf_op jit(solution)/shard_map/ppermute | solution.py:62
  102.7 30.6 %collective-permute-start.18 = (f32[256,1536]{1,0:T(8,128)S(1)}, f32[256,1536]{1,0:T(8,128)S(1)}, u32[]{:S(2)}, u32[]{:S(2)}) collective-permute-start(f32[256,1536]{1,0:T(8,128)S(1)} %get-tuple-element.141), channel_id=1, source_target_pairs={{0,8},{1,25},{2,10},{3,27},{4,12},{5,29},{6,14},{7,31},{8,16},{9,1... | collective-permute-start | bytes 4718600 | tf_op jit(solution)/shard_map/ppermute | solution.py:62
  107.7 18.2 %collective-permute-start.17 = (f32[256,1024]{1,0:T(8,128)S(1)}, f32[256,1024]{1,0:T(8,128)S(1)}, u32[]{:S(2)}, u32[]{:S(2)}) collective-permute-start(f32[256,1024]{1,0:T(8,128)S(1)} %get-tuple-element.139), channel_id=1, source_target_pairs={{0,32},{1,97},{2,34},{3,99},{4,36},{5,101},{6,38},{7,103},{8,40},{... | collective-permute-start | bytes 3145736 | tf_op jit(solution)/shard_map/ppermute | solution.py:62
  135.0 14.1 %collective-permute-start.23 = (f32[64,1536]{1,0:T(8,128)S(1)}, f32[64,1536]{1,0:T(8,128)S(1)}, u32[]{:S(2)}, u32[]{:S(2)}) collective-permute-start(f32[64,1536]{1,0:T(8,128)S(1)} %get-tuple-element.151), channel_id=1, source_target_pairs={{0,2},{1,7},{2,4},{3,1},{4,6},{5,3},{6,0},{7,5},{8,10},{9,15},{10,... | collective-permute-start | bytes 1179656 | tf_op jit(solution)/shard_map/ppermute | solution.py:62
  135.1 14.1 %collective-permute-start.24 = (f32[64,1536]{1,0:T(8,128)S(1)}, f32[64,1536]{1,0:T(8,128)S(1)}, u32[]{:S(2)}, u32[]{:S(2)}) collective-permute-start(f32[64,1536]{1,0:T(8,128)S(1)} %get-tuple-element.153), channel_id=1, source_target_pairs={{0,6},{1,3},{2,0},{3,5},{4,2},{5,7},{6,4},{7,1},{8,14},{9,11},{10,... | collective-permute-start | bytes 1179656 | tf_op jit(solution)/shard_map/ppermute | solution.py:62
  138.3 11.2 %collective-permute-start.25 = (f32[64,1536]{1,0:T(8,128)S(1)}, f32[64,1536]{1,0:T(8,128)S(1)}, u32[]{:S(2)}, u32[]{:S(2)}) collective-permute-start(f32[64,1536]{1,0:T(8,128)S(1)} %get-tuple-element.155), channel_id=1, source_target_pairs={{0,32},{1,97},{2,34},{3,99},{4,36},{5,101},{6,38},{7,103},{8,40},{... | collective-permute-start | bytes 1179656 | tf_op jit(solution)/shard_map/ppermute | solution.py:62
  139.8 9.7 %collective-permute-start.26 = (f32[64,1536]{1,0:T(8,128)S(1)}, f32[64,1536]{1,0:T(8,128)S(1)}, u32[]{:S(2)}, u32[]{:S(2)}) collective-permute-start(f32[64,1536]{1,0:T(8,128)S(1)} %get-tuple-element.157), channel_id=1, source_target_pairs={{0,96},{1,33},{2,98},{3,35},{4,100},{5,37},{6,102},{7,39},{8,104},... | collective-permute-start | bytes 1179656 | tf_op jit(solution)/shard_map/ppermute | solution.py:62
  141.5 7.6 %collective-permute-start.22 = (f32[64,1024]{1,0:T(8,128)S(1)}, f32[64,1024]{1,0:T(8,128)S(1)}, u32[]{:S(2)}, u32[]{:S(2)}) collective-permute-start(f32[64,1024]{1,0:T(8,128)S(1)} %get-tuple-element.148), channel_id=1, source_target_pairs={{0,8},{1,25},{2,10},{3,27},{4,12},{5,29},{6,14},{7,31},{8,16},{9,1... | collective-permute-start | bytes 786440 | tf_op jit(solution)/shard_map/ppermute | solution.py:62
  150.3 9.8 %collective-permute-start.29 = (f32[64,1536]{1,0:T(8,128)S(1)}, f32[64,1536]{1,0:T(8,128)S(1)}, u32[]{:S(2)}, u32[]{:S(2)}) collective-permute-start(f32[64,1536]{1,0:T(8,128)S(1)} %get-tuple-element.161), channel_id=1, source_target_pairs={{0,2},{1,7},{2,4},{3,1},{4,6},{5,3},{6,0},{7,5},{8,10},{9,15},{10,... | collective-permute-start | bytes 1179656 | tf_op jit(solution)/shard_map/ppermute | solution.py:62
  150.7 9.4 %collective-permute-start.30 = (f32[64,1536]{1,0:T(8,128)S(1)}, f32[64,1536]{1,0:T(8,128)S(1)}, u32[]{:S(2)}, u32[]{:S(2)}) collective-permute-start(f32[64,1536]{1,0:T(8,128)S(1)} %get-tuple-element.163), channel_id=1, source_target_pairs={{0,32},{1,97},{2,34},{3,99},{4,36},{5,101},{6,38},{7,103},{8,40},{... | collective-permute-start | bytes 1179656 | tf_op jit(solution)/shard_map/ppermute | solution.py:62
  150.7 8.4 %collective-permute-start.27 = (f32[64,1024]{1,0:T(8,128)S(1)}, f32[64,1024]{1,0:T(8,128)S(1)}, u32[]{:S(2)}, u32[]{:S(2)}) collective-permute-start(f32[64,1024]{1,0:T(8,128)S(1)} %get-tuple-element.158), channel_id=1, source_target_pairs={{0,8},{1,25},{2,10},{3,27},{4,12},{5,29},{6,14},{7,31},{8,16},{9,1... | collective-permute-start | bytes 786440 | tf_op jit(solution)/shard_map/ppermute | solution.py:62
  151.7 8.3 %collective-permute-start.28 = (f32[64,1024]{1,0:T(8,128)S(1)}, f32[64,1024]{1,0:T(8,128)S(1)}, u32[]{:S(2)}, u32[]{:S(2)}) collective-permute-start(f32[64,1024]{1,0:T(8,128)S(1)} %get-tuple-element.159), channel_id=1, source_target_pairs={{0,24},{1,9},{2,26},{3,11},{4,28},{5,13},{6,30},{7,15},{8,0},{9,17... | collective-permute-start | bytes 786440 | tf_op jit(solution)/shard_map/ppermute | solution.py:62
  160.8 10.7 %collective-permute-start.32 = (f32[32,1536]{1,0:T(8,128)S(1)}, f32[32,1536]{1,0:T(8,128)S(1)}, u32[]{:S(2)}, u32[]{:S(2)}) collective-permute-start(f32[32,1536]{1,0:T(8,128)S(1)} %get-tuple-element.167), channel_id=1, source_target_pairs={{0,64},{1,65},{2,66},{3,67},{4,68},{5,69},{6,70},{7,71},{8,72},{9,... | collective-permute-start | bytes 589832 | tf_op jit(solution)/shard_map/ppermute | solution.py:58
  163.0 9.0 %collective-permute-start.33 = (f32[32,1536]{1,0:T(8,128)S(1)}, f32[32,1536]{1,0:T(8,128)S(1)}, u32[]{:S(2)}, u32[]{:S(2)}) collective-permute-start(f32[32,1536]{1,0:T(8,128)S(1)} %get-tuple-element.169), channel_id=1, source_target_pairs={{0,16},{1,17},{2,18},{3,19},{4,20},{5,21},{6,22},{7,23},{8,24},{9,... | collective-permute-start | bytes 589832 | tf_op jit(solution)/shard_map/ppermute | solution.py:58
  165.1 6.5 %collective-permute-start.31 = (f32[32,1024]{1,0:T(8,128)S(1)}, f32[32,1024]{1,0:T(8,128)S(1)}, u32[]{:S(2)}, u32[]{:S(2)}) collective-permute-start(f32[32,1024]{1,0:T(8,128)S(1)} %get-tuple-element.165), channel_id=1, source_target_pairs={{0,4},{1,5},{2,6},{3,7},{4,0},{5,1},{6,2},{7,3},{8,12},{9,13},{10,... | collective-permute-start | bytes 393224 | tf_op jit(solution)/shard_map/ppermute | solution.py:58
  172.6 6.1 %collective-permute-start.34 = (f32[16,1536]{1,0:T(8,128)S(1)}, f32[16,1536]{1,0:T(8,128)S(1)}, u32[]{:S(2)}, u32[]{:S(2)}) collective-permute-start(f32[16,1536]{1,0:T(8,128)S(1)} %get-tuple-element.171), channel_id=1, source_target_pairs={{0,32},{1,33},{2,34},{3,35},{4,36},{5,37},{6,38},{7,39},{8,40},{9,... | collective-permute-start | bytes 294920 | tf_op jit(solution)/shard_map/ppermute | solution.py:58
  173.5 5.2 %collective-permute-start.35 = (f32[16,1536]{1,0:T(8,128)S(1)}, f32[16,1536]{1,0:T(8,128)S(1)}, u32[]{:S(2)}, u32[]{:S(2)}) collective-permute-start(f32[16,1536]{1,0:T(8,128)S(1)} %get-tuple-element.173), channel_id=1, source_target_pairs={{0,8},{1,9},{2,10},{3,11},{4,12},{5,13},{6,14},{7,15},{8,0},{9,1},... | collective-permute-start | bytes 294920 | tf_op jit(solution)/shard_map/ppermute | solution.py:58
  174.5 4.3 %collective-permute-start.36 = (f32[16,1024]{1,0:T(8,128)S(1)}, f32[16,1024]{1,0:T(8,128)S(1)}, u32[]{:S(2)}, u32[]{:S(2)}) collective-permute-start(f32[16,1024]{1,0:T(8,128)S(1)} %get-tuple-element.175), channel_id=1, source_target_pairs={{0,2},{1,3},{2,0},{3,1},{4,6},{5,7},{6,4},{7,5},{8,10},{9,11},{10,... | collective-permute-start | bytes 196616 | tf_op jit(solution)/shard_map/ppermute | solution.py:58
  179.3 10.0 %collective-permute-start.39 = (f32[16,4096]{1,0:T(8,128)S(1)}, f32[16,4096]{1,0:T(8,128)S(1)}, u32[]{:S(2)}, u32[]{:S(2)}) collective-permute-start(f32[16,4096]{1,0:T(8,128)S(1)} %last.1.refs_0_), channel_id=1, source_target_pairs={{0,64},{1,65},{2,66},{3,67},{4,68},{5,69},{6,70},{7,71},{8,72},{9,... | collective-permute-start | bytes 786440 | tf_op jit(solution)/shard_map/ppermute | solution.py:62
  182.4 8.4 %collective-permute-start.38 = (f32[16,4096]{1,0:T(8,128)S(1)}, f32[16,4096]{1,0:T(8,128)S(1)}, u32[]{:S(2)}, u32[]{:S(2)}) collective-permute-start(f32[16,4096]{1,0:T(8,128)S(1)} %last.1.refs_0_), channel_id=1, source_target_pairs={{0,96},{1,97},{2,98},{3,99},{4,100},{5,101},{6,102},{7,103},{8,104... | collective-permute-start | bytes 786440 | tf_op jit(solution)/shard_map/ppermute | solution.py:62
  183.3 9.7 %collective-permute-start.37 = (f32[16,4096]{1,0:T(8,128)S(1)}, f32[16,4096]{1,0:T(8,128)S(1)}, u32[]{:S(2)}, u32[]{:S(2)}) collective-permute-start(f32[16,4096]{1,0:T(8,128)S(1)} %last.1.refs_0_), channel_id=1, source_target_pairs={{0,32},{1,33},{2,34},{3,35},{4,36},{5,37},{6,38},{7,39},{8,40},{9,... | collective-permute-start | bytes 786440 | tf_op jit(solution)/shard_map/ppermute | solution.py:62
